TPU v7x, 256 devices: a whole 4x4x8 slice. The times are simulated.
256 devices in a mesh: space: 64 (over x, y, z_lo, core), sample: 4 (over z_hi).
Axes of the slice: x: 4, y: 4, z: 8 (z_hi: 4, z_lo: 2; z = z_hi * 2 + z_lo), core: 2. Of those that a mesh axis runs over, the one named last changes fastest.
Arguments:
- volume: bfloat16 [4, 128, 32, 64, 128], P('sample', 'space'), may hold values from -6 to 6
- upstream: bfloat16 [4, 128, 32, 64, 128], P('sample', 'space'), may hold values from -16 to 16
- weight: bfloat16 [3456, 128], replicated, may hold values from -0.109375 to 0.109375
- first_moment: float32 [3456, 128], P('sample'), may hold values from -1792 to 1792
- second_moment: float32 [3456, 128], P('sample'), may hold values from 2097.152 to 20971.52
Outputs:
- grad_volume: bfloat16 [4, 128, 32, 64, 128], P('sample', 'space')
- direction: float32 [3456, 128], P('sample')
All inputs are finite; a program needn't handle non-finite values.
Results may differ from a plain program's by a relative error of at most 0.0039.
Values may be sent and summed in bfloat16 or wider, within the bound.
No kernel may reach another device: no remote copies, remote signals or barrier semaphores. Data moves between devices by JAX's collectives and lax.ppermute only.
A program may use at most 64 MiB of HBM per device.

v0:
```python
import functools
import jax
import jax.numpy as jnp
from jax import lax
from jax.experimental import pallas as pl
from jax.experimental.pallas import tpu as pltpu
from jax.sharding import Mesh, PartitionSpec as P

ADAM_STEP = 10


beta_one = 0.9
beta_two = 0.999
eps_adam = 1e-08

SPACE = ("x", "y", "zl", "core")
CHUNK = 32
OWNERS = 32
C = 128
COLS = 64
ROWS = 32
CELLS = ROWS * COLS
PADDED = CELLS + 2 * COLS
STRIP = 256
TILE = 512
BF = jnp.bfloat16
F32 = jnp.float32
VMEM = pl.BlockSpec(memory_space=pltpu.VMEM)
SMEM = pl.BlockSpec(memory_space=pltpu.SMEM)
PARAMS = pltpu.CompilerParams(vmem_limit_bytes=48 * 1024 * 1024)


def cost(flops, moved, special=0):
    return pl.CostEstimate(flops=flops, bytes_accessed=moved, transcendentals=special)


def shifted_columns(planes, out, first, flip):
    width = 128 * len(planes)
    blank = jnp.zeros((COLS, width), BF)
    cols = slice(first, first + width)
    for c in range(3):
        out[c, 0:COLS, cols] = blank
        out[c, PADDED - COLS : PADDED, cols] = blank
    before, after = (2, 0) if flip else (0, 2)

    def strip(i, carry):
        at = pl.multiple_of(i * STRIP, STRIP)
        to = pl.ds(pl.multiple_of(at + COLS, COLS), STRIP)
        col = lax.broadcasted_iota(jnp.int32, (STRIP, C), 0) & (COLS - 1)
        for k, plane in enumerate(planes):
            cols = slice(first + k * C, first + (k + 1) * C)
            here = plane[pl.ds(at, STRIP), :]
            wide = here.astype(F32)
            out[1, to, cols] = here
            out[before, to, cols] = jnp.where(
                col == 0, 0.0, pltpu.roll(wide, 1, 0)
            ).astype(BF)
            out[after, to, cols] = jnp.where(
                col == COLS - 1, 0.0, pltpu.roll(wide, STRIP - 1, 0)
            ).astype(BF)
        return carry

    lax.fori_loop(0, CELLS // STRIP, strip, 0)


def tap(a, b, c):
    return (a * 3 + b) * 3 + c


def taps_of(field, at, rows):
    return jnp.concatenate(
        [
            field[c, pl.ds(pl.multiple_of(at + b * COLS, COLS), rows), :]
            for b in range(3)
            for c in range(3)
        ],
        axis=1,
    )


def inner_kernel(vol, weight, out, vol_t, field, mixed):
    shifted_columns([vol.at[0], vol.at[1]], field, 0, False)
    for b in range(3):
        for c in range(3):
            base = (b * 3 + c) * 256
            for p in range(2):
                for z in range(2):
                    t = tap(1 + p - z, b, c)
                    mixed[base + p * C : base + (p + 1) * C, z * C : (z + 1) * C] = (
                        weight[t * C : (t + 1) * C, :]
                    )

    def tile(i, carry):
        at = pl.multiple_of(i * TILE, TILE)
        out[pl.ds(at, TILE), :] = jnp.dot(
            taps_of(field, at, TILE), mixed[...], preferred_element_type=F32
        )
        return carry

    lax.fori_loop(0, CELLS // TILE, tile, 0)
    for p in range(2):
        vol_t[p * C : (p + 1) * C, :] = jnp.transpose(vol[p])


def inner_conv(vol, weight):
    return pl.pallas_call(
        inner_kernel,
        out_shape=[
            jax.ShapeDtypeStruct((CELLS, 2 * C), F32),
            jax.ShapeDtypeStruct((2 * C, CELLS), BF),
        ],
        in_specs=[VMEM, VMEM],
        out_specs=[VMEM, VMEM],
        scratch_shapes=[
            pltpu.VMEM((3, PADDED, 2 * C), BF),
            pltpu.VMEM((9 * 256, 2 * C), BF),
        ],
        compiler_params=PARAMS,
        cost_estimate=cost(2 * CELLS * 2304 * 256, 5 << 20),
        name="inner_conv",
    )(vol, weight)


def outer_kernel(before, after, weight, inner, upstream, grad, field, mixed):
    shifted_columns([before, after], field, 0, False)
    blank = jnp.zeros((C, C), BF)
    for b in range(3):
        for c in range(3):
            base = (b * 3 + c) * 256
            low, high = tap(0, b, c), tap(2, b, c)
            mixed[base : base + C, 0:C] = weight[low * C : (low + 1) * C, :]
            mixed[base : base + C, C : 2 * C] = blank
            mixed[base + C : base + 2 * C, 0:C] = blank
            mixed[base + C : base + 2 * C, C : 2 * C] = weight[
                high * C : (high + 1) * C, :
            ]

    def tile(i, carry):
        at = pl.multiple_of(i * TILE, TILE)
        rows = pl.ds(at, TILE)
        preact = inner[rows, :] + jnp.dot(
            taps_of(field, at, TILE), mixed[...], preferred_element_type=F32
        )
        s = jax.nn.sigmoid(preact)
        slopes = s * (1.0 + preact * (1.0 - s))
        for z in range(2):
            grad[z, rows, :] = (
                upstream[z, rows, :].astype(F32) * slopes[:, z * C : (z + 1) * C]
            ).astype(BF)
        return carry

    lax.fori_loop(0, CELLS // TILE, tile, 0)


def outer_conv(before, after, weight, inner, upstream):
    return pl.pallas_call(
        outer_kernel,
        out_shape=jax.ShapeDtypeStruct((2, CELLS, C), BF),
        in_specs=[VMEM] * 5,
        out_specs=VMEM,
        scratch_shapes=[
            pltpu.VMEM((3, PADDED, 2 * C), BF),
            pltpu.VMEM((9 * 256, 2 * C), BF),
        ],
        compiler_params=PARAMS,
        cost_estimate=cost(2 * CELLS * 2304 * 256, 6 << 20, CELLS * 256),
        name="outer_conv",
    )(before, after, weight, inner, upstream)


def taps_kernel(core_ref, grad, before, after, vol_t, kept, sent, field, lhs):
    core = core_ref[0]
    shifted_columns([grad.at[0], grad.at[1]], field, 0, False)
    lhs[0:C, :] = jnp.transpose(before[...])
    lhs[C : 3 * C, :] = vol_t[...]
    lhs[3 * C : 4 * C, :] = jnp.transpose(after[...])

    def store(j, block):
        group = j // 27
        owner = j - group * 27
        at = (owner % 16) * 4 + group

        @pl.when(owner // 16 == core)
        def _():
            kept[at] = block

        @pl.when(owner // 16 != core)
        def _():
            sent[at] = block.astype(BF)

    for owner in range(27, 32):
        for group in range(4):
            kept[(owner % 16) * 4 + group] = jnp.zeros((CHUNK, C), F32)
            sent[(owner % 16) * 4 + group] = jnp.zeros((CHUNK, C), BF)

    def row(b, carry):
        at = pl.multiple_of((2 - b) * COLS, COLS)
        for c in range(3):
            got = jnp.dot(
                lhs[...],
                field[2 - c, pl.ds(at, CELLS), :],
                preferred_element_type=F32,
            )
            for a in range(3):
                whole = (
                    got[a * C : (a + 1) * C, 0:C]
                    + got[(a + 1) * C : (a + 2) * C, C : 2 * C]
                )
                for i in range(4):
                    store(
                        4 * tap(a, b, c) + i, whole[i * CHUNK : (i + 1) * CHUNK, :]
                    )
        return carry

    lax.fori_loop(0, 3, row, 0)


def kernel_gradient(core, grad, before, after, vol_t):
    return pl.pallas_call(
        taps_kernel,
        out_shape=[
            jax.ShapeDtypeStruct((64, CHUNK, C), F32),
            jax.ShapeDtypeStruct((64, CHUNK, C), BF),
        ],
        in_specs=[SMEM] + [VMEM] * 4,
        out_specs=[VMEM, VMEM],
        scratch_shapes=[
            pltpu.VMEM((3, PADDED, 2 * C), BF),
            pltpu.VMEM((4 * C, CELLS), BF),
        ],
        compiler_params=PARAMS,
        cost_estimate=cost(2 * CELLS * 4608 * 256, 5 << 20),
        name="kernel_gradient",
    )(core, grad, before, after, vol_t)


def back_kernel(before, grad, after, weight, upstream, out, field, mixed):
    shifted_columns([before, grad.at[0], grad.at[1], after], field, 0, False)
    blank = jnp.zeros((C, C), BF)
    for b in range(3):
        for c in range(3):
            base = (b * 3 + c) * 512
            for p in range(4):
                for z in range(2):
                    a = 2 - (p - z)
                    t = tap(a, 2 - b, 2 - c)
                    mixed[z * C : (z + 1) * C, base + p * C : base + (p + 1) * C] = (
                        weight[t * C : (t + 1) * C, :] if 0 <= a < 3 else blank
                    )

    def tile(i, carry):
        at = pl.multiple_of(i * TILE, TILE)
        rows = pl.ds(at, TILE)
        got = lax.dot_general(
            taps_of(field, at, TILE),
            mixed[...],
            (((1,), (1,)), ((), ())),
            preferred_element_type=F32,
        )
        for z in range(2):
            out[z, rows, :] = (
                upstream[z, rows, :].astype(F32) + got[:, z * C : (z + 1) * C]
            ).astype(BF)
        return carry

    lax.fori_loop(0, CELLS // TILE, tile, 0)


def back_conv(before, grad, after, weight, upstream):
    return pl.pallas_call(
        back_kernel,
        out_shape=jax.ShapeDtypeStruct((2, CELLS, C), BF),
        in_specs=[VMEM] * 5,
        out_specs=VMEM,
        scratch_shapes=[
            pltpu.VMEM((3, PADDED, 4 * C), BF),
            pltpu.VMEM((2 * C, 9 * 512), BF),
        ],
        compiler_params=PARAMS,
        cost_estimate=cost(2 * CELLS * 4608 * 256, 5 << 20),
        name="back_conv",
    )(before, grad, after, weight, upstream)


def adam(grad, first, second):
    m_new = beta_one * first + (1.0 - beta_one) * grad
    v_new = beta_two * second + (1.0 - beta_two) * grad * grad
    return (
        m_new
        / (1.0 - beta_one**ADAM_STEP)
        / (jnp.sqrt(v_new / (1.0 - beta_two**ADAM_STEP)) + eps_adam)
    )


def from_neighbours(planes):
    size = lax.axis_size(SPACE)
    up = [(i, i + 1) for i in range(size - 1)]
    down = [(j, i) for i, j in up]
    return lax.ppermute(planes[1], SPACE, up), lax.ppermute(planes[0], SPACE, down)


def reduced_direction(kept, sent, core, first_moment, second_moment):
    rows, channels = first_moment.shape
    pad = OWNERS * CHUNK - rows
    mine_at = core * 16 + lax.axis_index("x") * 4 + lax.axis_index("y")
    other = lax.ppermute(sent, "core", [(0, 1), (1, 0)])
    half = (kept + other.astype(F32)).astype(BF).reshape(16, 4, CHUNK, channels)
    got = lax.all_to_all(half, ("x", "y"), 0, 0)
    part = jnp.sum(got.astype(F32), axis=0)
    part = jnp.broadcast_to(part[None], (2,) + part.shape).reshape(8, CHUNK, channels)
    got = lax.all_to_all(part, ("zl", "sample"), 0, 0)
    summed = jnp.sum(got, axis=0)
    first = jnp.pad(first_moment, ((0, pad), (0, 0)))
    second = jnp.pad(second_moment, ((0, pad), (0, 0)), constant_values=1.0)
    first = lax.dynamic_slice_in_dim(first, mine_at * CHUNK, CHUNK, 0)
    second = lax.dynamic_slice_in_dim(second, mine_at * CHUNK, CHUNK, 0)
    step = adam(summed, first, second)
    step = jnp.broadcast_to(step[None], (OWNERS, CHUNK, channels))
    whole = lax.all_to_all(step, ("core", "x", "y"), 0, 0)
    return whole.reshape(OWNERS * CHUNK, channels)[:rows]


def body(volume, upstream, weight, first_moment, second_moment):
    vol = volume.reshape(2, CELLS, C)
    up = upstream.reshape(2, CELLS, C)
    core = lax.axis_index("core")
    before, after = from_neighbours(vol)
    inner, vol_t = inner_conv(vol, weight)
    grad = outer_conv(before, after, weight, inner, up)
    grad_before, grad_after = from_neighbours(grad)
    kept, sent = kernel_gradient(core.reshape(1), grad, before, after, vol_t)
    direction = reduced_direction(kept, sent, core, first_moment, second_moment)
    grad_volume = back_conv(grad_before, grad, grad_after, weight, up)
    return (grad_volume.reshape(volume.shape), direction)


def solution(mesh):
    fine = Mesh(
        mesh.devices.reshape(4, 4, 2, 2, 4), ("x", "y", "zl", "core", "sample")
    )
    field = P("sample", SPACE, None, None, None)
    return jax.shard_map(
        body,
        mesh=fine,
        in_specs=(field, field, P(), P("sample", None), P("sample", None)),
        out_specs=(field, P("sample", None)),
        check_vma=False,
    )
```

profile of v0, /device:TPU:1, one launch (start us, length us, event | category | flops | bytes accessed | tf_op | source)
XLA Modules:
  0.0 102.8 jit_solution(15087490978982098833)
XLA Ops:
  0.6 2.4 %fusion.5 = (bf16[1,1,32,64,128]{4,3,2,1,0:T(8,128)(2,1)}, bf16[1,1,32,64,128]{4,3,2,1,0:T(8,128)(2,1)}) fusion(bf16[1,2,32,64,128]{4,3,2,1,0:T(8,128)(2,1)} %param.5), kind=kLoop, calls=%fused_computation.12 | loop fusion | bytes 2097152 | tf_op jit(solution)/shard_map/slice | solution.py:299
  3.0 4.9 %collective-permute-start = (bf16[2048,128]{1,0:T(8,128)(2,1)}, bf16[2048,128]{1,0:T(8,128)(2,1)S(1)}, u32[]{:S(2)}, u32[]{:S(2)}) collective-permute-start(bf16[2048,128]{1,0:T(8,128)(2,1)} %bitcast), channel_id=1, source_target_pairs={{0,4},{4,8},{8,12},{12,16},{16,20},{20,24},{24,28},{28,32},{32,36}... | collective-permute-start | bytes 1572872 | tf_op jit(solution)/shard_map/ppermute | solution.py:299
  8.0 1.9 %collective-permute-start.1 = (bf16[2048,128]{1,0:T(8,128)(2,1)}, bf16[2048,128]{1,0:T(8,128)(2,1)}, u32[]{:S(2)}, u32[]{:S(2)}) collective-permute-start(bf16[2048,128]{1,0:T(8,128)(2,1)} %bitcast.1), channel_id=1, source_target_pairs={{4,0},{8,4},{12,8},{16,12},{20,16},{24,20},{28,24},{32,28},{36,32}... | collective-permute-start | bytes 1572872 | tf_op jit(solution)/shard_map/ppermute | solution.py:299
  9.9 4.3 %inner_conv.1 = (f32[2048,256]{1,0:T(8,128)S(1)}, bf16[256,2048]{1,0:T(8,128)(2,1)S(1)}) custom-call(bf16[2,2048,128]{2,1,0:T(8,128)(2,1)S(1)} %bitcast.13, bf16[3456,128]{1,0:T(8,128)(2,1)S(1)} %copy-done.2), custom_call_target="tpu_custom_call" | custom-call | flops 2415919104 | bytes 5242880 | tf_op jit(solution)/shard_map/inner_conv/pallas_call | solution.py:106
  14.4 6.9 %collective-permute-done.1.after = bf16[2048,128]{1,0:T(8,128)(2,1)} collective-permute-done((bf16[2048,128]{1,0:T(8,128)(2,1)}, bf16[2048,128]{1,0:T(8,128)(2,1)}, u32[]{:S(2)}, u32[]{:S(2)}) %collective-permute-start.1) | collective-permute-done | bytes 524320 | tf_op jit(solution)/shard_map/ppermute | solution.py:299
  21.3 5.2 %outer_conv.1.grad = bf16[2,2048,128]{2,1,0:T(8,128)(2,1)S(1)} custom-call(bf16[2048,128]{1,0:T(8,128)(2,1)S(1)} %collective-permute-done.before, bf16[2048,128]{1,0:T(8,128)(2,1)} %collective-permute-done.1.after, bf16[3456,128]{1,0:T(8,128)(2,1)S(1)} %copy-done.2, f32[2048,256]{1,0:T(8,128)S(1)} %get-tuple-element.6.inner, bf16[2,2048,128]{2,1,0:T(8,128)(2,1)S(1)} %bitcast.14), custom_call_target="tpu_custom_call" | custom-call | flops 2415919104 | bytes 6291456 | tf_op jit(solution)/shard_map/outer_conv/pallas_call | solution.py:156
  26.5 14.3 %kernel_gradient.1 = (f32[64,32,128]{2,1,0:T(8,128)S(1)}, bf16[64,32,128]{2,1,0:T(8,128)(2,1)S(1)}) custom-call(s32[1]{0:T(128)} %bitcast.7.core_ref, bf16[2,2048,128]{2,1,0:T(8,128)(2,1)S(1)} %outer_conv.1.grad, bf16[2048,128]{1,0:T(8,128)(2,1)S(1)} %collective-permute-done.before, bf16[2048,128]{1,0:T(8,128)(2,1)} %collective-permute-done.1.after, ...), custom_call_target="tpu_custom_call" | custom-call | flops 4831838208 | bytes 5242880 | tf_op jit(solution)/shard_map/kernel_gradient/pallas_call | solution.py:219
  41.0 1.9 %collective-permute-done.4 = bf16[64,32,128]{2,1,0:T(8,128)(2,1)S(1)} collective-permute-done((bf16[64,32,128]{2,1,0:T(8,128)(2,1)S(1)}, bf16[64,32,128]{2,1,0:T(8,128)(2,1)S(1)}, u32[]{:S(2)}, u32[]{:S(2)}) %collective-permute-start.4) | collective-permute-done | bytes 524320 | tf_op jit(solution)/shard_map/ppermute | solution.py:306
  42.9 1.0 add_convert_fusion
  43.8 6.5 %all-to-all-start = ((bf16[16,4,32,128]{3,2,1,0:T(8,128)(2,1)}), bf16[16,4,32,128]{3,2,1,0:T(8,128)(2,1)}, u32[]{:S(2)}, u32[]{:S(2)}) async-start(bf16[16,4,32,128]{3,2,1,0:T(8,128)(2,1)} %bitcast.8), calls=%async_computation | async-start | bytes 1048576 | tf_op jit(solution)/shard_map/all_to_all | solution.py:308
  50.3 1.0 %slice_bitcast_fusion = (bf16[2048,128]{1,0:T(8,128)(2,1)}, bf16[2048,128]{1,0:T(8,128)(2,1)}) fusion(bf16[2,2048,128]{2,1,0:T(8,128)(2,1)S(1)} %outer_conv.1.grad), kind=kLoop, calls=%fused_computation.2 | loop fusion | bytes 2097152 | tf_op jit(solution)/shard_map/squeeze | solution.py:299
  51.4 3.9 %collective-permute-start.2 = (bf16[2048,128]{1,0:T(8,128)(2,1)}, bf16[2048,128]{1,0:T(8,128)(2,1)S(1)}, u32[]{:S(2)}, u32[]{:S(2)}) collective-permute-start(bf16[2048,128]{1,0:T(8,128)(2,1)} %get-tuple-element.11), channel_id=1, source_target_pairs={{0,4},{4,8},{8,12},{12,16},{16,20},{20,24},{24,28},{28,32},{32,36}... | collective-permute-start | bytes 1572872 | tf_op jit(solution)/shard_map/ppermute | solution.py:299
  55.2 1.9 %collective-permute-start.3 = (bf16[2048,128]{1,0:T(8,128)(2,1)}, bf16[2048,128]{1,0:T(8,128)(2,1)}, u32[]{:S(2)}, u32[]{:S(2)}) collective-permute-start(bf16[2048,128]{1,0:T(8,128)(2,1)} %get-tuple-element.10), channel_id=1, source_target_pairs={{4,0},{8,4},{12,8},{16,12},{20,16},{24,20},{28,24},{32,28},{36,32}... | collective-permute-start | bytes 1572872 | tf_op jit(solution)/shard_map/ppermute | solution.py:299
  57.2 3.9 %all-to-all-done = bf16[16,4,32,128]{3,2,1,0:T(8,128)(2,1)} async-done(((bf16[16,4,32,128]{3,2,1,0:T(8,128)(2,1)}), bf16[16,4,32,128]{3,2,1,0:T(8,128)(2,1)}, u32[]{:S(2)}, u32[]{:S(2)}) %all-to-all-start) | async-done | bytes 524320 | tf_op jit(solution)/shard_map/all_to_all | solution.py:308
  61.1 1.1 %convert_reduce_fusion = f32[4,32,128]{2,1,0:T(8,128)S(1)} fusion(bf16[16,4,32,128]{3,2,1,0:T(8,128)(2,1)} %all-to-all-done), kind=kLoop, calls=%fused_computation | loop fusion | flops 507904 | bytes 589824 | tf_op jit(solution)/shard_map/reduce_sum | solution.py:309
  62.9 8.2 %all-to-all-start.1 = ((f32[8,32,128]{2,1,0:T(8,128)}), f32[8,32,128]{2,1,0:T(8,128)}, u32[]{:S(2)}, u32[]{:S(2)}) async-start(f32[8,32,128]{2,1,0:T(8,128)} %bitcast.16), calls=%async_computation.1 | async-start | bytes 262144 | tf_op jit(solution)/shard_map/all_to_all | solution.py:311
  71.1 7.1 %all-to-all-done.1 = f32[8,32,128]{2,1,0:T(8,128)} async-done(((f32[8,32,128]{2,1,0:T(8,128)}), f32[8,32,128]{2,1,0:T(8,128)}, u32[]{:S(2)}, u32[]{:S(2)}) %all-to-all-start.1) | async-done | bytes 131104 | tf_op jit(solution)/shard_map/all_to_all | solution.py:311
  78.2 0.9 reduce_sum.19
  79.2 0.8 fusion.4
  79.9 0.9 broadcast_in_dim.5
  80.8 8.8 %all-to-all-start.2 = ((f32[32,32,128]{2,1,0:T(8,128)}), f32[32,32,128]{2,1,0:T(8,128)}, u32[]{:S(2)}, u32[]{:S(2)}) async-start(f32[32,32,128]{2,1,0:T(8,128)} %broadcast_in_dim.5), calls=%async_computation.2 | async-start | bytes 1048576 | tf_op jit(solution)/shard_map/all_to_all | solution.py:319
  89.7 9.4 %back_conv.1 = bf16[2,2048,128]{2,1,0:T(8,128)(2,1)} custom-call(bf16[2048,128]{1,0:T(8,128)(2,1)S(1)} %collective-permute-done.2.before, bf16[2,2048,128]{2,1,0:T(8,128)(2,1)S(1)} %outer_conv.1.grad, bf16[2048,128]{1,0:T(8,128)(2,1)} %collective-permute-done.3.after, bf16[3456,128]{1,0:T(8,128)(2,1)S(1)} %copy-done.2, bf16[2,2048,128]{2,1,0:T(8,128)(2,1)S(1)} %bitcast.15), custom_call_target="tpu_custom_call" | custom-call | flops 4831838208 | bytes 5242880 | tf_op jit(solution)/shard_map/back_conv/pallas_call | solution.py:270
  99.1 1.9 %all-to-all-done.2 = f32[32,32,128]{2,1,0:T(8,128)} async-done(((f32[32,32,128]{2,1,0:T(8,128)}), f32[32,32,128]{2,1,0:T(8,128)}, u32[]{:S(2)}, u32[]{:S(2)}) %all-to-all-start.2) | async-done | bytes 524320 | tf_op jit(solution)/shard_map/all_to_all | solution.py:319
  101.0 1.8 %slice.28 = f32[27,32,128]{2,1,0:T(8,128)} slice(f32[32,32,128]{2,1,0:T(8,128)} %all-to-all-done.2), slice={[0:27], [0:32], [0:128]} | slice | bytes 884736 | tf_op jit(solution)/shard_map/slice | solution.py:320
  (11 shorter events, 0.9 us)
Async XLA Ops:
  0.6 9.3 %copy-start = (bf16[1,2,32,64,128]{4,3,2,1,0:T(8,128)(2,1)S(1)}, bf16[1,2,32,64,128]{4,3,2,1,0:T(8,128)(2,1)}, u32[]{:S(2)}) copy-start(bf16[1,2,32,64,128]{4,3,2,1,0:T(8,128)(2,1)} %param.5) | copy-start | bytes 3145732
  0.6 9.3 %copy-start.2 = (bf16[3456,128]{1,0:T(8,128)(2,1)S(1)}, bf16[3456,128]{1,0:T(8,128)(2,1)}, u32[]{:S(2)}) copy-start(bf16[3456,128]{1,0:T(8,128)(2,1)} %weight.5) | copy-start | bytes 2654212
  3.0 11.4 %collective-permute-start = (bf16[2048,128]{1,0:T(8,128)(2,1)}, bf16[2048,128]{1,0:T(8,128)(2,1)S(1)}, u32[]{:S(2)}, u32[]{:S(2)}) collective-permute-start(bf16[2048,128]{1,0:T(8,128)(2,1)} %bitcast), channel_id=1, source_target_pairs={{0,4},{4,8},{8,12},{12,16},{16,20},{20,24},{24,28},{28,32},{32,36}... | collective-permute-start | bytes 1572872 | tf_op jit(solution)/shard_map/ppermute | solution.py:299
  8.0 13.3 %collective-permute-start.1 = (bf16[2048,128]{1,0:T(8,128)(2,1)}, bf16[2048,128]{1,0:T(8,128)(2,1)}, u32[]{:S(2)}, u32[]{:S(2)}) collective-permute-start(bf16[2048,128]{1,0:T(8,128)(2,1)} %bitcast.1), channel_id=1, source_target_pairs={{4,0},{8,4},{12,8},{16,12},{20,16},{24,20},{28,24},{32,28},{36,32}... | collective-permute-start | bytes 1572872 | tf_op jit(solution)/shard_map/ppermute | solution.py:299
  9.9 11.4 %copy-start.1 = (bf16[1,2,32,64,128]{4,3,2,1,0:T(8,128)(2,1)S(1)}, bf16[1,2,32,64,128]{4,3,2,1,0:T(8,128)(2,1)}, u32[]{:S(2)}) copy-start(bf16[1,2,32,64,128]{4,3,2,1,0:T(8,128)(2,1)} %param.6) | copy-start | bytes 3145732
  40.9 2.0 %collective-permute-start.4 = (bf16[64,32,128]{2,1,0:T(8,128)(2,1)S(1)}, bf16[64,32,128]{2,1,0:T(8,128)(2,1)S(1)}, u32[]{:S(2)}, u32[]{:S(2)}) collective-permute-start(bf16[64,32,128]{2,1,0:T(8,128)(2,1)S(1)} %get-tuple-element.9), channel_id=1, source_target_pairs={{0,4},{4,0},{1,5},{5,1},{2,6},{6,2},{3,7},{7,3},{8,12},{12,8},{9,1... | collective-permute-start | bytes 1572872 | tf_op jit(solution)/shard_map/ppermute | solution.py:306
  43.8 17.3 %all-to-all-start = ((bf16[16,4,32,128]{3,2,1,0:T(8,128)(2,1)}), bf16[16,4,32,128]{3,2,1,0:T(8,128)(2,1)}, u32[]{:S(2)}, u32[]{:S(2)}) async-start(bf16[16,4,32,128]{3,2,1,0:T(8,128)(2,1)} %bitcast.8), calls=%async_computation | async-start | bytes 1048576 | tf_op jit(solution)/shard_map/all_to_all | solution.py:308
  51.4 38.3 %collective-permute-start.2 = (bf16[2048,128]{1,0:T(8,128)(2,1)}, bf16[2048,128]{1,0:T(8,128)(2,1)S(1)}, u32[]{:S(2)}, u32[]{:S(2)}) collective-permute-start(bf16[2048,128]{1,0:T(8,128)(2,1)} %get-tuple-element.11), channel_id=1, source_target_pairs={{0,4},{4,8},{8,12},{12,16},{16,20},{20,24},{24,28},{28,32},{32,36}... | collective-permute-start | bytes 1572872 | tf_op jit(solution)/shard_map/ppermute | solution.py:299
  55.2 34.4 %collective-permute-start.3 = (bf16[2048,128]{1,0:T(8,128)(2,1)}, bf16[2048,128]{1,0:T(8,128)(2,1)}, u32[]{:S(2)}, u32[]{:S(2)}) collective-permute-start(bf16[2048,128]{1,0:T(8,128)(2,1)} %get-tuple-element.10), channel_id=1, source_target_pairs={{4,0},{8,4},{12,8},{16,12},{20,16},{24,20},{28,24},{32,28},{36,32}... | collective-permute-start | bytes 1572872 | tf_op jit(solution)/shard_map/ppermute | solution.py:299
  62.9 15.3 %all-to-all-start.1 = ((f32[8,32,128]{2,1,0:T(8,128)}), f32[8,32,128]{2,1,0:T(8,128)}, u32[]{:S(2)}, u32[]{:S(2)}) async-start(f32[8,32,128]{2,1,0:T(8,128)} %bitcast.16), calls=%async_computation.1 | async-start | bytes 262144 | tf_op jit(solution)/shard_map/all_to_all | solution.py:311
  80.8 20.2 %all-to-all-start.2 = ((f32[32,32,128]{2,1,0:T(8,128)}), f32[32,32,128]{2,1,0:T(8,128)}, u32[]{:S(2)}, u32[]{:S(2)}) async-start(f32[32,32,128]{2,1,0:T(8,128)} %broadcast_in_dim.5), calls=%async_computation.2 | async-start | bytes 1048576 | tf_op jit(solution)/shard_map/all_to_all | solution.py:319
where the time goes:
time: 104 us; the launch traced here: 103 us
  starting transfers between devices  36.3 us (35%)
  Pallas kernels  33.3 us (32%)
  waiting for transfers between devices  21.9 us (21%)
  local copies, waits for them, and re-layouts  6.78 us (7%)
  other arithmetic  3.77 us (4%)
    pallas_call x1, Pallas kernels, kernel_gradient(): pl.pallas_call(taps_kernel, out_shape=[jax.ShapeDtypeStruct((64, CHUNK, C...  14.3 us
    pallas_call x1, Pallas kernels, back_conv(): pl.pallas_call(back_kernel, out_shape=jax.ShapeDtypeStruct((2, CELLS, C),...  9.41 us
    all_to_all x1, starting transfers between devices, reduced_direction(): whole = lax.all_to_all(step, ('core', 'x', 'y'), 0, 0)  8.85 us
    ppermute x2, starting transfers between devices, from_neighbours(): lax.ppermute(planes[1], SPACE, up)  8.77 us
    all_to_all x1, starting transfers between devices, reduced_direction(): got = lax.all_to_all(part, ('zl', 'sample'), 0, 0)  8.19 us
    all_to_all x1, waiting for transfers between devices, reduced_direction(): got = lax.all_to_all(part, ('zl', 'sample'), 0, 0)  7.13 us
    ppermute x2, waiting for transfers between devices, from_neighbours(): lax.ppermute(planes[0], SPACE, down)  6.9 us
    all_to_all x1, starting transfers between devices, reduced_direction(): got = lax.all_to_all(half, ('x', 'y'), 0, 0)  6.51 us
  transfers between devices with their start and end apart: 8, of which 6 were waited for; matrix products, arithmetic and copies ran while one was open for 5% of the time, Pallas kernels for 13%

commit v1 on v0

v1 whole, which is shorter than its diff:
```python
import functools
import jax
import jax.numpy as jnp
from jax import lax
from jax.experimental import pallas as pl
from jax.experimental.pallas import tpu as pltpu
from jax.sharding import Mesh, PartitionSpec as P

ADAM_STEP = 10


beta_one = 0.9
beta_two = 0.999
eps_adam = 1e-08

SPACE = ("x", "y", "zl", "core")
CHUNK = 32
OWNERS = 32
C = 128
COLS = 64
ROWS = 32
CELLS = ROWS * COLS
PADDED = CELLS + 2 * COLS
STRIP = 256
TILE = 512
BF = jnp.bfloat16
F32 = jnp.float32
VMEM = pl.BlockSpec(memory_space=pltpu.VMEM)
ANY = pl.BlockSpec(memory_space=pl.ANY)
SMEM = pl.BlockSpec(memory_space=pltpu.SMEM)
SMALL = pltpu.CompilerParams(vmem_limit_bytes=4 * 1024 * 1024)
PARAMS = pltpu.CompilerParams(vmem_limit_bytes=32 * 1024 * 1024)


def cost(flops, moved, special=0):
    return pl.CostEstimate(flops=flops, bytes_accessed=moved, transcendentals=special)


def shifted_columns(planes, out, first, flip):
    width = 128 * len(planes)
    blank = jnp.zeros((COLS, width), BF)
    cols = slice(first, first + width)
    for c in range(3):
        out[c, 0:COLS, cols] = blank
        out[c, PADDED - COLS : PADDED, cols] = blank
    before, after = (2, 0) if flip else (0, 2)

    def strip(i, carry):
        at = pl.multiple_of(i * STRIP, STRIP)
        to = pl.ds(pl.multiple_of(at + COLS, COLS), STRIP)
        col = lax.broadcasted_iota(jnp.int32, (STRIP, C), 0) & (COLS - 1)
        for k, plane in enumerate(planes):
            cols = slice(first + k * C, first + (k + 1) * C)
            here = plane[pl.ds(at, STRIP), :]
            wide = here.astype(F32)
            out[1, to, cols] = here
            out[before, to, cols] = jnp.where(
                col == 0, 0.0, pltpu.roll(wide, 1, 0)
            ).astype(BF)
            out[after, to, cols] = jnp.where(
                col == COLS - 1, 0.0, pltpu.roll(wide, STRIP - 1, 0)
            ).astype(BF)
        return carry

    lax.fori_loop(0, CELLS // STRIP, strip, 0)


def transposed(plane, out, first):
    for at in range(0, CELLS, TILE):
        out[first : first + C, at : at + TILE] = jnp.transpose(
            plane[at : at + TILE, :]
        )


def tap(a, b, c):
    return (a * 3 + b) * 3 + c


def taps_of(field, at, rows):
    return jnp.concatenate(
        [
            field[c, pl.ds(pl.multiple_of(at + b * COLS, COLS), rows), :]
            for b in range(3)
            for c in range(3)
        ],
        axis=1,
    )


def inner_kernel(vol, weight, low, high, vol_t, field, mixed):
    shifted_columns([vol.at[0], vol.at[1]], field, 0, False)
    for b in range(3):
        for c in range(3):
            base = (b * 3 + c) * 256
            for p in range(2):
                for z in range(2):
                    t = tap(1 + p - z, b, c)
                    mixed[base + p * C : base + (p + 1) * C, z * C : (z + 1) * C] = (
                        weight[t * C : (t + 1) * C, :]
                    )

    def tile(i, carry):
        at = pl.multiple_of(i * TILE, TILE)
        got = jnp.dot(taps_of(field, at, TILE), mixed[...], preferred_element_type=F32)
        low[pl.ds(at, TILE), :] = got[:, 0:C]
        high[pl.ds(at, TILE), :] = got[:, C : 2 * C]
        return carry

    lax.fori_loop(0, CELLS // TILE, tile, 0)
    for p in range(2):
        transposed(vol.at[p], vol_t, p * C)


def inner_conv(vol, weight):
    return pl.pallas_call(
        inner_kernel,
        out_shape=[
            jax.ShapeDtypeStruct((CELLS, C), F32),
            jax.ShapeDtypeStruct((CELLS, C), F32),
            jax.ShapeDtypeStruct((2 * C, CELLS), BF),
        ],
        in_specs=[VMEM, VMEM],
        out_specs=[VMEM] * 3,
        scratch_shapes=[
            pltpu.VMEM((3, PADDED, 2 * C), BF),
            pltpu.VMEM((9 * 256, 2 * C), BF),
        ],
        compiler_params=PARAMS,
        cost_estimate=cost(2 * CELLS * 2304 * 256, 5 << 20),
        name="inner_conv",
    )(vol, weight)


def outer_kernel(z, halo, weight, inner, upstream, grad, field):
    shifted_columns([halo], field, 0, False)
    first = tap(2 * z, 0, 0) * C

    def tile(i, carry):
        at = pl.multiple_of(i * TILE, TILE)
        rows = pl.ds(at, TILE)
        preact = inner[rows, :] + jnp.dot(
            taps_of(field, at, TILE),
            weight[first : first + 9 * C, :],
            preferred_element_type=F32,
        )
        s = jax.nn.sigmoid(preact)
        slopes = s * (1.0 + preact * (1.0 - s))
        grad[rows, :] = (upstream[z, rows, :].astype(F32) * slopes).astype(BF)
        return carry

    lax.fori_loop(0, CELLS // TILE, tile, 0)


def outer_conv(z, halo, weight, inner, upstream):
    return pl.pallas_call(
        functools.partial(outer_kernel, z),
        out_shape=jax.ShapeDtypeStruct((CELLS, C), BF),
        in_specs=[VMEM] * 4,
        out_specs=VMEM,
        scratch_shapes=[pltpu.VMEM((3, PADDED, C), BF)],
        compiler_params=PARAMS,
        cost_estimate=cost(2 * CELLS * 1152 * 256, 3 << 20, CELLS * 128),
        name=f"outer_conv_{z}",
    )(halo, weight, inner, upstream)


def taps_kernel(core_ref, low, high, before, after, vol_t, kept, sent, field, lhs, whole):
    core = core_ref[0]
    shifted_columns([low, high], field, 0, False)
    lhs[C : 3 * C, :] = vol_t[...]
    transposed(before, lhs, 0)
    transposed(after, lhs, 3 * C)

    for owner in range(27, 32):
        for group in range(4):
            whole[group * 32 + owner] = jnp.zeros((CHUNK, C), F32)

    def row(b, carry):
        at = pl.multiple_of((2 - b) * COLS, COLS)
        for c in range(3):
            got = jnp.dot(
                lhs[...],
                field[2 - c, pl.ds(at, CELLS), :],
                preferred_element_type=F32,
            )
            for a in range(3):
                summed = (
                    got[a * C : (a + 1) * C, 0:C]
                    + got[(a + 1) * C : (a + 2) * C, C : 2 * C]
                )
                for i in range(4):
                    chunk = 4 * tap(a, b, c) + i
                    whole[chunk + 5 * (chunk // 27)] = summed[
                        i * CHUNK : (i + 1) * CHUNK, :
                    ]
        return carry

    lax.fori_loop(0, 3, row, 0)

    def share(owner, carry):
        for group in range(4):
            kept[owner * 4 + group] = whole[group * 32 + core * 16 + owner]
            sent[owner * 4 + group] = whole[
                group * 32 + (1 - core) * 16 + owner
            ].astype(BF)
        return carry

    lax.fori_loop(0, 16, share, 0)


def kernel_gradient(core, low, high, before, after, vol_t):
    return pl.pallas_call(
        taps_kernel,
        out_shape=[
            jax.ShapeDtypeStruct((64, CHUNK, C), F32),
            jax.ShapeDtypeStruct((64, CHUNK, C), BF),
        ],
        in_specs=[SMEM] + [VMEM] * 5,
        out_specs=[VMEM, VMEM],
        scratch_shapes=[
            pltpu.VMEM((3, PADDED, 2 * C), BF),
            pltpu.VMEM((4 * C, CELLS), BF),
            pltpu.VMEM((4 * 32, CHUNK, C), F32),
        ],
        compiler_params=PARAMS,
        cost_estimate=cost(2 * CELLS * 4608 * 256, 5 << 20),
        name="kernel_gradient",
    )(core, low, high, before, after, vol_t)


def inner_back_kernel(low, high, weight, upstream, later, out, field, mixed):
    shifted_columns([low, high], field, 0, False)
    for b in range(3):
        for c in range(3):
            base = (b * 3 + c) * 256
            for p in range(2):
                for z in range(2):
                    t = tap(1 + z - p, 2 - b, 2 - c)
                    mixed[z * C : (z + 1) * C, base + p * C : base + (p + 1) * C] = (
                        weight[t * C : (t + 1) * C, :]
                    )

    def tile(i, carry):
        at = pl.multiple_of(i * TILE, TILE)
        rows = pl.ds(at, TILE)
        got = lax.dot_general(
            taps_of(field, at, TILE),
            mixed[...],
            (((1,), (1,)), ((), ())),
            preferred_element_type=F32,
        )
        for z in range(2):
            out[z, rows, :] = (
                upstream[z, rows, :].astype(F32) + got[:, z * C : (z + 1) * C]
            )
        return carry

    lax.fori_loop(0, CELLS // TILE, tile, 0)


def inner_back(low, high, weight, upstream, later):
    return pl.pallas_call(
        inner_back_kernel,
        out_shape=jax.ShapeDtypeStruct((2, CELLS, C), F32),
        in_specs=[VMEM] * 4 + [ANY],
        out_specs=VMEM,
        scratch_shapes=[
            pltpu.VMEM((3, PADDED, 2 * C), BF),
            pltpu.VMEM((2 * C, 9 * 256), BF),
        ],
        compiler_params=PARAMS,
        cost_estimate=cost(2 * CELLS * 2304 * 256, 5 << 20),
        name="inner_back",
    )(low, high, weight, upstream, later)


def outer_back_kernel(before, after, weight, inner, out, field, mixed):
    shifted_columns([before, after], field, 0, False)
    for b in range(3):
        for c in range(3):
            base = (b * 3 + c) * C
            for z in range(2):
                t = tap(2 - 2 * z, 2 - b, 2 - c)
                mixed[z, :, base : base + C] = weight[t * C : (t + 1) * C, :]

    def tile(i, carry):
        at = pl.multiple_of(i * TILE, TILE)
        rows = pl.ds(at, TILE)
        for z in range(2):
            lhs = jnp.concatenate(
                [
                    field[
                        c,
                        pl.ds(pl.multiple_of(at + b * COLS, COLS), TILE),
                        z * C : (z + 1) * C,
                    ]
                    for b in range(3)
                    for c in range(3)
                ],
                axis=1,
            )
            got = lax.dot_general(
                lhs, mixed[z], (((1,), (1,)), ((), ())), preferred_element_type=F32
            )
            out[z, rows, :] = (inner[z, rows, :] + got).astype(BF)
        return carry

    lax.fori_loop(0, CELLS // TILE, tile, 0)


def outer_back(before, after, weight, inner):
    return pl.pallas_call(
        outer_back_kernel,
        out_shape=jax.ShapeDtypeStruct((2, CELLS, C), BF),
        in_specs=[VMEM] * 4,
        out_specs=VMEM,
        scratch_shapes=[
            pltpu.VMEM((3, PADDED, 2 * C), BF),
            pltpu.VMEM((2, C, 9 * C), BF),
        ],
        compiler_params=PARAMS,
        cost_estimate=cost(2 * CELLS * 2304 * 256, 5 << 20),
        name="outer_back",
    )(before, after, weight, inner)


def planes_kernel(vol, low, high, sems):
    first = pltpu.make_async_copy(vol.at[0], low, sems.at[0])
    second = pltpu.make_async_copy(vol.at[1], high, sems.at[1])
    first.start()
    second.start()
    first.wait()
    second.wait()


def both_planes(vol):
    plane = jax.ShapeDtypeStruct((CELLS, C), BF)
    return pl.pallas_call(
        planes_kernel,
        out_shape=[plane, plane],
        in_specs=[ANY],
        out_specs=[ANY, ANY],
        scratch_shapes=[pltpu.SemaphoreType.DMA((2,))],
        compiler_params=SMALL,
        cost_estimate=cost(0, 2 << 20),
        name="both_planes",
    )(vol)


def first_rows_kernel(whole, out, sem):
    copy = pltpu.make_async_copy(whole.at[0 : out.shape[0]], out, sem)
    copy.start()
    copy.wait()


def first_rows(whole, rows):
    return pl.pallas_call(
        first_rows_kernel,
        out_shape=jax.ShapeDtypeStruct((rows, C), F32),
        in_specs=[VMEM],
        out_specs=ANY,
        scratch_shapes=[pltpu.SemaphoreType.DMA],
        compiler_params=SMALL,
        cost_estimate=cost(0, 1 << 20),
        name="first_rows",
    )(whole)


def mix_kernel(got, out):
    for group in range(4):
        total = got[0, group].astype(F32)
        for k in range(1, 16):
            total += got[k, group].astype(F32)
        out[group] = total
        out[4 + group] = total


def mixed_rows(got):
    return pl.pallas_call(
        mix_kernel,
        out_shape=jax.ShapeDtypeStruct((8, CHUNK, C), F32),
        in_specs=[VMEM],
        out_specs=VMEM,
        compiler_params=SMALL,
        cost_estimate=cost(1 << 18, 1 << 20),
        name="mixed_rows",
    )(got)


def step_kernel(at_ref, got, first, second, later, out):
    total = got[0]
    for k in range(1, 8):
        total += got[k]
    at = pl.multiple_of(at_ref[0], CHUNK)
    rows = pl.ds(at, CHUNK)
    step = adam(total, first[rows, :], second[rows, :])
    for k in range(OWNERS):
        out[k] = step


def spread_step(at, got, first, second, later):
    return pl.pallas_call(
        step_kernel,
        out_shape=jax.ShapeDtypeStruct((OWNERS, CHUNK, C), F32),
        in_specs=[SMEM] + [VMEM] * 3 + [ANY],
        out_specs=VMEM,
        compiler_params=SMALL,
        cost_estimate=cost(1 << 18, 1 << 20),
        name="spread_step",
    )(at, got, first, second, later)


def adam(grad, first, second):
    m_new = beta_one * first + (1.0 - beta_one) * grad
    v_new = beta_two * second + (1.0 - beta_two) * grad * grad
    return (
        m_new
        / (1.0 - beta_one**ADAM_STEP)
        / (jnp.sqrt(v_new / (1.0 - beta_two**ADAM_STEP)) + eps_adam)
    )


def from_neighbours(low, high):
    size = lax.axis_size(SPACE)
    up = [(i, i + 1) for i in range(size - 1)]
    down = [(j, i) for i, j in up]
    return lax.ppermute(high, SPACE, up), lax.ppermute(low, SPACE, down)


def body(volume, upstream, weight, first_moment, second_moment):
    vol = volume.reshape(2, CELLS, C)
    up = upstream.reshape(2, CELLS, C)
    core = lax.axis_index("core")
    before, after = from_neighbours(*both_planes(vol))
    inner_low, inner_high, vol_t = inner_conv(vol, weight)
    low = outer_conv(0, before, weight, inner_low, up)
    high = outer_conv(1, after, weight, inner_high, up)
    kept, sent = kernel_gradient(core.reshape(1), low, high, before, after, vol_t)

    rows = first_moment.shape[0]
    other = lax.ppermute(sent, "core", [(0, 1), (1, 0)])
    half = (kept + other.astype(F32)).astype(BF).reshape(16, 4, CHUNK, C)
    got = lax.all_to_all(half, ("x", "y"), 0, 0)
    grad_before, grad_after = from_neighbours(low, high)
    part = mixed_rows(got)
    got = lax.all_to_all(part, ("zl", "sample"), 0, 0)
    local = inner_back(low, high, weight, up, part)
    owner = core * 16 + lax.axis_index("x") * 4 + lax.axis_index("y")
    at = jnp.minimum(owner * CHUNK, rows - CHUNK).reshape(1)
    step = spread_step(at, got, first_moment, second_moment, local)
    whole = lax.all_to_all(step, ("core", "x", "y"), 0, 0)
    direction = first_rows(whole.reshape(OWNERS * CHUNK, C), rows)
    grad_volume = outer_back(grad_before, grad_after, weight, local)
    return (grad_volume.reshape(volume.shape), direction)


def solution(mesh):
    fine = Mesh(
        mesh.devices.reshape(4, 4, 2, 2, 4), ("x", "y", "zl", "core", "sample")
    )
    field = P("sample", SPACE, None, None, None)
    return jax.shard_map(
        body,
        mesh=fine,
        in_specs=(field, field, P(), P("sample", None), P("sample", None)),
        out_specs=(field, P("sample", None)),
        check_vma=False,
    )
```

time: 104 us -> 94 us (0.904)
  waiting for transfers between devices: 21.9 us -> 7.04 us
  starting transfers between devices: 36.3 us -> 44.7 us
  other arithmetic: 3.77 us -> 0.99 us
    all_to_all x3, waiting for transfers between devices: 13 us -> 5.49 us  [the longest x1 3.92 us: body(): whole = lax.all_to_all(step, ('core', 'x', 'y'), 0, 0)]
    ppermute x5, waiting for transfers between devices: 8.96 us -> 1.55 us  [the longest x1 1.54 us: body(): other = lax.ppermute(sent, 'core', [(0, 1), (1, 0)])]
    unnamed x6 -> x20, local copies, waits for them, and re-layouts: 0.01 us -> 7.17 us
    pallas_call x1, Pallas kernels: 14.3 us -> 7.91 us  [kernel_gradient(): pl.pallas_call(taps_kernel, out_shape=[jax.ShapeDtypeStruct((64, CHUNK, C...]
    pallas_call x3 -> x9, Pallas kernels: 18.9 us -> 24.6 us  [the longest x2 6.41 us: outer_conv(): pl.pallas_call(functools.partial(outer_kernel, z), out_shape=jax.ShapeDty...]
    all_to_all x3, starting transfers between devices: 23.5 us -> 28.2 us  [the longest x1 11.7 us: body(): got = lax.all_to_all(part, ('zl', 'sample'), 0, 0)]
    slice x2 -> x0, local copies, waits for them, and re-layouts: 4.19 us -> none  [the longest x1 2.38 us: from_neighbours(): planes[0]]
    ppermute x5, starting transfers between devices: 12.7 us -> 16.5 us  [the longest x4 15.8 us: from_neighbours(): return (lax.ppermute(high, SPACE, up), lax.ppermute(low, SPACE, down))]
  transfers between devices with their start and end apart: 8 -> 8, of which waited for: 6 -> 3; matrix products, arithmetic and copies ran while one was open for 5% -> 0% of each run, Pallas kernels for 13% -> 22%
where the time goes in v1:
time: 94 us; the launch traced here: 93.2 us
  starting transfers between devices  44.7 us (48%)
  Pallas kernels  32.5 us (35%)
  local copies, waits for them, and re-layouts  7.17 us (8%)
  waiting for transfers between devices  7.04 us (7%)
  other arithmetic  0.99 us (1%)
    ppermute x4, starting transfers between devices, from_neighbours(): return (lax.ppermute(high, SPACE, up), lax.ppermute(low, SPACE, down))  15.8 us
    all_to_all x1, starting transfers between devices, body(): got = lax.all_to_all(part, ('zl', 'sample'), 0, 0)  11.7 us
    all_to_all x1, starting transfers between devices, body(): got = lax.all_to_all(half, ('x', 'y'), 0, 0)  8.78 us
    pallas_call x1, Pallas kernels, kernel_gradient(): pl.pallas_call(taps_kernel, out_shape=[jax.ShapeDtypeStruct((64, CHUNK, C...  7.91 us
    all_to_all x1, starting transfers between devices, body(): whole = lax.all_to_all(step, ('core', 'x', 'y'), 0, 0)  7.72 us
    unnamed x20, local copies, waits for them, and re-layouts  7.17 us
    pallas_call x2, Pallas kernels, outer_conv(): pl.pallas_call(functools.partial(outer_kernel, z), out_shape=jax.ShapeDty...  6.41 us
    pallas_call x1, Pallas kernels, outer_back(): pl.pallas_call(outer_back_kernel, out_shape=jax.ShapeDtypeStruct((2, CELL...  6.07 us
  transfers between devices with their start and end apart: 8, of which 3 were waited for; matrix products, arithmetic and copies ran while one was open for 0% of the time, Pallas kernels for 22%

profile of v1, /device:TPU:1, one launch (start us, length us, event | category | flops | bytes accessed | tf_op | source)
XLA Modules:
  0.0 93.2 jit_solution(17957137447518778034)
XLA Ops:
  0.6 1.2 %copy-done = bf16[1,2,32,64,128]{4,3,2,1,0:T(8,128)(2,1)S(1)} copy-done((bf16[1,2,32,64,128]{4,3,2,1,0:T(8,128)(2,1)S(1)}, bf16[1,2,32,64,128]{4,3,2,1,0:T(8,128)(2,1)}, u32[]{:S(2)}) %copy-start) | copy-done | bytes 1048600
  2.0 5.1 %collective-permute-start = (bf16[2048,128]{1,0:T(8,128)(2,1)S(1)}, bf16[2048,128]{1,0:T(8,128)(2,1)S(1)}, u32[]{:S(2)}, u32[]{:S(2)}) collective-permute-start(bf16[2048,128]{1,0:T(8,128)(2,1)S(1)} %get-tuple-element.9), channel_id=1, source_target_pairs={{4,0},{8,4},{12,8},{16,12},{20,16},{24,20},{28,24},{32,28},{36,32}... | collective-permute-start | bytes 1572872 | tf_op jit(solution)/shard_map/ppermute | solution.py:427
  7.1 1.9 %collective-permute-start.2 = (bf16[2048,128]{1,0:T(8,128)(2,1)S(1)}, bf16[2048,128]{1,0:T(8,128)(2,1)S(1)}, u32[]{:S(2)}, u32[]{:S(2)}) collective-permute-start(bf16[2048,128]{1,0:T(8,128)(2,1)S(1)} %get-tuple-element.11), channel_id=1, source_target_pairs={{0,4},{4,8},{8,12},{12,16},{16,20},{20,24},{24,28},{28,32},{32,36}... | collective-permute-start | bytes 1572872 | tf_op jit(solution)/shard_map/ppermute | solution.py:427
  9.1 1.2 %copy-done.1 = bf16[1,2,32,64,128]{4,3,2,1,0:T(8,128)(2,1)S(1)} copy-done((bf16[1,2,32,64,128]{4,3,2,1,0:T(8,128)(2,1)S(1)}, bf16[1,2,32,64,128]{4,3,2,1,0:T(8,128)(2,1)}, u32[]{:S(2)}) %copy-start.1) | copy-done | bytes 1048600
  10.3 1.2 %copy-done.6 = bf16[3456,128]{1,0:T(8,128)(2,1)S(1)} copy-done((bf16[3456,128]{1,0:T(8,128)(2,1)S(1)}, bf16[3456,128]{1,0:T(8,128)(2,1)}, u32[]{:S(2)}) %copy-start.6) | copy-done | bytes 884760
  11.4 4.3 %inner_conv.1 = (f32[2048,128]{1,0:T(8,128)S(1)}, f32[2048,128]{1,0:T(8,128)S(1)}, bf16[256,2048]{1,0:T(8,128)(2,1)S(1)}) custom-call(bf16[2,2048,128]{2,1,0:T(8,128)(2,1)S(1)} %bitcast.9, bf16[3456,128]{1,0:T(8,128)(2,1)S(1)} %copy-done.6), custom_call_target="tpu_custom_call" | custom-call | flops 2415919104 | bytes 5242880 | tf_op jit(solution)/shard_map/inner_conv/pallas_call | solution.py:115
  15.8 3.2 %outer_conv_1.1.high = bf16[2048,128]{1,0:T(8,128)(2,1)} custom-call(bf16[2048,128]{1,0:T(8,128)(2,1)S(1)} %collective-permute-done.halo.after, bf16[3456,128]{1,0:T(8,128)(2,1)S(1)} %copy-done.7, f32[2048,128]{1,0:T(8,128)S(1)} %get-tuple-element.10.inner, bf16[2,2048,128]{2,1,0:T(8,128)(2,1)S(1)} %bitcast.10), custom_call_target="tpu_custom_call" | custom-call | flops 1207959552 | bytes 3145728 | tf_op jit(solution)/shard_map/outer_conv_1/pallas_call | solution.py:155
  19.0 3.2 %outer_conv_0.1.low = bf16[2048,128]{1,0:T(8,128)(2,1)} custom-call(bf16[2048,128]{1,0:T(8,128)(2,1)S(1)} %collective-permute-done.2.halo.before, bf16[3456,128]{1,0:T(8,128)(2,1)S(1)} %copy-done.7, f32[2048,128]{1,0:T(8,128)S(1)} %get-tuple-element.12.inner, bf16[2,2048,128]{2,1,0:T(8,128)(2,1)S(1)} %bitcast.11), custom_call_target="tpu_custom_call" | custom-call | flops 1207959552 | bytes 3145728 | tf_op jit(solution)/shard_map/outer_conv_0/pallas_call | solution.py:155
  22.2 7.9 %kernel_gradient.1 = (f32[64,32,128]{2,1,0:T(8,128)S(1)}, bf16[64,32,128]{2,1,0:T(8,128)(2,1)S(1)}) custom-call(s32[1]{0:T(128)} %bitcast.2.core_ref, bf16[2048,128]{1,0:T(8,128)(2,1)} %outer_conv_0.1.low, bf16[2048,128]{1,0:T(8,128)(2,1)} %outer_conv_1.1.high, bf16[2048,128]{1,0:T(8,128)(2,1)S(1)} %collective-permute-done.2.halo.before, ...), custom_call_target="tpu_custom_call" | custom-call | flops 4831838208 | bytes 5242880 | tf_op jit(solution)/shard_map/kernel_gradient/pallas_call | solution.py:212
  30.7 1.5 %collective-permute-done.4 = bf16[64,32,128]{2,1,0:T(8,128)(2,1)S(1)} collective-permute-done((bf16[64,32,128]{2,1,0:T(8,128)(2,1)S(1)}, bf16[64,32,128]{2,1,0:T(8,128)(2,1)S(1)}, u32[]{:S(2)}, u32[]{:S(2)}) %collective-permute-start.4) | collective-permute-done | bytes 524320 | tf_op jit(solution)/shard_map/ppermute | solution.py:441
  32.3 1.0 %add_convert_fusion = bf16[64,32,128]{2,1,0:T(8,128)(2,1)} fusion(f32[64,32,128]{2,1,0:T(8,128)S(1)} %get-tuple-element.14, bf16[64,32,128]{2,1,0:T(8,128)(2,1)S(1)} %collective-permute-done.4), kind=kLoop, calls=%fused_computation | loop fusion | flops 786432 | bytes 2097152 | tf_op jit(solution)/shard_map/convert_element_type | solution.py:442
  33.2 8.8 %all-to-all-start = ((bf16[16,4,32,128]{3,2,1,0:T(8,128)(2,1)}), bf16[16,4,32,128]{3,2,1,0:T(8,128)(2,1)S(1)}, u32[]{:S(2)}, u32[]{:S(2)}) async-start(bf16[16,4,32,128]{3,2,1,0:T(8,128)(2,1)} %bitcast.3), calls=%async_computation | async-start | bytes 1048576 | tf_op jit(solution)/shard_map/all_to_all | solution.py:443
  42.0 2.6 %collective-permute-start.3 = (bf16[2048,128]{1,0:T(8,128)(2,1)}, bf16[2048,128]{1,0:T(8,128)(2,1)}, u32[]{:S(2)}, u32[]{:S(2)}) collective-permute-start(bf16[2048,128]{1,0:T(8,128)(2,1)} %outer_conv_0.1.low), channel_id=1, source_target_pairs={{4,0},{8,4},{12,8},{16,12},{20,16},{24,20},{28,24},{32,28},{36,32}... | collective-permute-start | bytes 1572872 | tf_op jit(solution)/shard_map/ppermute | solution.py:427
  44.6 6.2 %collective-permute-start.1 = (bf16[2048,128]{1,0:T(8,128)(2,1)}, bf16[2048,128]{1,0:T(8,128)(2,1)}, u32[]{:S(2)}, u32[]{:S(2)}) collective-permute-start(bf16[2048,128]{1,0:T(8,128)(2,1)} %outer_conv_1.1.high), channel_id=1, source_target_pairs={{0,4},{4,8},{8,12},{12,16},{16,20},{20,24},{24,28},{28,32},{32,36}... | collective-permute-start | bytes 1572872 | tf_op jit(solution)/shard_map/ppermute | solution.py:427
  50.8 1.6 %all-to-all-done.got = bf16[16,4,32,128]{3,2,1,0:T(8,128)(2,1)S(1)} async-done(((bf16[16,4,32,128]{3,2,1,0:T(8,128)(2,1)}), bf16[16,4,32,128]{3,2,1,0:T(8,128)(2,1)S(1)}, u32[]{:S(2)}, u32[]{:S(2)}) %all-to-all-start) | async-done | bytes 524320 | tf_op jit(solution)/shard_map/all_to_all | solution.py:443
  53.1 11.7 %all-to-all-start.1 = ((f32[8,32,128]{2,1,0:T(8,128)}), f32[8,32,128]{2,1,0:T(8,128)S(1)}, u32[]{:S(2)}, u32[]{:S(2)}) async-start(f32[8,32,128]{2,1,0:T(8,128)} %mixed_rows.1.later), calls=%async_computation.1 | async-start | bytes 262144 | tf_op jit(solution)/shard_map/all_to_all | solution.py:446
  64.8 1.2 %copy-done.5 = bf16[1,2,32,64,128]{4,3,2,1,0:T(8,128)(2,1)S(1)} copy-done((bf16[1,2,32,64,128]{4,3,2,1,0:T(8,128)(2,1)S(1)}, bf16[1,2,32,64,128]{4,3,2,1,0:T(8,128)(2,1)}, u32[]{:S(2)}) %copy-start.5) | copy-done | bytes 1048600
  66.1 1.2 %copy-done.8 = bf16[3456,128]{1,0:T(8,128)(2,1)S(1)} copy-done((bf16[3456,128]{1,0:T(8,128)(2,1)S(1)}, bf16[3456,128]{1,0:T(8,128)(2,1)}, u32[]{:S(2)}) %copy-start.8) | copy-done | bytes 884760
  67.2 5.4 %inner_back.1.inner.later = f32[2,2048,128]{2,1,0:T(8,128)S(1)} custom-call(bf16[2048,128]{1,0:T(8,128)(2,1)} %outer_conv_0.1.low, bf16[2048,128]{1,0:T(8,128)(2,1)} %outer_conv_1.1.high, bf16[3456,128]{1,0:T(8,128)(2,1)S(1)} %copy-done.8, bf16[2,2048,128]{2,1,0:T(8,128)(2,1)S(1)} %bitcast.12, f32[8,32,128]{2,1,0:T(8,128)} %mixed_rows.1.later), custom_call_target="tpu_custom_call" | custom-call | flops 2415919104 | bytes 5242880 | tf_op jit(solution)/shard_map/inner_back/pallas_call | solution.py:262
  72.6 0.9 spread_step.1
  73.5 7.7 %all-to-all-start.2 = ((f32[32,32,128]{2,1,0:T(8,128)}), f32[32,32,128]{2,1,0:T(8,128)S(1)}, u32[]{:S(2)}, u32[]{:S(2)}) async-start(f32[32,32,128]{2,1,0:T(8,128)} %spread_step.1), calls=%async_computation.2 | async-start | bytes 1048576 | tf_op jit(solution)/shard_map/all_to_all | solution.py:451
  81.3 1.2 %copy-done.9 = bf16[3456,128]{1,0:T(8,128)(2,1)S(1)} copy-done((bf16[3456,128]{1,0:T(8,128)(2,1)S(1)}, bf16[3456,128]{1,0:T(8,128)(2,1)}, u32[]{:S(2)}) %copy-start.9) | copy-done | bytes 884760
  82.5 6.1 %outer_back.1 = bf16[2,2048,128]{2,1,0:T(8,128)(2,1)} custom-call(bf16[2048,128]{1,0:T(8,128)(2,1)} %collective-permute-done.1.before, bf16[2048,128]{1,0:T(8,128)(2,1)} %collective-permute-done.3.after, bf16[3456,128]{1,0:T(8,128)(2,1)S(1)} %copy-done.9, f32[2,2048,128]{2,1,0:T(8,128)S(1)} %inner_back.1.inner.later), custom_call_target="tpu_custom_call" | custom-call | flops 2415919104 | bytes 5242880 | tf_op jit(solution)/shard_map/outer_back/pallas_call | solution.py:312
  88.5 3.9 %all-to-all-done.2 = f32[32,32,128]{2,1,0:T(8,128)S(1)} async-done(((f32[32,32,128]{2,1,0:T(8,128)}), f32[32,32,128]{2,1,0:T(8,128)S(1)}, u32[]{:S(2)}, u32[]{:S(2)}) %all-to-all-start.2) | async-done | bytes 524320 | tf_op jit(solution)/shard_map/all_to_all | solution.py:451
  (23 shorter events, 2.3 us)
Async XLA Ops:
  0.6 1.2 %copy-start = (bf16[1,2,32,64,128]{4,3,2,1,0:T(8,128)(2,1)S(1)}, bf16[1,2,32,64,128]{4,3,2,1,0:T(8,128)(2,1)}, u32[]{:S(2)}) copy-start(bf16[1,2,32,64,128]{4,3,2,1,0:T(8,128)(2,1)} %param.5) | copy-start | bytes 3145732
  2.0 13.8 %collective-permute-start = (bf16[2048,128]{1,0:T(8,128)(2,1)S(1)}, bf16[2048,128]{1,0:T(8,128)(2,1)S(1)}, u32[]{:S(2)}, u32[]{:S(2)}) collective-permute-start(bf16[2048,128]{1,0:T(8,128)(2,1)S(1)} %get-tuple-element.9), channel_id=1, source_target_pairs={{4,0},{8,4},{12,8},{16,12},{20,16},{24,20},{28,24},{32,28},{36,32}... | collective-permute-start | bytes 1572872 | tf_op jit(solution)/shard_map/ppermute | solution.py:427
  7.1 11.9 %collective-permute-start.2 = (bf16[2048,128]{1,0:T(8,128)(2,1)S(1)}, bf16[2048,128]{1,0:T(8,128)(2,1)S(1)}, u32[]{:S(2)}, u32[]{:S(2)}) collective-permute-start(bf16[2048,128]{1,0:T(8,128)(2,1)S(1)} %get-tuple-element.11), channel_id=1, source_target_pairs={{0,4},{4,8},{8,12},{12,16},{16,20},{20,24},{24,28},{28,32},{32,36}... | collective-permute-start | bytes 1572872 | tf_op jit(solution)/shard_map/ppermute | solution.py:427
  9.0 1.2 %copy-start.1 = (bf16[1,2,32,64,128]{4,3,2,1,0:T(8,128)(2,1)S(1)}, bf16[1,2,32,64,128]{4,3,2,1,0:T(8,128)(2,1)}, u32[]{:S(2)}) copy-start(bf16[1,2,32,64,128]{4,3,2,1,0:T(8,128)(2,1)} %param.5) | copy-start | bytes 3145732
  10.3 1.2 %copy-start.6 = (bf16[3456,128]{1,0:T(8,128)(2,1)S(1)}, bf16[3456,128]{1,0:T(8,128)(2,1)}, u32[]{:S(2)}) copy-start(bf16[3456,128]{1,0:T(8,128)(2,1)} %weight.9) | copy-start | bytes 2654212
  11.4 4.3 %copy-start.4 = (bf16[1,2,32,64,128]{4,3,2,1,0:T(8,128)(2,1)S(1)}, bf16[1,2,32,64,128]{4,3,2,1,0:T(8,128)(2,1)}, u32[]{:S(2)}) copy-start(bf16[1,2,32,64,128]{4,3,2,1,0:T(8,128)(2,1)} %param.6) | copy-start | bytes 3145732
  11.4 4.3 %copy-start.7 = (bf16[3456,128]{1,0:T(8,128)(2,1)S(1)}, bf16[3456,128]{1,0:T(8,128)(2,1)}, u32[]{:S(2)}) copy-start(bf16[3456,128]{1,0:T(8,128)(2,1)} %weight.9) | copy-start | bytes 2654212
  30.1 2.2 %collective-permute-start.4 = (bf16[64,32,128]{2,1,0:T(8,128)(2,1)S(1)}, bf16[64,32,128]{2,1,0:T(8,128)(2,1)S(1)}, u32[]{:S(2)}, u32[]{:S(2)}) collective-permute-start(bf16[64,32,128]{2,1,0:T(8,128)(2,1)S(1)} %get-tuple-element.15), channel_id=1, source_target_pairs={{0,4},{4,0},{1,5},{5,1},{2,6},{6,2},{3,7},{7,3},{8,12},{12,8},{9,1... | collective-permute-start | bytes 1572872 | tf_op jit(solution)/shard_map/ppermute | solution.py:441
  33.2 19.1 %all-to-all-start = ((bf16[16,4,32,128]{3,2,1,0:T(8,128)(2,1)}), bf16[16,4,32,128]{3,2,1,0:T(8,128)(2,1)S(1)}, u32[]{:S(2)}, u32[]{:S(2)}) async-start(bf16[16,4,32,128]{3,2,1,0:T(8,128)(2,1)} %bitcast.3), calls=%async_computation | async-start | bytes 1048576 | tf_op jit(solution)/shard_map/all_to_all | solution.py:443
  42.0 39.2 %collective-permute-start.3 = (bf16[2048,128]{1,0:T(8,128)(2,1)}, bf16[2048,128]{1,0:T(8,128)(2,1)}, u32[]{:S(2)}, u32[]{:S(2)}) collective-permute-start(bf16[2048,128]{1,0:T(8,128)(2,1)} %outer_conv_0.1.low), channel_id=1, source_target_pairs={{4,0},{8,4},{12,8},{16,12},{20,16},{24,20},{28,24},{32,28},{36,32}... | collective-permute-start | bytes 1572872 | tf_op jit(solution)/shard_map/ppermute | solution.py:427
  44.6 36.7 %collective-permute-start.1 = (bf16[2048,128]{1,0:T(8,128)(2,1)}, bf16[2048,128]{1,0:T(8,128)(2,1)}, u32[]{:S(2)}, u32[]{:S(2)}) collective-permute-start(bf16[2048,128]{1,0:T(8,128)(2,1)} %outer_conv_1.1.high), channel_id=1, source_target_pairs={{0,4},{4,8},{8,12},{12,16},{16,20},{20,24},{24,28},{28,32},{32,36}... | collective-permute-start | bytes 1572872 | tf_op jit(solution)/shard_map/ppermute | solution.py:427
  53.1 19.5 %all-to-all-start.1 = ((f32[8,32,128]{2,1,0:T(8,128)}), f32[8,32,128]{2,1,0:T(8,128)S(1)}, u32[]{:S(2)}, u32[]{:S(2)}) async-start(f32[8,32,128]{2,1,0:T(8,128)} %mixed_rows.1.later), calls=%async_computation.1 | async-start | bytes 262144 | tf_op jit(solution)/shard_map/all_to_all | solution.py:446
  64.8 1.2 %copy-start.5 = (bf16[1,2,32,64,128]{4,3,2,1,0:T(8,128)(2,1)S(1)}, bf16[1,2,32,64,128]{4,3,2,1,0:T(8,128)(2,1)}, u32[]{:S(2)}) copy-start(bf16[1,2,32,64,128]{4,3,2,1,0:T(8,128)(2,1)} %param.6) | copy-start | bytes 3145732
  66.0 1.2 %copy-start.8 = (bf16[3456,128]{1,0:T(8,128)(2,1)S(1)}, bf16[3456,128]{1,0:T(8,128)(2,1)}, u32[]{:S(2)}) copy-start(bf16[3456,128]{1,0:T(8,128)(2,1)} %weight.9) | copy-start | bytes 2654212
  67.2 5.4 %copy-start.2 = (f32[864,128]{1,0:T(8,128)S(1)}, f32[864,128]{1,0:T(8,128)}, u32[]{:S(2)}) copy-start(f32[864,128]{1,0:T(8,128)} %first.1) | copy-start | bytes 1327108
  67.2 5.4 %copy-start.3 = (f32[864,128]{1,0:T(8,128)S(1)}, f32[864,128]{1,0:T(8,128)}, u32[]{:S(2)}) copy-start(f32[864,128]{1,0:T(8,128)} %second.1) | copy-start | bytes 1327108
  73.5 18.9 %all-to-all-start.2 = ((f32[32,32,128]{2,1,0:T(8,128)}), f32[32,32,128]{2,1,0:T(8,128)S(1)}, u32[]{:S(2)}, u32[]{:S(2)}) async-start(f32[32,32,128]{2,1,0:T(8,128)} %spread_step.1), calls=%async_computation.2 | async-start | bytes 1048576 | tf_op jit(solution)/shard_map/all_to_all | solution.py:451
  81.3 1.2 %copy-start.9 = (bf16[3456,128]{1,0:T(8,128)(2,1)S(1)}, bf16[3456,128]{1,0:T(8,128)(2,1)}, u32[]{:S(2)}) copy-start(bf16[3456,128]{1,0:T(8,128)(2,1)} %weight.9) | copy-start | bytes 2654212

commit v2 on v1

v2 whole, which is shorter than its diff:
```python
import functools
import jax
import jax.numpy as jnp
from jax import lax
from jax.experimental import pallas as pl
from jax.experimental.pallas import tpu as pltpu
from jax.sharding import Mesh, PartitionSpec as P

ADAM_STEP = 10


beta_one = 0.9
beta_two = 0.999
eps_adam = 1e-08

SPACE = ("x", "y", "zl", "core")
CHUNK = 32
OWNERS = 32
C = 128
COLS = 64
ROWS = 32
CELLS = ROWS * COLS
PADDED = CELLS + 2 * COLS
STRIP = 256
TILE = 512
BF = jnp.bfloat16
F32 = jnp.float32
VMEM = pl.BlockSpec(memory_space=pltpu.VMEM)
ANY = pl.BlockSpec(memory_space=pl.ANY)
HBM = pl.BlockSpec(memory_space=pltpu.HBM)
SMEM = pl.BlockSpec(memory_space=pltpu.SMEM)
FLAG = jax.ShapeDtypeStruct((8, C), F32)
WHOLE = pltpu.CompilerParams(vmem_limit_bytes=60 * 1024 * 1024)
SMALL = pltpu.CompilerParams(vmem_limit_bytes=4 * 1024 * 1024)
PARAMS = pltpu.CompilerParams(vmem_limit_bytes=32 * 1024 * 1024)


def cost(flops, moved, special=0):
    return pl.CostEstimate(flops=flops, bytes_accessed=moved, transcendentals=special)


def shifted_columns(planes, out, first, flip):
    width = 128 * len(planes)
    blank = jnp.zeros((COLS, width), BF)
    cols = slice(first, first + width)
    for c in range(3):
        out[c, 0:COLS, cols] = blank
        out[c, PADDED - COLS : PADDED, cols] = blank
    before, after = (2, 0) if flip else (0, 2)

    def strip(i, carry):
        at = pl.multiple_of(i * STRIP, STRIP)
        to = pl.ds(pl.multiple_of(at + COLS, COLS), STRIP)
        col = lax.broadcasted_iota(jnp.int32, (STRIP, C), 0) & (COLS - 1)
        for k, plane in enumerate(planes):
            cols = slice(first + k * C, first + (k + 1) * C)
            here = plane(pl.ds(at, STRIP))
            wide = here.astype(F32)
            out[1, to, cols] = here
            out[before, to, cols] = jnp.where(
                col == 0, 0.0, pltpu.roll(wide, 1, 0)
            ).astype(BF)
            out[after, to, cols] = jnp.where(
                col == COLS - 1, 0.0, pltpu.roll(wide, STRIP - 1, 0)
            ).astype(BF)
        return carry

    lax.fori_loop(0, CELLS // STRIP, strip, 0)


def transposed(plane, out, first):
    for at in range(0, CELLS, TILE):
        out[first : first + C, at : at + TILE] = jnp.transpose(
            plane(pl.ds(at, TILE))
        )


def rows_of(plane):
    return lambda rows: plane[rows, :]


def ordered(core, near, far):
    def pick(first, second):
        return lambda rows: jnp.where(core == 0, first[rows, :], second[rows, :])

    return pick(far, near), pick(near, far)


def fetched(source, held, sem):
    copy = pltpu.make_async_copy(source, held, sem)
    copy.start()
    return copy


def tap(a, b, c):
    return (a * 3 + b) * 3 + c


def taps_of(field, at, rows):
    return jnp.concatenate(
        [
            field[c, pl.ds(pl.multiple_of(at + b * COLS, COLS), rows), :]
            for b in range(3)
            for c in range(3)
        ],
        axis=1,
    )


def inner_kernel(vol, weight, out, vol_t, field, mixed, held, sem):
    copy = fetched(weight, held, sem)
    planes = [rows_of(vol.at[0]), rows_of(vol.at[1])]
    shifted_columns(planes, field, 0, False)
    copy.wait()
    for b in range(3):
        for c in range(3):
            base = (b * 3 + c) * 256
            for p in range(2):
                for z in range(2):
                    t = tap(1 + p - z, b, c)
                    mixed[base + p * C : base + (p + 1) * C, z * C : (z + 1) * C] = (
                        held[t * C : (t + 1) * C, :]
                    )

    def tile(i, carry):
        at = pl.multiple_of(i * TILE, TILE)
        got = jnp.dot(taps_of(field, at, TILE), mixed[...], preferred_element_type=F32)
        out[0, pl.ds(at, TILE), :] = got[:, 0:C]
        out[1, pl.ds(at, TILE), :] = got[:, C : 2 * C]
        return carry

    lax.fori_loop(0, CELLS // TILE, tile, 0)
    for p in range(2):
        transposed(planes[p], vol_t, p * C)


def inner_conv(vol, weight):
    return pl.pallas_call(
        inner_kernel,
        out_shape=[
            jax.ShapeDtypeStruct((2, CELLS, C), F32),
            jax.ShapeDtypeStruct((2 * C, CELLS), BF),
        ],
        in_specs=[VMEM, HBM],
        out_specs=[VMEM] * 2,
        scratch_shapes=[
            pltpu.VMEM((3, PADDED, 2 * C), BF),
            pltpu.VMEM((9 * 256, 2 * C), BF),
            pltpu.VMEM((27 * C, C), BF),
            pltpu.SemaphoreType.DMA,
        ],
        compiler_params=PARAMS,
        cost_estimate=cost(2 * CELLS * 2304 * 256, 5 << 20),
        name="inner_conv",
    )(vol, weight)


def outer_kernel(
    at_ref, halo, weight, inner, upstream, later, grad, ended, field, held, sem
):
    z = at_ref[0]
    ended[...] = jnp.zeros_like(ended)
    first = pl.multiple_of(z * 18 * C, 18 * C)
    copy = fetched(weight.at[pl.ds(first, 9 * C), :], held, sem)
    shifted_columns([rows_of(halo)], field, 0, False)
    copy.wait()

    def tile(i, carry):
        at = pl.multiple_of(i * TILE, TILE)
        rows = pl.ds(at, TILE)
        preact = inner[z, rows, :] + jnp.dot(
            taps_of(field, at, TILE), held[...], preferred_element_type=F32
        )
        s = jax.nn.sigmoid(preact)
        slopes = s * (1.0 + preact * (1.0 - s))
        grad[rows, :] = (upstream[z, rows, :].astype(F32) * slopes).astype(BF)
        return carry

    lax.fori_loop(0, CELLS // TILE, tile, 0)


def outer_conv(name, z, halo, weight, inner, upstream, later):
    return pl.pallas_call(
        outer_kernel,
        out_shape=[jax.ShapeDtypeStruct((CELLS, C), BF), FLAG],
        in_specs=[SMEM, VMEM, HBM, VMEM, VMEM, ANY],
        out_specs=[VMEM, VMEM],
        scratch_shapes=[
            pltpu.VMEM((3, PADDED, C), BF),
            pltpu.VMEM((9 * C, C), BF),
            pltpu.SemaphoreType.DMA,
        ],
        compiler_params=PARAMS,
        cost_estimate=cost(2 * CELLS * 1152 * 256, 3 << 20, CELLS * 128),
        name=name,
    )(z, halo, weight, inner, upstream, later)


def taps_kernel(core_ref, near, far, near_halo, far_halo, vol_t, kept, sent, field, lhs, whole):
    core = core_ref[0]
    shifted_columns(ordered(core, near, far), field, 0, False)
    before, after = ordered(core, near_halo, far_halo)
    lhs[C : 3 * C, :] = vol_t[...]
    transposed(before, lhs, 0)
    transposed(after, lhs, 3 * C)

    for owner in range(27, 32):
        for group in range(4):
            whole[group * 32 + owner] = jnp.zeros((CHUNK, C), F32)

    def row(b, carry):
        at = pl.multiple_of((2 - b) * COLS, COLS)
        for c in range(3):
            got = jnp.dot(
                lhs[...],
                field[2 - c, pl.ds(at, CELLS), :],
                preferred_element_type=F32,
            )
            for a in range(3):
                summed = (
                    got[a * C : (a + 1) * C, 0:C]
                    + got[(a + 1) * C : (a + 2) * C, C : 2 * C]
                )
                for i in range(4):
                    chunk = 4 * tap(a, b, c) + i
                    whole[chunk + 5 * (chunk // 27)] = summed[
                        i * CHUNK : (i + 1) * CHUNK, :
                    ]
        return carry

    lax.fori_loop(0, 3, row, 0)

    def share(owner, carry):
        for group in range(4):
            kept[owner * 4 + group] = whole[group * 32 + core * 16 + owner]
            sent[owner * 4 + group] = whole[
                group * 32 + (1 - core) * 16 + owner
            ].astype(BF)
        return carry

    lax.fori_loop(0, 16, share, 0)


def kernel_gradient(core, near, far, near_halo, far_halo, vol_t):
    return pl.pallas_call(
        taps_kernel,
        out_shape=[
            jax.ShapeDtypeStruct((64, CHUNK, C), F32),
            jax.ShapeDtypeStruct((64, CHUNK, C), BF),
        ],
        in_specs=[SMEM] + [VMEM] * 5,
        out_specs=[VMEM, VMEM],
        scratch_shapes=[
            pltpu.VMEM((3, PADDED, 2 * C), BF),
            pltpu.VMEM((4 * C, CELLS), BF),
            pltpu.VMEM((4 * 32, CHUNK, C), F32),
        ],
        compiler_params=PARAMS,
        cost_estimate=cost(2 * CELLS * 4608 * 256, 5 << 20),
        name="kernel_gradient",
    )(core, near, far, near_halo, far_halo, vol_t)


def inner_back_kernel(
    core_ref, near, far, weight, upstream, later, out, ended, field, mixed, held, sem
):
    copy = fetched(weight, held, sem)
    ended[...] = jnp.zeros_like(ended)
    shifted_columns(ordered(core_ref[0], near, far), field, 0, False)
    copy.wait()
    for b in range(3):
        for c in range(3):
            base = (b * 3 + c) * 256
            for p in range(2):
                for z in range(2):
                    t = tap(1 + z - p, 2 - b, 2 - c)
                    mixed[z * C : (z + 1) * C, base + p * C : base + (p + 1) * C] = (
                        held[t * C : (t + 1) * C, :]
                    )

    def tile(i, carry):
        at = pl.multiple_of(i * TILE, TILE)
        rows = pl.ds(at, TILE)
        got = lax.dot_general(
            taps_of(field, at, TILE),
            mixed[...],
            (((1,), (1,)), ((), ())),
            preferred_element_type=F32,
        )
        for z in range(2):
            out[z, rows, :] = (
                upstream[z, rows, :].astype(F32) + got[:, z * C : (z + 1) * C]
            )
        return carry

    lax.fori_loop(0, CELLS // TILE, tile, 0)


def inner_back(core, near, far, weight, upstream, later):
    return pl.pallas_call(
        inner_back_kernel,
        out_shape=[
            jax.ShapeDtypeStruct((2, CELLS, C), F32),
            FLAG,
        ],
        in_specs=[SMEM, VMEM, VMEM, HBM, VMEM, ANY],
        out_specs=[VMEM, VMEM],
        scratch_shapes=[
            pltpu.VMEM((3, PADDED, 2 * C), BF),
            pltpu.VMEM((2 * C, 9 * 256), BF),
            pltpu.VMEM((27 * C, C), BF),
            pltpu.SemaphoreType.DMA,
        ],
        compiler_params=WHOLE,
        cost_estimate=cost(2 * CELLS * 2304 * 256, 5 << 20),
        name="inner_back",
    )(core, near, far, weight, upstream, later)


def outer_back_kernel(
    core_ref, near, far, weight, kept, out, field, mixed, held, inner, sem, kept_sem
):
    copy = fetched(weight, held, sem)
    kept_copy = fetched(kept, inner, kept_sem)
    core = core_ref[0]
    shifted_columns([rows_of(near), rows_of(far)], field, 0, False)
    copy.wait()
    for k in range(2):
        z = 1 - core if k == 0 else core
        first = pl.multiple_of((2 - 2 * z) * 9 * C, C)
        for b in range(3):
            for c in range(3):
                base = (b * 3 + c) * C
                mixed[k, :, base : base + C] = held[
                    pl.ds(first + tap(0, 2 - b, 2 - c) * C, C), :
                ]

    kept_copy.wait()

    def tile(i, carry):
        at = pl.multiple_of(i * TILE, TILE)
        rows = pl.ds(at, TILE)
        for k in range(2):
            z = 1 - core if k == 0 else core
            lhs = jnp.concatenate(
                [
                    field[
                        c,
                        pl.ds(pl.multiple_of(at + b * COLS, COLS), TILE),
                        k * C : (k + 1) * C,
                    ]
                    for b in range(3)
                    for c in range(3)
                ],
                axis=1,
            )
            got = lax.dot_general(
                lhs, mixed[k], (((1,), (1,)), ((), ())), preferred_element_type=F32
            )
            out[z, rows, :] = (inner[z, rows, :] + got).astype(BF)
        return carry

    lax.fori_loop(0, CELLS // TILE, tile, 0)


def outer_back(core, near, far, weight, inner):
    return pl.pallas_call(
        outer_back_kernel,
        out_shape=jax.ShapeDtypeStruct((2, CELLS, C), BF),
        in_specs=[SMEM, VMEM, VMEM, HBM, HBM],
        out_specs=VMEM,
        scratch_shapes=[
            pltpu.VMEM((3, PADDED, 2 * C), BF),
            pltpu.VMEM((2, C, 9 * C), BF),
            pltpu.VMEM((27 * C, C), BF),
            pltpu.VMEM((2, CELLS, C), F32),
            pltpu.SemaphoreType.DMA,
            pltpu.SemaphoreType.DMA,
        ],
        compiler_params=WHOLE,
        cost_estimate=cost(2 * CELLS * 2304 * 256, 5 << 20),
        name="outer_back",
    )(core, near, far, weight, inner)


def plane_kernel(at_ref, vol, later, plane, ended, sem):
    copy = fetched(vol.at[at_ref[0]], plane, sem)
    ended[...] = jnp.zeros_like(ended)
    copy.wait()


def one_plane(name, at, vol, later):
    return pl.pallas_call(
        plane_kernel,
        out_shape=[jax.ShapeDtypeStruct((CELLS, C), BF), FLAG],
        in_specs=[SMEM, HBM, ANY],
        out_specs=[HBM, VMEM],
        scratch_shapes=[pltpu.SemaphoreType.DMA],
        compiler_params=WHOLE,
        cost_estimate=cost(0, 1 << 20),
        name=name,
    )(at, vol, later)


def first_rows_kernel(whole, out):
    out[...] = whole[0 : out.shape[0], :].astype(F32)


def first_rows(whole, rows):
    return pl.pallas_call(
        first_rows_kernel,
        out_shape=jax.ShapeDtypeStruct((rows, C), F32),
        in_specs=[VMEM],
        out_specs=VMEM,
        compiler_params=SMALL,
        cost_estimate=cost(0, 1 << 20),
        name="first_rows",
    )(whole)


def mix_kernel(got, later, out):
    for group in range(4):
        total = got[0, group].astype(F32)
        for k in range(1, 16):
            total += got[k, group].astype(F32)
        out[group] = total
        out[4 + group] = total


def mixed_rows(got, later):
    return pl.pallas_call(
        mix_kernel,
        out_shape=jax.ShapeDtypeStruct((8, CHUNK, C), F32),
        in_specs=[VMEM, ANY],
        out_specs=VMEM,
        compiler_params=SMALL,
        cost_estimate=cost(1 << 18, 1 << 20),
        name="mixed_rows",
    )(got, later)


def step_kernel(at_ref, got, first, second, out):
    total = got[0]
    for k in range(1, 8):
        total += got[k]
    at = pl.multiple_of(at_ref[0], CHUNK)
    rows = pl.ds(at, CHUNK)
    step = adam(total, first[rows, :], second[rows, :])
    step = step.astype(BF)
    for k in range(OWNERS):
        out[k] = step


def spread_step(at, got, first, second):
    return pl.pallas_call(
        step_kernel,
        out_shape=jax.ShapeDtypeStruct((OWNERS, CHUNK, C), BF),
        in_specs=[SMEM] + [VMEM] * 3,
        out_specs=VMEM,
        compiler_params=SMALL,
        cost_estimate=cost(1 << 18, 1 << 20),
        name="spread_step",
    )(at, got, first, second)


def adam(grad, first, second):
    m_new = beta_one * first + (1.0 - beta_one) * grad
    v_new = beta_two * second + (1.0 - beta_two) * grad * grad
    return (
        m_new
        / (1.0 - beta_one**ADAM_STEP)
        / (jnp.sqrt(v_new / (1.0 - beta_two**ADAM_STEP)) + eps_adam)
    )


def from_neighbours(near, far):
    size = lax.axis_size(SPACE)
    pairs = [(i, i + 1) for i in range(1, size - 1, 2)]
    far_halo = lax.ppermute(far, SPACE, pairs + [(j, i) for i, j in pairs])
    near_halo = lax.ppermute(near, "core", [(0, 1), (1, 0)])
    return near_halo, far_halo


def body(volume, upstream, weight, first_moment, second_moment):
    vol = volume.reshape(2, CELLS, C)
    up = upstream.reshape(2, CELLS, C)
    core = lax.axis_index("core")
    at_core, at_near = core.reshape(1), (1 - core).reshape(1)
    far_plane, ended = one_plane("far_plane", at_core, vol, at_core)
    near_plane, ended = one_plane("near_plane", at_near, vol, ended)
    near_halo, far_halo = from_neighbours(near_plane, far_plane)
    inner, vol_t = inner_conv(vol, weight)
    near, ended = outer_conv(
        "near_conv", at_near, near_halo, weight, inner, up, at_core
    )
    far, ended = outer_conv(
        "far_conv", at_core, far_halo, weight, inner, up, ended
    )
    kept, sent = kernel_gradient(at_core, near, far, near_halo, far_halo, vol_t)

    rows = first_moment.shape[0]
    other = lax.ppermute(sent, "core", [(0, 1), (1, 0)])
    half = (kept + other.astype(F32)).astype(BF).reshape(16, 4, CHUNK, C)
    got = lax.all_to_all(half, ("x", "y"), 0, 0)
    grad_near, grad_far = from_neighbours(near, far)
    local, ended = inner_back(at_core, near, far, weight, up, half)
    part = mixed_rows(got, ended)
    got = lax.all_to_all(part, ("zl", "sample"), 0, 0)
    owner = core * 16 + lax.axis_index("x") * 4 + lax.axis_index("y")
    at = jnp.minimum(owner * CHUNK, rows - CHUNK).reshape(1)
    step = spread_step(at, got, first_moment, second_moment)
    whole = lax.all_to_all(step, ("core", "x", "y"), 0, 0)
    grad_volume = outer_back(at_core, grad_near, grad_far, weight, local)
    direction = first_rows(whole.reshape(OWNERS * CHUNK, C), rows)
    return (grad_volume.reshape(volume.shape), direction)


def solution(mesh):
    fine = Mesh(
        mesh.devices.reshape(4, 4, 2, 2, 4), ("x", "y", "zl", "core", "sample")
    )
    field = P("sample", SPACE, None, None, None)
    return jax.shard_map(
        body,
        mesh=fine,
        in_specs=(field, field, P(), P("sample", None), P("sample", None)),
        out_specs=(field, P("sample", None)),
        check_vma=False,
    )
```

time: 94 us -> 121 us (1.29)
  Pallas kernels: 32.5 us -> 68.7 us
  starting transfers between devices: 44.7 us -> 32.8 us
  waiting for transfers between devices: 7.04 us -> 15.6 us
  local copies, waits for them, and re-layouts: 7.17 us -> 1.69 us
    pallas_call x5 -> x6, Pallas kernels: 16.2 us -> 52.4 us  [the longest x2 35.2 us: one_plane(): pl.pallas_call(plane_kernel, out_shape=[jax.ShapeDtypeStruct((CELLS, C),...]
    all_to_all x1, waiting for transfers between devices: 0.01 us -> 7.03 us  [body(): got = lax.all_to_all(part, ('zl', 'sample'), 0, 0)]
    ppermute x4, starting transfers between devices: 15.8 us -> 9.21 us  [the longest x2 5.79 us: from_neighbours(): far_halo = lax.ppermute(far, SPACE, pairs + [(j, i) for i, j in pairs])]
    ppermute x4, waiting for transfers between devices: 0.01 us -> 5.97 us  [the longest x2 5.97 us: from_neighbours(): far_halo = lax.ppermute(far, SPACE, pairs + [(j, i) for i, j in pairs])]
    unnamed x20 -> x22, local copies, waits for them, and re-layouts: 7.17 us -> 1.69 us
    all_to_all x1, waiting for transfers between devices: 3.92 us -> 0.66 us  [body(): whole = lax.all_to_all(step, ('core', 'x', 'y'), 0, 0)]
    all_to_all x1, starting transfers between devices: 11.7 us -> 8.65 us  [body(): got = lax.all_to_all(part, ('zl', 'sample'), 0, 0)]
    all_to_all x1, starting transfers between devices: 8.78 us -> 6.71 us  [body(): got = lax.all_to_all(half, ('x', 'y'), 0, 0)]
  transfers between devices with their start and end apart: 8 -> 8, of which waited for: 3 -> 4; matrix products, arithmetic and copies ran while one was open for 0% -> 0% of each run, Pallas kernels for 22% -> 19%
where the time goes in v2:
time: 121 us
  Pallas kernels  68.7 us (57%)
  starting transfers between devices  32.8 us (27%)
  waiting for transfers between devices  15.6 us (13%)
  local copies, waits for them, and re-layouts  1.69 us (1%)
    pallas_call x2, Pallas kernels, one_plane(): pl.pallas_call(plane_kernel, out_shape=[jax.ShapeDtypeStruct((CELLS, C),...  35.2 us
    all_to_all x1, starting transfers between devices, body(): got = lax.all_to_all(part, ('zl', 'sample'), 0, 0)  8.65 us
    all_to_all x1, starting transfers between devices, body(): whole = lax.all_to_all(step, ('core', 'x', 'y'), 0, 0)  8.18 us
    pallas_call x1, Pallas kernels, inner_back(): pl.pallas_call(inner_back_kernel, out_shape=[jax.ShapeDtypeStruct((2, CEL...  7.49 us
    pallas_call x1, Pallas kernels, outer_back(): pl.pallas_call(outer_back_kernel, out_shape=jax.ShapeDtypeStruct((2, CELL...  7.15 us
    all_to_all x1, waiting for transfers between devices, body(): got = lax.all_to_all(part, ('zl', 'sample'), 0, 0)  7.03 us
    pallas_call x1, Pallas kernels, kernel_gradient(): pl.pallas_call(taps_kernel, out_shape=[jax.ShapeDtypeStruct((64, CHUNK, C...  6.78 us
    all_to_all x1, starting transfers between devices, body(): got = lax.all_to_all(half, ('x', 'y'), 0, 0)  6.71 us
  transfers between devices with their start and end apart: 8, of which 4 were waited for; matrix products, arithmetic and copies ran while one was open for 0% of the time, Pallas kernels for 19%

profile of v2, /device:TPU:1, one launch (start us, length us, event | category | flops | bytes accessed | tf_op | source)
XLA Modules:
  0.0 120.6 jit_solution(13609040318885741588)
XLA Ops:
  0.7 17.6 %far_plane.1 = (bf16[2048,128]{1,0:T(8,128)(2,1)}, f32[8,128]{1,0:T(8,128)}) custom-call(s32[1]{0:T(128)} %bitcast.at_ref.later.core_ref, bf16[2,2048,128]{2,1,0:T(8,128)(2,1)} %bitcast.8, s32[1]{0:T(128)} %bitcast.at_ref.later.core_ref), custom_call_target="tpu_custom_call" | custom-call | bytes 1048576 | tf_op jit(solution)/shard_map/far_plane/pallas_call | solution.py:393
  18.3 17.6 %near_plane.1 = (bf16[2048,128]{1,0:T(8,128)(2,1)}, f32[8,128]{1,0:T(8,128)}) custom-call(s32[1]{0:T(128)} %bitcast.1.at_ref, bf16[2,2048,128]{2,1,0:T(8,128)(2,1)} %bitcast.9, f32[8,128]{1,0:T(8,128)} %get-tuple-element.14.later), custom_call_target="tpu_custom_call" | custom-call | bytes 1048576 | tf_op jit(solution)/shard_map/near_plane/pallas_call | solution.py:393
  35.8 3.3 %collective-permute-start = (bf16[2048,128]{1,0:T(8,128)(2,1)}, bf16[2048,128]{1,0:T(8,128)(2,1)S(1)}, u32[]{:S(2)}, u32[]{:S(2)}) collective-permute-start(bf16[2048,128]{1,0:T(8,128)(2,1)} %get-tuple-element.15), channel_id=1, source_target_pairs={{0,4},{4,0},{1,5},{5,1},{2,6},{6,2},{3,7},{7,3},{8,12},{12,8},{9,1... | collective-permute-start | bytes 1572872 | tf_op jit(solution)/shard_map/ppermute | solution.py:480
  39.2 2.0 %collective-permute-start.2 = (bf16[2048,128]{1,0:T(8,128)(2,1)}, bf16[2048,128]{1,0:T(8,128)(2,1)S(1)}, u32[]{:S(2)}, u32[]{:S(2)}) collective-permute-start(bf16[2048,128]{1,0:T(8,128)(2,1)} %get-tuple-element.18), channel_id=1, source_target_pairs={{4,8},{12,16},{20,24},{28,32},{36,40},{44,48},{52,56},{60,64},{68,... | collective-permute-start | bytes 1572872 | tf_op jit(solution)/shard_map/ppermute | solution.py:479
  41.2 4.5 %inner_conv.1 = (f32[2,2048,128]{2,1,0:T(8,128)S(1)}, bf16[256,2048]{1,0:T(8,128)(2,1)S(1)}) custom-call(bf16[2,2048,128]{2,1,0:T(8,128)(2,1)S(1)} %bitcast.10, bf16[3456,128]{1,0:T(8,128)(2,1)S(1)} %copy-done.2), custom_call_target="tpu_custom_call" | custom-call | flops 2415919104 | bytes 5242880 | tf_op jit(solution)/shard_map/inner_conv/pallas_call | solution.py:138
  45.8 2.5 %near_conv.1 = (bf16[2048,128]{1,0:T(8,128)(2,1)S(1)}, f32[8,128]{1,0:T(8,128)S(1)}) custom-call(s32[1]{0:T(128)} %bitcast.1.at_ref, bf16[2048,128]{1,0:T(8,128)(2,1)S(1)} %collective-permute-done.halo.near_halo, bf16[3456,128]{1,0:T(8,128)(2,1)S(1)} %copy-done.2, f32[2,2048,128]{2,1,0:T(8,128)S(1)} %get-tuple-element.16.inner, ...), custom_call_target="tpu_custom_call" | custom-call | flops 1207959552 | bytes 3145728 | tf_op jit(solution)/shard_map/near_conv/pallas_call | solution.py:183
  48.3 6.0 %collective-permute-done.2.halo.far_halo = bf16[2048,128]{1,0:T(8,128)(2,1)S(1)} collective-permute-done((bf16[2048,128]{1,0:T(8,128)(2,1)}, bf16[2048,128]{1,0:T(8,128)(2,1)S(1)}, u32[]{:S(2)}, u32[]{:S(2)}) %collective-permute-start.2) | collective-permute-done | bytes 524320 | tf_op jit(solution)/shard_map/ppermute | solution.py:479
  54.2 2.8 %far_conv.1 = (bf16[2048,128]{1,0:T(8,128)(2,1)S(1)}, f32[8,128]{1,0:T(8,128)}) custom-call(s32[1]{0:T(128)} %bitcast.at_ref.later.core_ref, bf16[2048,128]{1,0:T(8,128)(2,1)S(1)} %collective-permute-done.2.halo.far_halo, bf16[3456,128]{1,0:T(8,128)(2,1)S(1)} %copy-done.2, f32[2,2048,128]{2,1,0:T(8,128)S(1)} %get-tuple-element.16.inner, ...), custom_call_target="tpu_custom_call" | custom-call | flops 1207959552 | bytes 3145728 | tf_op jit(solution)/shard_map/far_conv/pallas_call | solution.py:183
  57.1 6.8 %kernel_gradient.1 = (f32[64,32,128]{2,1,0:T(8,128)S(1)}, bf16[64,32,128]{2,1,0:T(8,128)(2,1)S(1)}) custom-call(s32[1]{0:T(128)} %bitcast.at_ref.later.core_ref, bf16[2048,128]{1,0:T(8,128)(2,1)S(1)} %get-tuple-element.17.near, bf16[2048,128]{1,0:T(8,128)(2,1)S(1)} %get-tuple-element.20.far, bf16[2048,128]{1,0:T(8,128)(2,1)S(1)} %collective-permute-done.halo.near_halo, ...), custom_call_target="tpu_custom_call" | custom-call | flops 4831838208 | bytes 5242880 | tf_op jit(solution)/shard_map/kernel_gradient/pallas_call | solution.py:245
  64.0 1.9 %collective-permute-done.4 = bf16[64,32,128]{2,1,0:T(8,128)(2,1)S(1)} collective-permute-done((bf16[64,32,128]{2,1,0:T(8,128)(2,1)S(1)}, bf16[64,32,128]{2,1,0:T(8,128)(2,1)S(1)}, u32[]{:S(2)}, u32[]{:S(2)}) %collective-permute-start.4) | collective-permute-done | bytes 524320 | tf_op jit(solution)/shard_map/ppermute | solution.py:502
  65.9 1.0 add_convert_fusion
  66.8 6.7 %all-to-all-start = ((bf16[16,4,32,128]{3,2,1,0:T(8,128)(2,1)}), bf16[16,4,32,128]{3,2,1,0:T(8,128)(2,1)S(1)}, u32[]{:S(2)}, u32[]{:S(2)}) async-start(bf16[16,4,32,128]{3,2,1,0:T(8,128)(2,1)} %bitcast.4.later), calls=%async_computation | async-start | bytes 1048576 | tf_op jit(solution)/shard_map/all_to_all | solution.py:504
  73.6 3.7 %collective-permute-start.3 = (bf16[2048,128]{1,0:T(8,128)(2,1)S(1)}, bf16[2048,128]{1,0:T(8,128)(2,1)S(1)}, u32[]{:S(2)}, u32[]{:S(2)}) collective-permute-start(bf16[2048,128]{1,0:T(8,128)(2,1)S(1)} %copy-done.8), channel_id=1, source_target_pairs={{4,8},{12,16},{20,24},{28,32},{36,40},{44,48},{52,56},{60,64},{68,... | collective-permute-start | bytes 1572872 | tf_op jit(solution)/shard_map/ppermute | solution.py:479
  77.5 7.5 %inner_back.1 = (f32[2,2048,128]{2,1,0:T(8,128)}, f32[8,128]{1,0:T(8,128)}) custom-call(s32[1]{0:T(128)} %bitcast.at_ref.later.core_ref, bf16[2048,128]{1,0:T(8,128)(2,1)} %copy-done.6, bf16[2048,128]{1,0:T(8,128)(2,1)} %copy-done.7, bf16[3456,128]{1,0:T(8,128)(2,1)} %weight.9, bf16[2,2048,128]{2,1,0:T(8,128)(2,1)} %bitcast.11, ...), custom_call_target="tpu_custom_call" | custom-call | flops 2415919104 | bytes 5242880 | tf_op jit(solution)/shard_map/inner_back/pallas_call | solution.py:300
  85.0 0.7 copy-done.5
  85.7 0.7 mixed_rows.1
  86.4 8.7 %all-to-all-start.1 = ((f32[8,32,128]{2,1,0:T(8,128)}), f32[8,32,128]{2,1,0:T(8,128)S(1)}, u32[]{:S(2)}, u32[]{:S(2)}) async-start(f32[8,32,128]{2,1,0:T(8,128)} %mixed_rows.1), calls=%async_computation.1 | async-start | bytes 262144 | tf_op jit(solution)/shard_map/all_to_all | solution.py:508
  95.0 7.0 %all-to-all-done.1.got = f32[8,32,128]{2,1,0:T(8,128)S(1)} async-done(((f32[8,32,128]{2,1,0:T(8,128)}), f32[8,32,128]{2,1,0:T(8,128)S(1)}, u32[]{:S(2)}, u32[]{:S(2)}) %all-to-all-start.1) | async-done | bytes 131104 | tf_op jit(solution)/shard_map/all_to_all | solution.py:508
  102.1 0.8 spread_step.1
  102.8 8.2 %all-to-all-start.2 = ((bf16[32,32,128]{2,1,0:T(8,128)(2,1)}), bf16[32,32,128]{2,1,0:T(8,128)(2,1)S(1)}, u32[]{:S(2)}, u32[]{:S(2)}) async-start(bf16[32,32,128]{2,1,0:T(8,128)(2,1)} %spread_step.1), calls=%async_computation.2 | async-start | bytes 524288 | tf_op jit(solution)/shard_map/all_to_all | solution.py:512
  111.1 0.8 copy-done.9
  112.0 7.2 %outer_back.1 = bf16[2,2048,128]{2,1,0:T(8,128)(2,1)} custom-call(s32[1]{0:T(128)} %bitcast.at_ref.later.core_ref, bf16[2048,128]{1,0:T(8,128)(2,1)} %copy-done.10, bf16[2048,128]{1,0:T(8,128)(2,1)} %copy-done.9, bf16[3456,128]{1,0:T(8,128)(2,1)} %weight.9, f32[2,2048,128]{2,1,0:T(8,128)} %get-tuple-element.24.kept), custom_call_target="tpu_custom_call" | custom-call | flops 2415919104 | bytes 5242880 | tf_op jit(solution)/shard_map/outer_back/pallas_call | solution.py:367
  119.2 0.7 all-to-all-done.2
  119.8 0.8 first_rows.1
  (26 shorter events, 0.4 us)
Async XLA Ops:
  0.6 40.6 %copy-start = (bf16[1,2,32,64,128]{4,3,2,1,0:T(8,128)(2,1)S(1)}, bf16[1,2,32,64,128]{4,3,2,1,0:T(8,128)(2,1)}, u32[]{:S(2)}) copy-start(bf16[1,2,32,64,128]{4,3,2,1,0:T(8,128)(2,1)} %param.5) | copy-start | bytes 3145732
  0.6 40.6 %copy-start.2 = (bf16[3456,128]{1,0:T(8,128)(2,1)S(1)}, bf16[3456,128]{1,0:T(8,128)(2,1)}, u32[]{:S(2)}) copy-start(bf16[3456,128]{1,0:T(8,128)(2,1)} %weight.9) | copy-start | bytes 2654212
  35.8 9.9 %collective-permute-start = (bf16[2048,128]{1,0:T(8,128)(2,1)}, bf16[2048,128]{1,0:T(8,128)(2,1)S(1)}, u32[]{:S(2)}, u32[]{:S(2)}) collective-permute-start(bf16[2048,128]{1,0:T(8,128)(2,1)} %get-tuple-element.15), channel_id=1, source_target_pairs={{0,4},{4,0},{1,5},{5,1},{2,6},{6,2},{3,7},{7,3},{8,12},{12,8},{9,1... | collective-permute-start | bytes 1572872 | tf_op jit(solution)/shard_map/ppermute | solution.py:480
  39.2 6.6 %copy-start.1 = (bf16[1,2,32,64,128]{4,3,2,1,0:T(8,128)(2,1)S(1)}, bf16[1,2,32,64,128]{4,3,2,1,0:T(8,128)(2,1)}, u32[]{:S(2)}) copy-start(bf16[1,2,32,64,128]{4,3,2,1,0:T(8,128)(2,1)} %param.6) | copy-start | bytes 3145732
  39.2 15.1 %collective-permute-start.2 = (bf16[2048,128]{1,0:T(8,128)(2,1)}, bf16[2048,128]{1,0:T(8,128)(2,1)S(1)}, u32[]{:S(2)}, u32[]{:S(2)}) collective-permute-start(bf16[2048,128]{1,0:T(8,128)(2,1)} %get-tuple-element.18), channel_id=1, source_target_pairs={{4,8},{12,16},{20,24},{28,32},{36,40},{44,48},{52,56},{60,64},{68,... | collective-permute-start | bytes 1572872 | tf_op jit(solution)/shard_map/ppermute | solution.py:479
  48.3 29.1 %copy-start.6 = (bf16[2048,128]{1,0:T(8,128)(2,1)}, bf16[2048,128]{1,0:T(8,128)(2,1)S(1)}, u32[]{:S(2)}) copy-start(bf16[2048,128]{1,0:T(8,128)(2,1)S(1)} %get-tuple-element.17.near) | copy-start | bytes 1572868
  57.1 6.8 %copy-start.7 = (bf16[2048,128]{1,0:T(8,128)(2,1)}, bf16[2048,128]{1,0:T(8,128)(2,1)S(1)}, u32[]{:S(2)}) copy-start(bf16[2048,128]{1,0:T(8,128)(2,1)S(1)} %get-tuple-element.20.far) | copy-start | bytes 1572868
  63.9 9.7 %copy-start.8 = (bf16[2048,128]{1,0:T(8,128)(2,1)S(1)}, bf16[2048,128]{1,0:T(8,128)(2,1)}, u32[]{:S(2)}) copy-start(bf16[2048,128]{1,0:T(8,128)(2,1)} %copy-done.7) | copy-start | bytes 1572868
  63.9 2.0 %collective-permute-start.4 = (bf16[64,32,128]{2,1,0:T(8,128)(2,1)S(1)}, bf16[64,32,128]{2,1,0:T(8,128)(2,1)S(1)}, u32[]{:S(2)}, u32[]{:S(2)}) collective-permute-start(bf16[64,32,128]{2,1,0:T(8,128)(2,1)S(1)} %get-tuple-element.23), channel_id=1, source_target_pairs={{0,4},{4,0},{1,5},{5,1},{2,6},{6,2},{3,7},{7,3},{8,12},{12,8},{9,1... | collective-permute-start | bytes 1572872 | tf_op jit(solution)/shard_map/ppermute | solution.py:502
  66.8 18.1 %all-to-all-start = ((bf16[16,4,32,128]{3,2,1,0:T(8,128)(2,1)}), bf16[16,4,32,128]{3,2,1,0:T(8,128)(2,1)S(1)}, u32[]{:S(2)}, u32[]{:S(2)}) async-start(bf16[16,4,32,128]{3,2,1,0:T(8,128)(2,1)} %bitcast.4.later), calls=%async_computation | async-start | bytes 1048576 | tf_op jit(solution)/shard_map/all_to_all | solution.py:504
  73.6 28.5 %copy-start.3 = (f32[864,128]{1,0:T(8,128)S(1)}, f32[864,128]{1,0:T(8,128)}, u32[]{:S(2)}) copy-start(f32[864,128]{1,0:T(8,128)} %first.1) | copy-start | bytes 1327108
  73.6 28.5 %copy-start.4 = (f32[864,128]{1,0:T(8,128)S(1)}, f32[864,128]{1,0:T(8,128)}, u32[]{:S(2)}) copy-start(f32[864,128]{1,0:T(8,128)} %second.1) | copy-start | bytes 1327108
  73.6 37.4 %collective-permute-start.3 = (bf16[2048,128]{1,0:T(8,128)(2,1)S(1)}, bf16[2048,128]{1,0:T(8,128)(2,1)S(1)}, u32[]{:S(2)}, u32[]{:S(2)}) collective-permute-start(bf16[2048,128]{1,0:T(8,128)(2,1)S(1)} %copy-done.8), channel_id=1, source_target_pairs={{4,8},{12,16},{20,24},{28,32},{36,40},{44,48},{52,56},{60,64},{68,... | collective-permute-start | bytes 1572872 | tf_op jit(solution)/shard_map/ppermute | solution.py:479
  77.4 33.7 %collective-permute-start.1 = (bf16[2048,128]{1,0:T(8,128)(2,1)S(1)}, bf16[2048,128]{1,0:T(8,128)(2,1)S(1)}, u32[]{:S(2)}, u32[]{:S(2)}) collective-permute-start(bf16[2048,128]{1,0:T(8,128)(2,1)S(1)} %get-tuple-element.17.near), channel_id=1, source_target_pairs={{0,4},{4,0},{1,5},{5,1},{2,6},{6,2},{3,7},{7,3},{8,12},{12,8},{9,1... | collective-permute-start | bytes 1572872 | tf_op jit(solution)/shard_map/ppermute | solution.py:480
  85.0 0.7 copy-start.5
  86.4 15.7 %all-to-all-start.1 = ((f32[8,32,128]{2,1,0:T(8,128)}), f32[8,32,128]{2,1,0:T(8,128)S(1)}, u32[]{:S(2)}, u32[]{:S(2)}) async-start(f32[8,32,128]{2,1,0:T(8,128)} %mixed_rows.1), calls=%async_computation.1 | async-start | bytes 262144 | tf_op jit(solution)/shard_map/all_to_all | solution.py:508
  102.8 17.0 %all-to-all-start.2 = ((bf16[32,32,128]{2,1,0:T(8,128)(2,1)}), bf16[32,32,128]{2,1,0:T(8,128)(2,1)S(1)}, u32[]{:S(2)}, u32[]{:S(2)}) async-start(bf16[32,32,128]{2,1,0:T(8,128)(2,1)} %spread_step.1), calls=%async_computation.2 | async-start | bytes 524288 | tf_op jit(solution)/shard_map/all_to_all | solution.py:512
  111.0 0.8 copy-start.9
  111.0 1.0 copy-start.10

commit v3 on v2

--- a/solution.py
+++ b/solution.py
@@ -261,22 +261,43 @@
     )(core, near, far, near_halo, far_halo, vol_t)
 
 
-def inner_back_kernel(
-    core_ref, near, far, weight, upstream, later, out, ended, field, mixed, held, sem
+def back_kernel(
+    core_ref,
+    near,
+    far,
+    near_halo,
+    far_halo,
+    weight,
+    given,
+    later,
+    out,
+    field,
+    mixed,
+    held,
+    upstream,
+    sem,
+    given_sem,
 ):
     copy = fetched(weight, held, sem)
-    ended[...] = jnp.zeros_like(ended)
-    shifted_columns(ordered(core_ref[0], near, far), field, 0, False)
+    given_copy = fetched(given, upstream, given_sem)
+    core = core_ref[0]
+    low, high = ordered(core, near, far)
+    before, after = ordered(core, near_halo, far_halo)
+    shifted_columns([before, low, high, after], field, 0, False)
+    blank = jnp.zeros((C, C), BF)
     copy.wait()
     for b in range(3):
         for c in range(3):
-            base = (b * 3 + c) * 256
-            for p in range(2):
+            base = (b * 3 + c) * 512
+            for p in range(4):
                 for z in range(2):
-                    t = tap(1 + z - p, 2 - b, 2 - c)
+                    a = 2 - (p - z)
+                    t = tap(a, 2 - b, 2 - c)
                     mixed[z * C : (z + 1) * C, base + p * C : base + (p + 1) * C] = (
-                        held[t * C : (t + 1) * C, :]
+                        held[t * C : (t + 1) * C, :] if 0 <= a < 3 else blank
                     )
+
+    given_copy.wait()
 
     def tile(i, carry):
         at = pl.multiple_of(i * TILE, TILE)
@@ -290,116 +311,52 @@
         for z in range(2):
             out[z, rows, :] = (
                 upstream[z, rows, :].astype(F32) + got[:, z * C : (z + 1) * C]
-            )
+            ).astype(BF)
         return carry
 
     lax.fori_loop(0, CELLS // TILE, tile, 0)
 
 
-def inner_back(core, near, far, weight, upstream, later):
-    return pl.pallas_call(
-        inner_back_kernel,
-        out_shape=[
-            jax.ShapeDtypeStruct((2, CELLS, C), F32),
-            FLAG,
-        ],
-        in_specs=[SMEM, VMEM, VMEM, HBM, VMEM, ANY],
-        out_specs=[VMEM, VMEM],
-        scratch_shapes=[
-            pltpu.VMEM((3, PADDED, 2 * C), BF),
-            pltpu.VMEM((2 * C, 9 * 256), BF),
-            pltpu.VMEM((27 * C, C), BF),
-            pltpu.SemaphoreType.DMA,
-        ],
-        compiler_params=WHOLE,
-        cost_estimate=cost(2 * CELLS * 2304 * 256, 5 << 20),
-        name="inner_back",
-    )(core, near, far, weight, upstream, later)
-
-
-def outer_back_kernel(
-    core_ref, near, far, weight, kept, out, field, mixed, held, inner, sem, kept_sem
-):
-    copy = fetched(weight, held, sem)
-    kept_copy = fetched(kept, inner, kept_sem)
-    core = core_ref[0]
-    shifted_columns([rows_of(near), rows_of(far)], field, 0, False)
-    copy.wait()
-    for k in range(2):
-        z = 1 - core if k == 0 else core
-        first = pl.multiple_of((2 - 2 * z) * 9 * C, C)
-        for b in range(3):
-            for c in range(3):
-                base = (b * 3 + c) * C
-                mixed[k, :, base : base + C] = held[
-                    pl.ds(first + tap(0, 2 - b, 2 - c) * C, C), :
-                ]
-
-    kept_copy.wait()
-
-    def tile(i, carry):
-        at = pl.multiple_of(i * TILE, TILE)
-        rows = pl.ds(at, TILE)
-        for k in range(2):
-            z = 1 - core if k == 0 else core
-            lhs = jnp.concatenate(
-                [
-                    field[
-                        c,
-                        pl.ds(pl.multiple_of(at + b * COLS, COLS), TILE),
-                        k * C : (k + 1) * C,
-                    ]
-                    for b in range(3)
-                    for c in range(3)
-                ],
-                axis=1,
-            )
-            got = lax.dot_general(
-                lhs, mixed[k], (((1,), (1,)), ((), ())), preferred_element_type=F32
-            )
-            out[z, rows, :] = (inner[z, rows, :] + got).astype(BF)
-        return carry
-
-    lax.fori_loop(0, CELLS // TILE, tile, 0)
-
-
-def outer_back(core, near, far, weight, inner):
-    return pl.pallas_call(
-        outer_back_kernel,
+def back_conv(core, near, far, near_halo, far_halo, weight, upstream, later):
+    return pl.pallas_call(
+        back_kernel,
         out_shape=jax.ShapeDtypeStruct((2, CELLS, C), BF),
-        in_specs=[SMEM, VMEM, VMEM, HBM, HBM],
+        in_specs=[SMEM, VMEM, VMEM, VMEM, VMEM, HBM, HBM, ANY],
         out_specs=VMEM,
         scratch_shapes=[
-            pltpu.VMEM((3, PADDED, 2 * C), BF),
-            pltpu.VMEM((2, C, 9 * C), BF),
+            pltpu.VMEM((3, PADDED, 4 * C), BF),
+            pltpu.VMEM((2 * C, 9 * 512), BF),
             pltpu.VMEM((27 * C, C), BF),
-            pltpu.VMEM((2, CELLS, C), F32),
+            pltpu.VMEM((2, CELLS, C), BF),
             pltpu.SemaphoreType.DMA,
             pltpu.SemaphoreType.DMA,
         ],
         compiler_params=WHOLE,
-        cost_estimate=cost(2 * CELLS * 2304 * 256, 5 << 20),
-        name="outer_back",
-    )(core, near, far, weight, inner)
-
-
-def plane_kernel(at_ref, vol, later, plane, ended, sem):
-    copy = fetched(vol.at[at_ref[0]], plane, sem)
-    ended[...] = jnp.zeros_like(ended)
-    copy.wait()
-
-
-def one_plane(name, at, vol, later):
-    return pl.pallas_call(
-        plane_kernel,
-        out_shape=[jax.ShapeDtypeStruct((CELLS, C), BF), FLAG],
-        in_specs=[SMEM, HBM, ANY],
-        out_specs=[HBM, VMEM],
-        scratch_shapes=[pltpu.SemaphoreType.DMA],
+        cost_estimate=cost(2 * CELLS * 4608 * 256, 5 << 20),
+        name="back_conv",
+    )(core, near, far, near_halo, far_halo, weight, upstream, later)
+
+
+def planes_kernel(core_ref, vol, near, far, sems):
+    core = core_ref[0]
+    first = fetched(vol.at[core], far, sems.at[0])
+    second = fetched(vol.at[1 - core], near, sems.at[1])
+    first.wait()
+    second.wait()
+
+
+def both_planes(core, vol):
+    plane = jax.ShapeDtypeStruct((CELLS, C), BF)
+    return pl.pallas_call(
+        planes_kernel,
+        out_shape=[plane, plane],
+        in_specs=[SMEM, HBM],
+        out_specs=[VMEM, VMEM],
+        scratch_shapes=[pltpu.SemaphoreType.DMA((2,))],
         compiler_params=WHOLE,
-        cost_estimate=cost(0, 1 << 20),
-        name=name,
-    )(at, vol, later)
+        cost_estimate=cost(0, 2 << 20),
+        name="both_planes",
+    )(core, vol)
 
 
 def first_rows_kernel(whole, out):
@@ -418,34 +375,35 @@
     )(whole)
 
 
-def mix_kernel(got, later, out):
+def mix_kernel(got, out):
     for group in range(4):
         total = got[0, group].astype(F32)
         for k in range(1, 16):
             total += got[k, group].astype(F32)
-        out[group] = total
-        out[4 + group] = total
-
-
-def mixed_rows(got, later):
+        out[group] = total.astype(BF)
+        out[4 + group] = total.astype(BF)
+
+
+def mixed_rows(got):
     return pl.pallas_call(
         mix_kernel,
-        out_shape=jax.ShapeDtypeStruct((8, CHUNK, C), F32),
-        in_specs=[VMEM, ANY],
+        out_shape=jax.ShapeDtypeStruct((8, CHUNK, C), BF),
+        in_specs=[VMEM],
         out_specs=VMEM,
         compiler_params=SMALL,
         cost_estimate=cost(1 << 18, 1 << 20),
         name="mixed_rows",
-    )(got, later)
-
-
-def step_kernel(at_ref, got, first, second, out):
-    total = got[0]
+    )(got)
+
+
+def step_kernel(at_ref, got, first, second, out, ended):
+    total = got[0].astype(F32)
     for k in range(1, 8):
-        total += got[k]
+        total += got[k].astype(F32)
     at = pl.multiple_of(at_ref[0], CHUNK)
     rows = pl.ds(at, CHUNK)
     step = adam(total, first[rows, :], second[rows, :])
+    ended[...] = jnp.zeros_like(ended)
     step = step.astype(BF)
     for k in range(OWNERS):
         out[k] = step
@@ -454,9 +412,9 @@
 def spread_step(at, got, first, second):
     return pl.pallas_call(
         step_kernel,
-        out_shape=jax.ShapeDtypeStruct((OWNERS, CHUNK, C), BF),
+        out_shape=[jax.ShapeDtypeStruct((OWNERS, CHUNK, C), BF), FLAG],
         in_specs=[SMEM] + [VMEM] * 3,
-        out_specs=VMEM,
+        out_specs=[VMEM, VMEM],
         compiler_params=SMALL,
         cost_estimate=cost(1 << 18, 1 << 20),
         name="spread_step",
@@ -486,9 +444,7 @@
     up = upstream.reshape(2, CELLS, C)
     core = lax.axis_index("core")
     at_core, at_near = core.reshape(1), (1 - core).reshape(1)
-    far_plane, ended = one_plane("far_plane", at_core, vol, at_core)
-    near_plane, ended = one_plane("near_plane", at_near, vol, ended)
-    near_halo, far_halo = from_neighbours(near_plane, far_plane)
+    near_halo, far_halo = from_neighbours(*both_planes(at_core, vol))
     inner, vol_t = inner_conv(vol, weight)
     near, ended = outer_conv(
         "near_conv", at_near, near_halo, weight, inner, up, at_core
@@ -503,14 +459,15 @@
     half = (kept + other.astype(F32)).astype(BF).reshape(16, 4, CHUNK, C)
     got = lax.all_to_all(half, ("x", "y"), 0, 0)
     grad_near, grad_far = from_neighbours(near, far)
-    local, ended = inner_back(at_core, near, far, weight, up, half)
-    part = mixed_rows(got, ended)
+    part = mixed_rows(got)
     got = lax.all_to_all(part, ("zl", "sample"), 0, 0)
     owner = core * 16 + lax.axis_index("x") * 4 + lax.axis_index("y")
     at = jnp.minimum(owner * CHUNK, rows - CHUNK).reshape(1)
-    step = spread_step(at, got, first_moment, second_moment)
+    step, ended = spread_step(at, got, first_moment, second_moment)
     whole = lax.all_to_all(step, ("core", "x", "y"), 0, 0)
-    grad_volume = outer_back(at_core, grad_near, grad_far, weight, local)
+    grad_volume = back_conv(
+        at_core, near, far, grad_near, grad_far, weight, up, ended
+    )
     direction = first_rows(whole.reshape(OWNERS * CHUNK, C), rows)
     return (grad_volume.reshape(volume.shape), direction)
 

time: 121 us -> 87.9 us (0.73)
  Pallas kernels: 68.7 us -> 31 us
  waiting for transfers between devices: 15.6 us -> 19.2 us
  local copies, waits for them, and re-layouts: 1.69 us -> 3.77 us
    pallas_call x5 -> x3, Pallas kernels: 50.6 us -> 12.9 us  [the longest x1 9.96 us: back_conv(): pl.pallas_call(back_kernel, out_shape=jax.ShapeDtypeStruct((2, CELLS, C),...]
    all_to_all x1, waiting for transfers between devices: 0.01 us -> 7.05 us  [body(): got = lax.all_to_all(half, ('x', 'y'), 0, 0)]
    ppermute x2, waiting for transfers between devices: 5.97 us -> 3.59 us  [from_neighbours(): far_halo = lax.ppermute(far, SPACE, pairs + [(j, i) for i, j in pairs])]
    unnamed x22 -> x18, local copies, waits for them, and re-layouts: 1.69 us -> 3.77 us
  transfers between devices with their start and end apart: 8 -> 8, of which waited for: 4 -> 4; matrix products, arithmetic and copies ran while one was open for 0% -> 0% of each run, Pallas kernels for 19% -> 21%
where the time goes in v3:
time: 87.9 us; the launch traced here: 87.4 us
  starting transfers between devices  31.7 us (36%)
  Pallas kernels  31 us (35%)
  waiting for transfers between devices  19.2 us (22%)
  local copies, waits for them, and re-layouts  3.77 us (4%)
  other arithmetic  0.98 us (1%)
    pallas_call x1, Pallas kernels, back_conv(): pl.pallas_call(back_kernel, out_shape=jax.ShapeDtypeStruct((2, CELLS, C),...  9.96 us
    all_to_all x1, starting transfers between devices, body(): got = lax.all_to_all(part, ('zl', 'sample'), 0, 0)  8.17 us
    all_to_all x1, starting transfers between devices, body(): whole = lax.all_to_all(step, ('core', 'x', 'y'), 0, 0)  7.77 us
    all_to_all x1, waiting for transfers between devices, body(): got = lax.all_to_all(half, ('x', 'y'), 0, 0)  7.05 us
    pallas_call x1, Pallas kernels, kernel_gradient(): pl.pallas_call(taps_kernel, out_shape=[jax.ShapeDtypeStruct((64, CHUNK, C...  6.79 us
    all_to_all x1, starting transfers between devices, body(): got = lax.all_to_all(half, ('x', 'y'), 0, 0)  6.72 us
    all_to_all x1, waiting for transfers between devices, body(): got = lax.all_to_all(part, ('zl', 'sample'), 0, 0)  6.63 us
    ppermute x2, starting transfers between devices, from_neighbours(): far_halo = lax.ppermute(far, SPACE, pairs + [(j, i) for i, j in pairs])  5.5 us
  transfers between devices with their start and end apart: 8, of which 4 were waited for; matrix products, arithmetic and copies ran while one was open for 0% of the time, Pallas kernels for 21%

profile of v3, /device:TPU:1, one launch (start us, length us, event | category | flops | bytes accessed | tf_op | source)
XLA Modules:
  0.0 87.4 jit_solution(7664058891499169010)
XLA Ops:
  0.6 2.2 %both_planes.1 = (bf16[2048,128]{1,0:T(8,128)(2,1)}, bf16[2048,128]{1,0:T(8,128)(2,1)}) custom-call(s32[1]{0:T(128)} %bitcast.core_ref.later.at_ref, bf16[2,2048,128]{2,1,0:T(8,128)(2,1)} %bitcast.11), custom_call_target="tpu_custom_call" | custom-call | bytes 2097152 | tf_op jit(solution)/shard_map/both_planes/pallas_call | solution.py:350
  2.8 3.3 %collective-permute-start = (bf16[2048,128]{1,0:T(8,128)(2,1)}, bf16[2048,128]{1,0:T(8,128)(2,1)S(1)}, u32[]{:S(2)}, u32[]{:S(2)}) collective-permute-start(bf16[2048,128]{1,0:T(8,128)(2,1)} %get-tuple-element.13), channel_id=1, source_target_pairs={{0,4},{4,0},{1,5},{5,1},{2,6},{6,2},{3,7},{7,3},{8,12},{12,8},{9,1... | collective-permute-start | bytes 1572872 | tf_op jit(solution)/shard_map/ppermute | solution.py:438
  6.2 1.9 %collective-permute-start.1 = (bf16[2048,128]{1,0:T(8,128)(2,1)}, bf16[2048,128]{1,0:T(8,128)(2,1)S(1)}, u32[]{:S(2)}, u32[]{:S(2)}) collective-permute-start(bf16[2048,128]{1,0:T(8,128)(2,1)} %get-tuple-element.16), channel_id=1, source_target_pairs={{4,8},{12,16},{20,24},{28,32},{36,40},{44,48},{52,56},{60,64},{68,... | collective-permute-start | bytes 1572872 | tf_op jit(solution)/shard_map/ppermute | solution.py:437
  8.1 1.2 %copy-done.1 = bf16[3456,128]{1,0:T(8,128)(2,1)S(1)} copy-done((bf16[3456,128]{1,0:T(8,128)(2,1)S(1)}, bf16[3456,128]{1,0:T(8,128)(2,1)}, u32[]{:S(2)}) %copy-start.1) | copy-done | bytes 884760
  9.3 1.2 %copy-done.2 = bf16[1,2,32,64,128]{4,3,2,1,0:T(8,128)(2,1)S(1)} copy-done((bf16[1,2,32,64,128]{4,3,2,1,0:T(8,128)(2,1)S(1)}, bf16[1,2,32,64,128]{4,3,2,1,0:T(8,128)(2,1)}, u32[]{:S(2)}) %copy-start.2) | copy-done | bytes 1048600
  10.5 4.5 %inner_conv.1 = (f32[2,2048,128]{2,1,0:T(8,128)S(1)}, bf16[256,2048]{1,0:T(8,128)(2,1)S(1)}) custom-call(bf16[2,2048,128]{2,1,0:T(8,128)(2,1)S(1)} %bitcast.12, bf16[3456,128]{1,0:T(8,128)(2,1)S(1)} %copy-done.1), custom_call_target="tpu_custom_call" | custom-call | flops 2415919104 | bytes 5242880 | tf_op jit(solution)/shard_map/inner_conv/pallas_call | solution.py:138
  15.0 2.5 %near_conv.1 = (bf16[2048,128]{1,0:T(8,128)(2,1)S(1)}, f32[8,128]{1,0:T(8,128)S(1)}) custom-call(s32[1]{0:T(128)} %bitcast.1.at_ref, bf16[2048,128]{1,0:T(8,128)(2,1)S(1)} %collective-permute-done.halo.near_halo, bf16[3456,128]{1,0:T(8,128)(2,1)S(1)} %copy-done.1, f32[2,2048,128]{2,1,0:T(8,128)S(1)} %get-tuple-element.14.inner, ...), custom_call_target="tpu_custom_call" | custom-call | flops 1207959552 | bytes 3145728 | tf_op jit(solution)/shard_map/near_conv/pallas_call | solution.py:183
  17.5 3.6 %collective-permute-done.1.halo.far_halo = bf16[2048,128]{1,0:T(8,128)(2,1)S(1)} collective-permute-done((bf16[2048,128]{1,0:T(8,128)(2,1)}, bf16[2048,128]{1,0:T(8,128)(2,1)S(1)}, u32[]{:S(2)}, u32[]{:S(2)}) %collective-permute-start.1) | collective-permute-done | bytes 524320 | tf_op jit(solution)/shard_map/ppermute | solution.py:437
  21.1 2.8 %far_conv.1 = (bf16[2048,128]{1,0:T(8,128)(2,1)S(1)}, f32[8,128]{1,0:T(8,128)}) custom-call(s32[1]{0:T(128)} %bitcast.core_ref.later.at_ref, bf16[2048,128]{1,0:T(8,128)(2,1)S(1)} %collective-permute-done.1.halo.far_halo, bf16[3456,128]{1,0:T(8,128)(2,1)S(1)} %copy-done.1, f32[2,2048,128]{2,1,0:T(8,128)S(1)} %get-tuple-element.14.inner, ...), custom_call_target="tpu_custom_call" | custom-call | flops 1207959552 | bytes 3145728 | tf_op jit(solution)/shard_map/far_conv/pallas_call | solution.py:183
  23.9 6.8 %kernel_gradient.1 = (f32[64,32,128]{2,1,0:T(8,128)S(1)}, bf16[64,32,128]{2,1,0:T(8,128)(2,1)S(1)}) custom-call(s32[1]{0:T(128)} %bitcast.core_ref.later.at_ref, bf16[2048,128]{1,0:T(8,128)(2,1)S(1)} %get-tuple-element.15.near, bf16[2048,128]{1,0:T(8,128)(2,1)S(1)} %get-tuple-element.18.far, bf16[2048,128]{1,0:T(8,128)(2,1)S(1)} %collective-permute-done.halo.near_halo, ...), custom_call_target="tpu_custom_call" | custom-call | flops 4831838208 | bytes 5242880 | tf_op jit(solution)/shard_map/kernel_gradient/pallas_call | solution.py:245
  30.8 1.9 %collective-permute-done.4 = bf16[64,32,128]{2,1,0:T(8,128)(2,1)S(1)} collective-permute-done((bf16[64,32,128]{2,1,0:T(8,128)(2,1)S(1)}, bf16[64,32,128]{2,1,0:T(8,128)(2,1)S(1)}, u32[]{:S(2)}, u32[]{:S(2)}) %collective-permute-start.4) | collective-permute-done | bytes 524320 | tf_op jit(solution)/shard_map/ppermute | solution.py:458
  32.7 1.0 %add_convert_fusion = bf16[64,32,128]{2,1,0:T(8,128)(2,1)} fusion(f32[64,32,128]{2,1,0:T(8,128)S(1)} %get-tuple-element.20, bf16[64,32,128]{2,1,0:T(8,128)(2,1)S(1)} %collective-permute-done.4), kind=kLoop, calls=%fused_computation | loop fusion | flops 786432 | bytes 2097152 | tf_op jit(solution)/shard_map/convert_element_type | solution.py:459
  33.7 6.7 %all-to-all-start = ((bf16[16,4,32,128]{3,2,1,0:T(8,128)(2,1)}), bf16[16,4,32,128]{3,2,1,0:T(8,128)(2,1)S(1)}, u32[]{:S(2)}, u32[]{:S(2)}) async-start(bf16[16,4,32,128]{3,2,1,0:T(8,128)(2,1)} %bitcast.5), calls=%async_computation | async-start | bytes 1048576 | tf_op jit(solution)/shard_map/all_to_all | solution.py:460
  40.4 3.6 %collective-permute-start.3 = (bf16[2048,128]{1,0:T(8,128)(2,1)S(1)}, bf16[2048,128]{1,0:T(8,128)(2,1)S(1)}, u32[]{:S(2)}, u32[]{:S(2)}) collective-permute-start(bf16[2048,128]{1,0:T(8,128)(2,1)S(1)} %get-tuple-element.18.far), channel_id=1, source_target_pairs={{4,8},{12,16},{20,24},{28,32},{36,40},{44,48},{52,56},{60,64},{68,... | collective-permute-start | bytes 1572872 | tf_op jit(solution)/shard_map/ppermute | solution.py:437
  44.2 7.0 %all-to-all-done.got = bf16[16,4,32,128]{3,2,1,0:T(8,128)(2,1)S(1)} async-done(((bf16[16,4,32,128]{3,2,1,0:T(8,128)(2,1)}), bf16[16,4,32,128]{3,2,1,0:T(8,128)(2,1)S(1)}, u32[]{:S(2)}, u32[]{:S(2)}) %all-to-all-start) | async-done | bytes 524320 | tf_op jit(solution)/shard_map/all_to_all | solution.py:460
  51.2 0.7 mixed_rows.1
  51.9 8.2 %all-to-all-start.1 = ((bf16[8,32,128]{2,1,0:T(8,128)(2,1)}), bf16[8,32,128]{2,1,0:T(8,128)(2,1)S(1)}, u32[]{:S(2)}, u32[]{:S(2)}) async-start(bf16[8,32,128]{2,1,0:T(8,128)(2,1)} %mixed_rows.1), calls=%async_computation.1 | async-start | bytes 131072 | tf_op jit(solution)/shard_map/all_to_all | solution.py:463
  60.1 6.6 %all-to-all-done.1.got = bf16[8,32,128]{2,1,0:T(8,128)(2,1)S(1)} async-done(((bf16[8,32,128]{2,1,0:T(8,128)(2,1)}), bf16[8,32,128]{2,1,0:T(8,128)(2,1)S(1)}, u32[]{:S(2)}, u32[]{:S(2)}) %all-to-all-start.1) | async-done | bytes 65568 | tf_op jit(solution)/shard_map/all_to_all | solution.py:463
  66.7 0.8 spread_step.1
  67.5 0.6 copy-done.7
  68.0 7.8 %all-to-all-start.2 = ((bf16[32,32,128]{2,1,0:T(8,128)(2,1)}), bf16[32,32,128]{2,1,0:T(8,128)(2,1)S(1)}, u32[]{:S(2)}, u32[]{:S(2)}) async-start(bf16[32,32,128]{2,1,0:T(8,128)(2,1)} %get-tuple-element.23), calls=%async_computation.2 | async-start | bytes 524288 | tf_op jit(solution)/shard_map/all_to_all | solution.py:467
  75.9 0.8 copy-done.8
  76.6 10.0 %back_conv.1 = bf16[2,2048,128]{2,1,0:T(8,128)(2,1)} custom-call(s32[1]{0:T(128)} %bitcast.core_ref.later.at_ref, bf16[2048,128]{1,0:T(8,128)(2,1)} %copy-done.5, bf16[2048,128]{1,0:T(8,128)(2,1)} %copy-done.6, bf16[2048,128]{1,0:T(8,128)(2,1)} %collective-permute-done.2.near_halo, bf16[2048,128]{1,0:T(8,128)(2,1)} %copy-done.8, bf16[3456,128]{1,0:T(8,128)(2,1)} %weight.7, ...), custom_call_target="tpu_custom_call" | custom-call | flops 4831838208 | bytes 5242880 | tf_op jit(solution)/shard_map/back_conv/pallas_call | solution.py:321
  86.6 0.8 first_rows.1
  (20 shorter events, 0.2 us)
Async XLA Ops:
  2.8 12.1 %collective-permute-start = (bf16[2048,128]{1,0:T(8,128)(2,1)}, bf16[2048,128]{1,0:T(8,128)(2,1)S(1)}, u32[]{:S(2)}, u32[]{:S(2)}) collective-permute-start(bf16[2048,128]{1,0:T(8,128)(2,1)} %get-tuple-element.13), channel_id=1, source_target_pairs={{0,4},{4,0},{1,5},{5,1},{2,6},{6,2},{3,7},{7,3},{8,12},{12,8},{9,1... | collective-permute-start | bytes 1572872 | tf_op jit(solution)/shard_map/ppermute | solution.py:438
  6.2 14.9 %collective-permute-start.1 = (bf16[2048,128]{1,0:T(8,128)(2,1)}, bf16[2048,128]{1,0:T(8,128)(2,1)S(1)}, u32[]{:S(2)}, u32[]{:S(2)}) collective-permute-start(bf16[2048,128]{1,0:T(8,128)(2,1)} %get-tuple-element.16), channel_id=1, source_target_pairs={{4,8},{12,16},{20,24},{28,32},{36,40},{44,48},{52,56},{60,64},{68,... | collective-permute-start | bytes 1572872 | tf_op jit(solution)/shard_map/ppermute | solution.py:437
  8.1 1.2 %copy-start.1 = (bf16[3456,128]{1,0:T(8,128)(2,1)S(1)}, bf16[3456,128]{1,0:T(8,128)(2,1)}, u32[]{:S(2)}) copy-start(bf16[3456,128]{1,0:T(8,128)(2,1)} %weight.7) | copy-start | bytes 2654212
  9.2 1.2 %copy-start.2 = (bf16[1,2,32,64,128]{4,3,2,1,0:T(8,128)(2,1)S(1)}, bf16[1,2,32,64,128]{4,3,2,1,0:T(8,128)(2,1)}, u32[]{:S(2)}) copy-start(bf16[1,2,32,64,128]{4,3,2,1,0:T(8,128)(2,1)} %param.5) | copy-start | bytes 3145732
  10.5 4.5 %copy-start = (bf16[1,2,32,64,128]{4,3,2,1,0:T(8,128)(2,1)S(1)}, bf16[1,2,32,64,128]{4,3,2,1,0:T(8,128)(2,1)}, u32[]{:S(2)}) copy-start(bf16[1,2,32,64,128]{4,3,2,1,0:T(8,128)(2,1)} %param.6) | copy-start | bytes 3145732
  17.5 26.6 %copy-start.5 = (bf16[2048,128]{1,0:T(8,128)(2,1)}, bf16[2048,128]{1,0:T(8,128)(2,1)S(1)}, u32[]{:S(2)}) copy-start(bf16[2048,128]{1,0:T(8,128)(2,1)S(1)} %get-tuple-element.15.near) | copy-start | bytes 1572868
  23.9 16.5 %copy-start.6 = (bf16[2048,128]{1,0:T(8,128)(2,1)}, bf16[2048,128]{1,0:T(8,128)(2,1)S(1)}, u32[]{:S(2)}) copy-start(bf16[2048,128]{1,0:T(8,128)(2,1)S(1)} %get-tuple-element.18.far) | copy-start | bytes 1572868
  30.7 36.0 %copy-start.3 = (f32[864,128]{1,0:T(8,128)S(1)}, f32[864,128]{1,0:T(8,128)}, u32[]{:S(2)}) copy-start(f32[864,128]{1,0:T(8,128)} %first.1) | copy-start | bytes 1327108
  30.7 36.0 %copy-start.4 = (f32[864,128]{1,0:T(8,128)S(1)}, f32[864,128]{1,0:T(8,128)}, u32[]{:S(2)}) copy-start(f32[864,128]{1,0:T(8,128)} %second.1) | copy-start | bytes 1327108
  30.7 2.0 %collective-permute-start.4 = (bf16[64,32,128]{2,1,0:T(8,128)(2,1)S(1)}, bf16[64,32,128]{2,1,0:T(8,128)(2,1)S(1)}, u32[]{:S(2)}, u32[]{:S(2)}) collective-permute-start(bf16[64,32,128]{2,1,0:T(8,128)(2,1)S(1)} %get-tuple-element.21), channel_id=1, source_target_pairs={{0,4},{4,0},{1,5},{5,1},{2,6},{6,2},{3,7},{7,3},{8,12},{12,8},{9,1... | collective-permute-start | bytes 1572872 | tf_op jit(solution)/shard_map/ppermute | solution.py:458
  33.7 17.5 %all-to-all-start = ((bf16[16,4,32,128]{3,2,1,0:T(8,128)(2,1)}), bf16[16,4,32,128]{3,2,1,0:T(8,128)(2,1)S(1)}, u32[]{:S(2)}, u32[]{:S(2)}) async-start(bf16[16,4,32,128]{3,2,1,0:T(8,128)(2,1)} %bitcast.5), calls=%async_computation | async-start | bytes 1048576 | tf_op jit(solution)/shard_map/all_to_all | solution.py:460
  40.4 35.4 %collective-permute-start.3 = (bf16[2048,128]{1,0:T(8,128)(2,1)S(1)}, bf16[2048,128]{1,0:T(8,128)(2,1)S(1)}, u32[]{:S(2)}, u32[]{:S(2)}) collective-permute-start(bf16[2048,128]{1,0:T(8,128)(2,1)S(1)} %get-tuple-element.18.far), channel_id=1, source_target_pairs={{4,8},{12,16},{20,24},{28,32},{36,40},{44,48},{52,56},{60,64},{68,... | collective-permute-start | bytes 1572872 | tf_op jit(solution)/shard_map/ppermute | solution.py:437
  44.1 31.8 %collective-permute-start.2 = (bf16[2048,128]{1,0:T(8,128)(2,1)S(1)}, bf16[2048,128]{1,0:T(8,128)(2,1)}, u32[]{:S(2)}, u32[]{:S(2)}) collective-permute-start(bf16[2048,128]{1,0:T(8,128)(2,1)S(1)} %get-tuple-element.15.near), channel_id=1, source_target_pairs={{0,4},{4,0},{1,5},{5,1},{2,6},{6,2},{3,7},{7,3},{8,12},{12,8},{9,1... | collective-permute-start | bytes 1572872 | tf_op jit(solution)/shard_map/ppermute | solution.py:438
  51.9 14.8 %all-to-all-start.1 = ((bf16[8,32,128]{2,1,0:T(8,128)(2,1)}), bf16[8,32,128]{2,1,0:T(8,128)(2,1)S(1)}, u32[]{:S(2)}, u32[]{:S(2)}) async-start(bf16[8,32,128]{2,1,0:T(8,128)(2,1)} %mixed_rows.1), calls=%async_computation.1 | async-start | bytes 131072 | tf_op jit(solution)/shard_map/all_to_all | solution.py:463
  67.5 0.6 copy-start.7
  68.0 18.6 %all-to-all-start.2 = ((bf16[32,32,128]{2,1,0:T(8,128)(2,1)}), bf16[32,32,128]{2,1,0:T(8,128)(2,1)S(1)}, u32[]{:S(2)}, u32[]{:S(2)}) async-start(bf16[32,32,128]{2,1,0:T(8,128)(2,1)} %get-tuple-element.23), calls=%async_computation.2 | async-start | bytes 524288 | tf_op jit(solution)/shard_map/all_to_all | solution.py:467
  75.8 0.8 copy-start.8

commit v4 on v2

--- a/solution.py
+++ b/solution.py
@@ -31,6 +31,7 @@
 SMEM = pl.BlockSpec(memory_space=pltpu.SMEM)
 FLAG = jax.ShapeDtypeStruct((8, C), F32)
 WHOLE = pltpu.CompilerParams(vmem_limit_bytes=60 * 1024 * 1024)
+LARGE = pltpu.CompilerParams(vmem_limit_bytes=62 * 1024 * 1024)
 SMALL = pltpu.CompilerParams(vmem_limit_bytes=4 * 1024 * 1024)
 PARAMS = pltpu.CompilerParams(vmem_limit_bytes=32 * 1024 * 1024)
 
@@ -262,10 +263,10 @@
 
 
 def inner_back_kernel(
-    core_ref, near, far, weight, upstream, later, out, ended, field, mixed, held, sem
+    core_ref, near, far, weight, later, out, ended, field, mixed, held, made, sem, sems
 ):
     copy = fetched(weight, held, sem)
-    ended[...] = jnp.zeros_like(ended)
+    ended[0] = 0
     shifted_columns(ordered(core_ref[0], near, far), field, 0, False)
     copy.wait()
     for b in range(3):
@@ -277,10 +278,16 @@
                     mixed[z * C : (z + 1) * C, base + p * C : base + (p + 1) * C] = (
                         held[t * C : (t + 1) * C, :]
                     )
+    tiles = CELLS // TILE
+
+    def leave(i, z):
+        rows = pl.ds(pl.multiple_of(i * TILE, TILE), TILE)
+        return pltpu.make_async_copy(
+            made.at[z, rows, :], out.at[z, rows, :], sems.at[i, z]
+        )
 
     def tile(i, carry):
         at = pl.multiple_of(i * TILE, TILE)
-        rows = pl.ds(at, TILE)
         got = lax.dot_general(
             taps_of(field, at, TILE),
             mixed[...],
@@ -288,40 +295,45 @@
             preferred_element_type=F32,
         )
         for z in range(2):
-            out[z, rows, :] = (
-                upstream[z, rows, :].astype(F32) + got[:, z * C : (z + 1) * C]
-            )
-        return carry
-
-    lax.fori_loop(0, CELLS // TILE, tile, 0)
-
-
-def inner_back(core, near, far, weight, upstream, later):
+            made[z, pl.ds(at, TILE), :] = got[:, z * C : (z + 1) * C]
+            leave(i, z).start()
+        return carry
+
+    lax.fori_loop(0, tiles, tile, 0)
+    for i in range(tiles):
+        for z in range(2):
+            leave(i, z).wait()
+
+
+def inner_back(core, near, far, weight, later):
     return pl.pallas_call(
         inner_back_kernel,
         out_shape=[
             jax.ShapeDtypeStruct((2, CELLS, C), F32),
-            FLAG,
-        ],
-        in_specs=[SMEM, VMEM, VMEM, HBM, VMEM, ANY],
-        out_specs=[VMEM, VMEM],
+            jax.ShapeDtypeStruct((1,), jnp.int32),
+        ],
+        in_specs=[SMEM, VMEM, VMEM, HBM, ANY],
+        out_specs=[HBM, SMEM],
         scratch_shapes=[
             pltpu.VMEM((3, PADDED, 2 * C), BF),
             pltpu.VMEM((2 * C, 9 * 256), BF),
             pltpu.VMEM((27 * C, C), BF),
+            pltpu.VMEM((2, CELLS, C), F32),
             pltpu.SemaphoreType.DMA,
+            pltpu.SemaphoreType.DMA((CELLS // TILE, 2)),
         ],
         compiler_params=WHOLE,
         cost_estimate=cost(2 * CELLS * 2304 * 256, 5 << 20),
         name="inner_back",
-    )(core, near, far, weight, upstream, later)
+    )(core, near, far, weight, later)
 
 
 def outer_back_kernel(
-    core_ref, near, far, weight, kept, out, field, mixed, held, inner, sem, kept_sem
+    core_ref, near, far, weight, given, kept, out, field, mixed, held, upstream, inner, sems
 ):
-    copy = fetched(weight, held, sem)
-    kept_copy = fetched(kept, inner, kept_sem)
+    copy = fetched(weight, held, sems.at[0])
+    kept_copy = fetched(kept, inner, sems.at[1])
+    given_copy = fetched(given, upstream, sems.at[2])
     core = core_ref[0]
     shifted_columns([rows_of(near), rows_of(far)], field, 0, False)
     copy.wait()
@@ -334,8 +346,8 @@
                 mixed[k, :, base : base + C] = held[
                     pl.ds(first + tap(0, 2 - b, 2 - c) * C, C), :
                 ]
-
     kept_copy.wait()
+    given_copy.wait()
 
     def tile(i, carry):
         at = pl.multiple_of(i * TILE, TILE)
@@ -357,49 +369,54 @@
             got = lax.dot_general(
                 lhs, mixed[k], (((1,), (1,)), ((), ())), preferred_element_type=F32
             )
-            out[z, rows, :] = (inner[z, rows, :] + got).astype(BF)
+            out[z, rows, :] = (
+                upstream[z, rows, :].astype(F32) + (inner[z, rows, :] + got)
+            ).astype(BF)
         return carry
 
     lax.fori_loop(0, CELLS // TILE, tile, 0)
 
 
-def outer_back(core, near, far, weight, inner):
+def outer_back(core, near, far, weight, given, inner):
     return pl.pallas_call(
         outer_back_kernel,
         out_shape=jax.ShapeDtypeStruct((2, CELLS, C), BF),
-        in_specs=[SMEM, VMEM, VMEM, HBM, HBM],
+        in_specs=[SMEM, VMEM, VMEM, HBM, HBM, HBM],
         out_specs=VMEM,
         scratch_shapes=[
             pltpu.VMEM((3, PADDED, 2 * C), BF),
             pltpu.VMEM((2, C, 9 * C), BF),
             pltpu.VMEM((27 * C, C), BF),
+            pltpu.VMEM((2, CELLS, C), BF),
             pltpu.VMEM((2, CELLS, C), F32),
-            pltpu.SemaphoreType.DMA,
-            pltpu.SemaphoreType.DMA,
-        ],
-        compiler_params=WHOLE,
+            pltpu.SemaphoreType.DMA((3,)),
+        ],
+        compiler_params=LARGE,
         cost_estimate=cost(2 * CELLS * 2304 * 256, 5 << 20),
         name="outer_back",
-    )(core, near, far, weight, inner)
-
-
-def plane_kernel(at_ref, vol, later, plane, ended, sem):
-    copy = fetched(vol.at[at_ref[0]], plane, sem)
-    ended[...] = jnp.zeros_like(ended)
-    copy.wait()
-
-
-def one_plane(name, at, vol, later):
-    return pl.pallas_call(
-        plane_kernel,
-        out_shape=[jax.ShapeDtypeStruct((CELLS, C), BF), FLAG],
-        in_specs=[SMEM, HBM, ANY],
-        out_specs=[HBM, VMEM],
-        scratch_shapes=[pltpu.SemaphoreType.DMA],
-        compiler_params=WHOLE,
-        cost_estimate=cost(0, 1 << 20),
-        name=name,
-    )(at, vol, later)
+    )(core, near, far, weight, given, inner)
+
+
+def planes_kernel(core_ref, vol, near, far, sems):
+    core = core_ref[0]
+    first = fetched(vol.at[core], far, sems.at[0])
+    second = fetched(vol.at[1 - core], near, sems.at[1])
+    first.wait()
+    second.wait()
+
+
+def both_planes(core, vol):
+    plane = jax.ShapeDtypeStruct((CELLS, C), BF)
+    return pl.pallas_call(
+        planes_kernel,
+        out_shape=[plane, plane],
+        in_specs=[SMEM, HBM],
+        out_specs=[HBM, HBM],
+        scratch_shapes=[pltpu.SemaphoreType.DMA((2,))],
+        compiler_params=SMALL,
+        cost_estimate=cost(0, 2 << 20),
+        name="both_planes",
+    )(core, vol)
 
 
 def first_rows_kernel(whole, out):
@@ -423,15 +440,15 @@
         total = got[0, group].astype(F32)
         for k in range(1, 16):
             total += got[k, group].astype(F32)
-        out[group] = total
-        out[4 + group] = total
+        out[group] = total.astype(BF)
+        out[4 + group] = total.astype(BF)
 
 
 def mixed_rows(got, later):
     return pl.pallas_call(
         mix_kernel,
-        out_shape=jax.ShapeDtypeStruct((8, CHUNK, C), F32),
-        in_specs=[VMEM, ANY],
+        out_shape=jax.ShapeDtypeStruct((8, CHUNK, C), BF),
+        in_specs=[VMEM, SMEM],
         out_specs=VMEM,
         compiler_params=SMALL,
         cost_estimate=cost(1 << 18, 1 << 20),
@@ -440,9 +457,9 @@
 
 
 def step_kernel(at_ref, got, first, second, out):
-    total = got[0]
+    total = got[0].astype(F32)
     for k in range(1, 8):
-        total += got[k]
+        total += got[k].astype(F32)
     at = pl.multiple_of(at_ref[0], CHUNK)
     rows = pl.ds(at, CHUNK)
     step = adam(total, first[rows, :], second[rows, :])
@@ -486,9 +503,7 @@
     up = upstream.reshape(2, CELLS, C)
     core = lax.axis_index("core")
     at_core, at_near = core.reshape(1), (1 - core).reshape(1)
-    far_plane, ended = one_plane("far_plane", at_core, vol, at_core)
-    near_plane, ended = one_plane("near_plane", at_near, vol, ended)
-    near_halo, far_halo = from_neighbours(near_plane, far_plane)
+    near_halo, far_halo = from_neighbours(*both_planes(at_core, vol))
     inner, vol_t = inner_conv(vol, weight)
     near, ended = outer_conv(
         "near_conv", at_near, near_halo, weight, inner, up, at_core
@@ -503,14 +518,14 @@
     half = (kept + other.astype(F32)).astype(BF).reshape(16, 4, CHUNK, C)
     got = lax.all_to_all(half, ("x", "y"), 0, 0)
     grad_near, grad_far = from_neighbours(near, far)
-    local, ended = inner_back(at_core, near, far, weight, up, half)
+    local, ended = inner_back(at_core, near, far, weight, half)
     part = mixed_rows(got, ended)
     got = lax.all_to_all(part, ("zl", "sample"), 0, 0)
     owner = core * 16 + lax.axis_index("x") * 4 + lax.axis_index("y")
     at = jnp.minimum(owner * CHUNK, rows - CHUNK).reshape(1)
     step = spread_step(at, got, first_moment, second_moment)
     whole = lax.all_to_all(step, ("core", "x", "y"), 0, 0)
-    grad_volume = outer_back(at_core, grad_near, grad_far, weight, local)
+    grad_volume = outer_back(at_core, grad_near, grad_far, weight, up, local)
     direction = first_rows(whole.reshape(OWNERS * CHUNK, C), rows)
     return (grad_volume.reshape(volume.shape), direction)
 

time: 121 us -> 87.5 us (0.72)
  Pallas kernels: 68.7 us -> 34.9 us
  waiting for transfers between devices: 15.6 us -> 13.6 us
  local copies, waits for them, and re-layouts: 1.69 us -> 3.64 us
    pallas_call x2 -> x1, Pallas kernels: 35.2 us -> 0.81 us  [both_planes(): pl.pallas_call(planes_kernel, out_shape=[plane, plane], in_specs=[SMEM, H...]
    ppermute x2, waiting for transfers between devices: 5.97 us -> 3.59 us  [from_neighbours(): far_halo = lax.ppermute(far, SPACE, pairs + [(j, i) for i, j in pairs])]
    unnamed x22 -> x18, local copies, waits for them, and re-layouts: 1.69 us -> 3.64 us
  transfers between devices with their start and end apart: 8 -> 8, of which waited for: 4 -> 4; matrix products, arithmetic and copies ran while one was open for 0% -> 0% of each run, Pallas kernels for 19% -> 27%
where the time goes in v4:
time: 87.5 us; the launch traced here: 86.8 us
  Pallas kernels  34.9 us (40%)
  starting transfers between devices  32.9 us (38%)
  waiting for transfers between devices  13.6 us (16%)
  local copies, waits for them, and re-layouts  3.64 us (4%)
  other arithmetic  0.97 us (1%)
    all_to_all x1, starting transfers between devices, body(): got = lax.all_to_all(part, ('zl', 'sample'), 0, 0)  8.67 us
    all_to_all x1, starting transfers between devices, body(): whole = lax.all_to_all(step, ('core', 'x', 'y'), 0, 0)  8.33 us
    pallas_call x1, Pallas kernels, outer_back(): pl.pallas_call(outer_back_kernel, out_shape=jax.ShapeDtypeStruct((2, CELL...  7.44 us
    pallas_call x1, Pallas kernels, inner_back(): pl.pallas_call(inner_back_kernel, out_shape=[jax.ShapeDtypeStruct((2, CEL...  7.22 us
    pallas_call x1, Pallas kernels, kernel_gradient(): pl.pallas_call(taps_kernel, out_shape=[jax.ShapeDtypeStruct((64, CHUNK, C...  6.78 us
    all_to_all x1, waiting for transfers between devices, body(): got = lax.all_to_all(part, ('zl', 'sample'), 0, 0)  6.73 us
    all_to_all x1, starting transfers between devices, body(): got = lax.all_to_all(half, ('x', 'y'), 0, 0)  6.72 us
    ppermute x2, starting transfers between devices, from_neighbours(): far_halo = lax.ppermute(far, SPACE, pairs + [(j, i) for i, j in pairs])  5.65 us
  transfers between devices with their start and end apart: 8, of which 4 were waited for; matrix products, arithmetic and copies ran while one was open for 0% of the time, Pallas kernels for 27%

profile of v4, /device:TPU:1, one launch (start us, length us, event | category | flops | bytes accessed | tf_op | source)
XLA Modules:
  0.0 86.8 jit_solution(7032441323822941232)
XLA Ops:
  0.6 1.2 %copy-done.2 = bf16[1,2,32,64,128]{4,3,2,1,0:T(8,128)(2,1)S(1)} copy-done((bf16[1,2,32,64,128]{4,3,2,1,0:T(8,128)(2,1)S(1)}, bf16[1,2,32,64,128]{4,3,2,1,0:T(8,128)(2,1)}, u32[]{:S(2)}) %copy-start.2) | copy-done | bytes 1048600
  1.9 0.8 both_planes.1
  2.7 3.3 %collective-permute-start = (bf16[2048,128]{1,0:T(8,128)(2,1)S(1)}, bf16[2048,128]{1,0:T(8,128)(2,1)S(1)}, u32[]{:S(2)}, u32[]{:S(2)}) collective-permute-start(bf16[2048,128]{1,0:T(8,128)(2,1)S(1)} %get-tuple-element.13), channel_id=1, source_target_pairs={{0,4},{4,0},{1,5},{5,1},{2,6},{6,2},{3,7},{7,3},{8,12},{12,8},{9,1... | collective-permute-start | bytes 1572872 | tf_op jit(solution)/shard_map/ppermute | solution.py:497
  6.0 1.9 %collective-permute-start.2 = (bf16[2048,128]{1,0:T(8,128)(2,1)}, bf16[2048,128]{1,0:T(8,128)(2,1)S(1)}, u32[]{:S(2)}, u32[]{:S(2)}) collective-permute-start(bf16[2048,128]{1,0:T(8,128)(2,1)} %get-tuple-element.16), channel_id=1, source_target_pairs={{4,8},{12,16},{20,24},{28,32},{36,40},{44,48},{52,56},{60,64},{68,... | collective-permute-start | bytes 1572872 | tf_op jit(solution)/shard_map/ppermute | solution.py:496
  7.9 1.2 %copy-done.1 = bf16[3456,128]{1,0:T(8,128)(2,1)S(1)} copy-done((bf16[3456,128]{1,0:T(8,128)(2,1)S(1)}, bf16[3456,128]{1,0:T(8,128)(2,1)}, u32[]{:S(2)}) %copy-start.1) | copy-done | bytes 884760
  9.1 1.2 %copy-done.3 = bf16[1,2,32,64,128]{4,3,2,1,0:T(8,128)(2,1)S(1)} copy-done((bf16[1,2,32,64,128]{4,3,2,1,0:T(8,128)(2,1)S(1)}, bf16[1,2,32,64,128]{4,3,2,1,0:T(8,128)(2,1)}, u32[]{:S(2)}) %copy-start.3) | copy-done | bytes 1048600
  10.3 4.5 %inner_conv.1 = (f32[2,2048,128]{2,1,0:T(8,128)S(1)}, bf16[256,2048]{1,0:T(8,128)(2,1)S(1)}) custom-call(bf16[2,2048,128]{2,1,0:T(8,128)(2,1)S(1)} %bitcast.12, bf16[3456,128]{1,0:T(8,128)(2,1)S(1)} %copy-done.1), custom_call_target="tpu_custom_call" | custom-call | flops 2415919104 | bytes 5242880 | tf_op jit(solution)/shard_map/inner_conv/pallas_call | solution.py:139
  14.8 2.5 %near_conv.1 = (bf16[2048,128]{1,0:T(8,128)(2,1)S(1)}, f32[8,128]{1,0:T(8,128)S(1)}) custom-call(s32[1]{0:T(128)} %bitcast.1.at_ref, bf16[2048,128]{1,0:T(8,128)(2,1)S(1)} %collective-permute-done.halo.near_halo, bf16[3456,128]{1,0:T(8,128)(2,1)S(1)} %copy-done.1, f32[2,2048,128]{2,1,0:T(8,128)S(1)} %get-tuple-element.14.inner, ...), custom_call_target="tpu_custom_call" | custom-call | flops 1207959552 | bytes 3145728 | tf_op jit(solution)/shard_map/near_conv/pallas_call | solution.py:184
  17.4 3.6 %collective-permute-done.2.halo.far_halo = bf16[2048,128]{1,0:T(8,128)(2,1)S(1)} collective-permute-done((bf16[2048,128]{1,0:T(8,128)(2,1)}, bf16[2048,128]{1,0:T(8,128)(2,1)S(1)}, u32[]{:S(2)}, u32[]{:S(2)}) %collective-permute-start.2) | collective-permute-done | bytes 524320 | tf_op jit(solution)/shard_map/ppermute | solution.py:496
  20.9 2.8 %far_conv.1 = (bf16[2048,128]{1,0:T(8,128)(2,1)S(1)}, f32[8,128]{1,0:T(8,128)}) custom-call(s32[1]{0:T(128)} %bitcast.core_ref.later.at_ref, bf16[2048,128]{1,0:T(8,128)(2,1)S(1)} %collective-permute-done.2.halo.far_halo, bf16[3456,128]{1,0:T(8,128)(2,1)S(1)} %copy-done.1, f32[2,2048,128]{2,1,0:T(8,128)S(1)} %get-tuple-element.14.inner, ...), custom_call_target="tpu_custom_call" | custom-call | flops 1207959552 | bytes 3145728 | tf_op jit(solution)/shard_map/far_conv/pallas_call | solution.py:184
  23.8 6.8 %kernel_gradient.1 = (f32[64,32,128]{2,1,0:T(8,128)S(1)}, bf16[64,32,128]{2,1,0:T(8,128)(2,1)S(1)}) custom-call(s32[1]{0:T(128)} %bitcast.core_ref.later.at_ref, bf16[2048,128]{1,0:T(8,128)(2,1)S(1)} %get-tuple-element.15.near, bf16[2048,128]{1,0:T(8,128)(2,1)S(1)} %get-tuple-element.18.far, bf16[2048,128]{1,0:T(8,128)(2,1)S(1)} %collective-permute-done.halo.near_halo, ...), custom_call_target="tpu_custom_call" | custom-call | flops 4831838208 | bytes 5242880 | tf_op jit(solution)/shard_map/kernel_gradient/pallas_call | solution.py:246
  30.7 1.9 %collective-permute-done.4 = bf16[64,32,128]{2,1,0:T(8,128)(2,1)S(1)} collective-permute-done((bf16[64,32,128]{2,1,0:T(8,128)(2,1)S(1)}, bf16[64,32,128]{2,1,0:T(8,128)(2,1)S(1)}, u32[]{:S(2)}, u32[]{:S(2)}) %collective-permute-start.4) | collective-permute-done | bytes 524320 | tf_op jit(solution)/shard_map/ppermute | solution.py:517
  32.6 1.0 %add_convert_fusion = bf16[64,32,128]{2,1,0:T(8,128)(2,1)} fusion(f32[64,32,128]{2,1,0:T(8,128)S(1)} %get-tuple-element.20, bf16[64,32,128]{2,1,0:T(8,128)(2,1)S(1)} %collective-permute-done.4), kind=kLoop, calls=%fused_computation | loop fusion | flops 786432 | bytes 2097152 | tf_op jit(solution)/shard_map/convert_element_type | solution.py:518
  33.5 6.7 %all-to-all-start = ((bf16[16,4,32,128]{3,2,1,0:T(8,128)(2,1)}), bf16[16,4,32,128]{3,2,1,0:T(8,128)(2,1)S(1)}, u32[]{:S(2)}, u32[]{:S(2)}) async-start(bf16[16,4,32,128]{3,2,1,0:T(8,128)(2,1)} %bitcast.4.later), calls=%async_computation | async-start | bytes 1048576 | tf_op jit(solution)/shard_map/all_to_all | solution.py:519
  40.3 3.7 %collective-permute-start.3 = (bf16[2048,128]{1,0:T(8,128)(2,1)S(1)}, bf16[2048,128]{1,0:T(8,128)(2,1)}, u32[]{:S(2)}, u32[]{:S(2)}) collective-permute-start(bf16[2048,128]{1,0:T(8,128)(2,1)S(1)} %copy-done.8), channel_id=1, source_target_pairs={{4,8},{12,16},{20,24},{28,32},{36,40},{44,48},{52,56},{60,64},{68,... | collective-permute-start | bytes 1572872 | tf_op jit(solution)/shard_map/ppermute | solution.py:496
  44.2 7.2 %inner_back.1 = (f32[2,2048,128]{2,1,0:T(8,128)}, s32[1]{0:T(128)}) custom-call(s32[1]{0:T(128)} %bitcast.core_ref.later.at_ref, bf16[2048,128]{1,0:T(8,128)(2,1)} %copy-done.6, bf16[2048,128]{1,0:T(8,128)(2,1)} %copy-done.7, bf16[3456,128]{1,0:T(8,128)(2,1)} %weight.9, bf16[16,4,32,128]{3,2,1,0:T(8,128)(2,1)} %bitcast.4.later), custom_call_target="tpu_custom_call" | custom-call | flops 2415919104 | bytes 5242880 | tf_op jit(solution)/shard_map/inner_back/pallas_call | solution.py:309
  51.4 1.3 %mixed_rows.1 = bf16[8,32,128]{2,1,0:T(8,128)(2,1)} custom-call(bf16[16,4,32,128]{3,2,1,0:T(8,128)(2,1)S(1)} %all-to-all-done.got, s32[1]{0:T(128)} %get-tuple-element.23.later), custom_call_target="tpu_custom_call" | custom-call | flops 262144 | bytes 1048576 | tf_op jit(solution)/shard_map/mixed_rows/pallas_call | solution.py:448
  52.7 8.7 %all-to-all-start.1 = ((bf16[8,32,128]{2,1,0:T(8,128)(2,1)}), bf16[8,32,128]{2,1,0:T(8,128)(2,1)S(1)}, u32[]{:S(2)}, u32[]{:S(2)}) async-start(bf16[8,32,128]{2,1,0:T(8,128)(2,1)} %mixed_rows.1), calls=%async_computation.1 | async-start | bytes 131072 | tf_op jit(solution)/shard_map/all_to_all | solution.py:523
  61.4 6.7 %all-to-all-done.1.got = bf16[8,32,128]{2,1,0:T(8,128)(2,1)S(1)} async-done(((bf16[8,32,128]{2,1,0:T(8,128)(2,1)}), bf16[8,32,128]{2,1,0:T(8,128)(2,1)S(1)}, u32[]{:S(2)}, u32[]{:S(2)}) %all-to-all-start.1) | async-done | bytes 65568 | tf_op jit(solution)/shard_map/all_to_all | solution.py:523
  68.1 0.8 spread_step.1
  68.9 8.3 %all-to-all-start.2 = ((bf16[32,32,128]{2,1,0:T(8,128)(2,1)}), bf16[32,32,128]{2,1,0:T(8,128)(2,1)S(1)}, u32[]{:S(2)}, u32[]{:S(2)}) async-start(bf16[32,32,128]{2,1,0:T(8,128)(2,1)} %spread_step.1), calls=%async_computation.2 | async-start | bytes 524288 | tf_op jit(solution)/shard_map/all_to_all | solution.py:527
  77.2 7.4 %outer_back.1 = bf16[2,2048,128]{2,1,0:T(8,128)(2,1)} custom-call(s32[1]{0:T(128)} %bitcast.core_ref.later.at_ref, bf16[2048,128]{1,0:T(8,128)(2,1)} %collective-permute-done.1.near, bf16[2048,128]{1,0:T(8,128)(2,1)} %collective-permute-done.3.far, bf16[3456,128]{1,0:T(8,128)(2,1)} %weight.9, bf16[2,2048,128]{2,1,0:T(8,128)(2,1)} %bitcast.8, ...), custom_call_target="tpu_custom_call" | custom-call | flops 2415919104 | bytes 5242880 | tf_op jit(solution)/shard_map/outer_back/pallas_call | solution.py:381
  84.7 1.4 %all-to-all-done.2 = bf16[32,32,128]{2,1,0:T(8,128)(2,1)S(1)} async-done(((bf16[32,32,128]{2,1,0:T(8,128)(2,1)}), bf16[32,32,128]{2,1,0:T(8,128)(2,1)S(1)}, u32[]{:S(2)}, u32[]{:S(2)}) %all-to-all-start.2) | async-done | bytes 262176 | tf_op jit(solution)/shard_map/all_to_all | solution.py:527
  86.0 0.8 first_rows.1
  (21 shorter events, 0.2 us)
Async XLA Ops:
  0.6 1.2 %copy-start.2 = (bf16[1,2,32,64,128]{4,3,2,1,0:T(8,128)(2,1)S(1)}, bf16[1,2,32,64,128]{4,3,2,1,0:T(8,128)(2,1)}, u32[]{:S(2)}) copy-start(bf16[1,2,32,64,128]{4,3,2,1,0:T(8,128)(2,1)} %param.5) | copy-start | bytes 3145732
  2.7 12.1 %collective-permute-start = (bf16[2048,128]{1,0:T(8,128)(2,1)S(1)}, bf16[2048,128]{1,0:T(8,128)(2,1)S(1)}, u32[]{:S(2)}, u32[]{:S(2)}) collective-permute-start(bf16[2048,128]{1,0:T(8,128)(2,1)S(1)} %get-tuple-element.13), channel_id=1, source_target_pairs={{0,4},{4,0},{1,5},{5,1},{2,6},{6,2},{3,7},{7,3},{8,12},{12,8},{9,1... | collective-permute-start | bytes 1572872 | tf_op jit(solution)/shard_map/ppermute | solution.py:497
  6.0 14.9 %collective-permute-start.2 = (bf16[2048,128]{1,0:T(8,128)(2,1)}, bf16[2048,128]{1,0:T(8,128)(2,1)S(1)}, u32[]{:S(2)}, u32[]{:S(2)}) collective-permute-start(bf16[2048,128]{1,0:T(8,128)(2,1)} %get-tuple-element.16), channel_id=1, source_target_pairs={{4,8},{12,16},{20,24},{28,32},{36,40},{44,48},{52,56},{60,64},{68,... | collective-permute-start | bytes 1572872 | tf_op jit(solution)/shard_map/ppermute | solution.py:496
  7.9 1.2 %copy-start.1 = (bf16[3456,128]{1,0:T(8,128)(2,1)S(1)}, bf16[3456,128]{1,0:T(8,128)(2,1)}, u32[]{:S(2)}) copy-start(bf16[3456,128]{1,0:T(8,128)(2,1)} %weight.9) | copy-start | bytes 2654212
  9.1 1.2 %copy-start.3 = (bf16[1,2,32,64,128]{4,3,2,1,0:T(8,128)(2,1)S(1)}, bf16[1,2,32,64,128]{4,3,2,1,0:T(8,128)(2,1)}, u32[]{:S(2)}) copy-start(bf16[1,2,32,64,128]{4,3,2,1,0:T(8,128)(2,1)} %param.5) | copy-start | bytes 3145732
  10.3 4.5 %copy-start = (bf16[1,2,32,64,128]{4,3,2,1,0:T(8,128)(2,1)S(1)}, bf16[1,2,32,64,128]{4,3,2,1,0:T(8,128)(2,1)}, u32[]{:S(2)}) copy-start(bf16[1,2,32,64,128]{4,3,2,1,0:T(8,128)(2,1)} %param.6) | copy-start | bytes 3145732
  17.3 26.7 %copy-start.6 = (bf16[2048,128]{1,0:T(8,128)(2,1)}, bf16[2048,128]{1,0:T(8,128)(2,1)S(1)}, u32[]{:S(2)}) copy-start(bf16[2048,128]{1,0:T(8,128)(2,1)S(1)} %get-tuple-element.15.near) | copy-start | bytes 1572868
  23.7 6.8 %copy-start.7 = (bf16[2048,128]{1,0:T(8,128)(2,1)}, bf16[2048,128]{1,0:T(8,128)(2,1)S(1)}, u32[]{:S(2)}) copy-start(bf16[2048,128]{1,0:T(8,128)(2,1)S(1)} %get-tuple-element.18.far) | copy-start | bytes 1572868
  30.6 9.7 %copy-start.8 = (bf16[2048,128]{1,0:T(8,128)(2,1)S(1)}, bf16[2048,128]{1,0:T(8,128)(2,1)}, u32[]{:S(2)}) copy-start(bf16[2048,128]{1,0:T(8,128)(2,1)} %copy-done.7) | copy-start | bytes 1572868
  30.6 2.0 %collective-permute-start.4 = (bf16[64,32,128]{2,1,0:T(8,128)(2,1)S(1)}, bf16[64,32,128]{2,1,0:T(8,128)(2,1)S(1)}, u32[]{:S(2)}, u32[]{:S(2)}) collective-permute-start(bf16[64,32,128]{2,1,0:T(8,128)(2,1)S(1)} %get-tuple-element.21), channel_id=1, source_target_pairs={{0,4},{4,0},{1,5},{5,1},{2,6},{6,2},{3,7},{7,3},{8,12},{12,8},{9,1... | collective-permute-start | bytes 1572872 | tf_op jit(solution)/shard_map/ppermute | solution.py:517
  33.5 17.9 %all-to-all-start = ((bf16[16,4,32,128]{3,2,1,0:T(8,128)(2,1)}), bf16[16,4,32,128]{3,2,1,0:T(8,128)(2,1)S(1)}, u32[]{:S(2)}, u32[]{:S(2)}) async-start(bf16[16,4,32,128]{3,2,1,0:T(8,128)(2,1)} %bitcast.4.later), calls=%async_computation | async-start | bytes 1048576 | tf_op jit(solution)/shard_map/all_to_all | solution.py:519
  40.3 27.9 %copy-start.4 = (f32[864,128]{1,0:T(8,128)S(1)}, f32[864,128]{1,0:T(8,128)}, u32[]{:S(2)}) copy-start(f32[864,128]{1,0:T(8,128)} %first.1) | copy-start | bytes 1327108
  40.3 27.9 %copy-start.5 = (f32[864,128]{1,0:T(8,128)S(1)}, f32[864,128]{1,0:T(8,128)}, u32[]{:S(2)}) copy-start(f32[864,128]{1,0:T(8,128)} %second.1) | copy-start | bytes 1327108
  40.3 36.9 %collective-permute-start.3 = (bf16[2048,128]{1,0:T(8,128)(2,1)S(1)}, bf16[2048,128]{1,0:T(8,128)(2,1)}, u32[]{:S(2)}, u32[]{:S(2)}) collective-permute-start(bf16[2048,128]{1,0:T(8,128)(2,1)S(1)} %copy-done.8), channel_id=1, source_target_pairs={{4,8},{12,16},{20,24},{28,32},{36,40},{44,48},{52,56},{60,64},{68,... | collective-permute-start | bytes 1572872 | tf_op jit(solution)/shard_map/ppermute | solution.py:496
  44.1 33.2 %collective-permute-start.1 = (bf16[2048,128]{1,0:T(8,128)(2,1)S(1)}, bf16[2048,128]{1,0:T(8,128)(2,1)}, u32[]{:S(2)}, u32[]{:S(2)}) collective-permute-start(bf16[2048,128]{1,0:T(8,128)(2,1)S(1)} %get-tuple-element.15.near), channel_id=1, source_target_pairs={{0,4},{4,0},{1,5},{5,1},{2,6},{6,2},{3,7},{7,3},{8,12},{12,8},{9,1... | collective-permute-start | bytes 1572872 | tf_op jit(solution)/shard_map/ppermute | solution.py:497
  52.7 15.4 %all-to-all-start.1 = ((bf16[8,32,128]{2,1,0:T(8,128)(2,1)}), bf16[8,32,128]{2,1,0:T(8,128)(2,1)S(1)}, u32[]{:S(2)}, u32[]{:S(2)}) async-start(bf16[8,32,128]{2,1,0:T(8,128)(2,1)} %mixed_rows.1), calls=%async_computation.1 | async-start | bytes 131072 | tf_op jit(solution)/shard_map/all_to_all | solution.py:523
  68.9 17.2 %all-to-all-start.2 = ((bf16[32,32,128]{2,1,0:T(8,128)(2,1)}), bf16[32,32,128]{2,1,0:T(8,128)(2,1)S(1)}, u32[]{:S(2)}, u32[]{:S(2)}) async-start(bf16[32,32,128]{2,1,0:T(8,128)(2,1)} %spread_step.1), calls=%async_computation.2 | async-start | bytes 524288 | tf_op jit(solution)/shard_map/all_to_all | solution.py:527

commit v5 on v4

--- a/solution.py
+++ b/solution.py
@@ -29,9 +29,8 @@
 ANY = pl.BlockSpec(memory_space=pl.ANY)
 HBM = pl.BlockSpec(memory_space=pltpu.HBM)
 SMEM = pl.BlockSpec(memory_space=pltpu.SMEM)
-FLAG = jax.ShapeDtypeStruct((8, C), F32)
 WHOLE = pltpu.CompilerParams(vmem_limit_bytes=60 * 1024 * 1024)
-LARGE = pltpu.CompilerParams(vmem_limit_bytes=62 * 1024 * 1024)
+LARGE = pltpu.CompilerParams(vmem_limit_bytes=62 * 1024 * 1024 + 512 * 1024)
 SMALL = pltpu.CompilerParams(vmem_limit_bytes=4 * 1024 * 1024)
 PARAMS = pltpu.CompilerParams(vmem_limit_bytes=32 * 1024 * 1024)
 
@@ -156,117 +155,137 @@
     )(vol, weight)
 
 
-def outer_kernel(
-    at_ref, halo, weight, inner, upstream, later, grad, ended, field, held, sem
-):
-    z = at_ref[0]
-    ended[...] = jnp.zeros_like(ended)
+def side(z, halo, weight, inner, upstream, vol_t, grad, part, field, held, shifts, turned, sem):
     first = pl.multiple_of(z * 18 * C, 18 * C)
     copy = fetched(weight.at[pl.ds(first, 9 * C), :], held, sem)
     shifted_columns([rows_of(halo)], field, 0, False)
+    transposed(rows_of(halo), turned, 0)
+    blank = jnp.zeros((COLS, C), BF)
+    for c in range(3):
+        shifts[c, 0:COLS, :] = blank
+        shifts[c, PADDED - COLS : PADDED, :] = blank
     copy.wait()
 
     def tile(i, carry):
         at = pl.multiple_of(i * TILE, TILE)
         rows = pl.ds(at, TILE)
+        to = pl.ds(pl.multiple_of(at + COLS, COLS), TILE)
         preact = inner[z, rows, :] + jnp.dot(
             taps_of(field, at, TILE), held[...], preferred_element_type=F32
         )
         s = jax.nn.sigmoid(preact)
         slopes = s * (1.0 + preact * (1.0 - s))
-        grad[rows, :] = (upstream[z, rows, :].astype(F32) * slopes).astype(BF)
+        here = (upstream[z, rows, :].astype(F32) * slopes).astype(BF)
+        grad[rows, :] = here
+        wide = here.astype(F32)
+        col = lax.broadcasted_iota(jnp.int32, (TILE, C), 0) & (COLS - 1)
+        shifts[1, to, :] = here
+        shifts[0, to, :] = jnp.where(col == 0, 0.0, pltpu.roll(wide, 1, 0)).astype(BF)
+        shifts[2, to, :] = jnp.where(
+            col == COLS - 1, 0.0, pltpu.roll(wide, TILE - 1, 0)
+        ).astype(BF)
         return carry
 
     lax.fori_loop(0, CELLS // TILE, tile, 0)
 
-
-def outer_conv(name, z, halo, weight, inner, upstream, later):
-    return pl.pallas_call(
-        outer_kernel,
-        out_shape=[jax.ShapeDtypeStruct((CELLS, C), BF), FLAG],
-        in_specs=[SMEM, VMEM, HBM, VMEM, VMEM, ANY],
-        out_specs=[VMEM, VMEM],
-        scratch_shapes=[
-            pltpu.VMEM((3, PADDED, C), BF),
-            pltpu.VMEM((9 * C, C), BF),
-            pltpu.SemaphoreType.DMA,
-        ],
-        compiler_params=PARAMS,
-        cost_estimate=cost(2 * CELLS * 1152 * 256, 3 << 20, CELLS * 128),
-        name=name,
-    )(z, halo, weight, inner, upstream, later)
-
-
-def taps_kernel(core_ref, near, far, near_halo, far_halo, vol_t, kept, sent, field, lhs, whole):
-    core = core_ref[0]
-    shifted_columns(ordered(core, near, far), field, 0, False)
-    before, after = ordered(core, near_halo, far_halo)
-    lhs[C : 3 * C, :] = vol_t[...]
-    transposed(before, lhs, 0)
-    transposed(after, lhs, 3 * C)
-
+    lhs = jnp.concatenate([vol_t[...], turned[...]], axis=0)
+    offset_of = (1 - z, 2 - z, 2 * z)
+    couples = [((b, 0), (b, 1)) for b in range(3)] + [((0, 2), (1, 2)), ((2, 2),)]
+    for couple in couples:
+        rhs = jnp.concatenate(
+            [
+                shifts[2 - c, (2 - b) * COLS : (2 - b) * COLS + CELLS, :]
+                for b, c in couple
+            ],
+            axis=1,
+        )
+        got = jnp.dot(lhs, rhs, preferred_element_type=F32)
+        for k, (b, c) in enumerate(couple):
+            for p in range(3):
+                for i in range(4):
+                    chunk = 4 * tap(offset_of[p], b, c) + i
+                    at = p * C + i * CHUNK
+                    part[chunk + 5 * (chunk // 27)] = got[
+                        at : at + CHUNK, k * C : (k + 1) * C
+                    ]
+
+
+def near_kernel(
+    core_ref, halo, weight, inner, upstream, vol_t, grad, part, *scratch
+):
+    side(
+        1 - core_ref[0], halo, weight, inner, upstream, vol_t, grad, part, *scratch
+    )
     for owner in range(27, 32):
         for group in range(4):
-            whole[group * 32 + owner] = jnp.zeros((CHUNK, C), F32)
-
-    def row(b, carry):
-        at = pl.multiple_of((2 - b) * COLS, COLS)
-        for c in range(3):
-            got = jnp.dot(
-                lhs[...],
-                field[2 - c, pl.ds(at, CELLS), :],
-                preferred_element_type=F32,
-            )
-            for a in range(3):
-                summed = (
-                    got[a * C : (a + 1) * C, 0:C]
-                    + got[(a + 1) * C : (a + 2) * C, C : 2 * C]
-                )
-                for i in range(4):
-                    chunk = 4 * tap(a, b, c) + i
-                    whole[chunk + 5 * (chunk // 27)] = summed[
-                        i * CHUNK : (i + 1) * CHUNK, :
-                    ]
-        return carry
-
-    lax.fori_loop(0, 3, row, 0)
+            part[group * 32 + owner] = jnp.zeros((CHUNK, C), F32)
+
+
+def far_kernel(
+    core_ref, halo, weight, inner, upstream, vol_t, near, grad, kept, sent, part, *scratch
+):
+    core = core_ref[0]
+    side(core, halo, weight, inner, upstream, vol_t, grad, part, *scratch)
+    for owner in range(27, 32):
+        for group in range(4):
+            part[group * 32 + owner] = jnp.zeros((CHUNK, C), F32)
 
     def share(owner, carry):
         for group in range(4):
-            kept[owner * 4 + group] = whole[group * 32 + core * 16 + owner]
-            sent[owner * 4 + group] = whole[
-                group * 32 + (1 - core) * 16 + owner
-            ].astype(BF)
+            mine = group * 32 + core * 16 + owner
+            other = group * 32 + (1 - core) * 16 + owner
+            kept[owner * 4 + group] = part[mine] + near[mine]
+            sent[owner * 4 + group] = (part[other] + near[other]).astype(BF)
         return carry
 
     lax.fori_loop(0, 16, share, 0)
 
 
-def kernel_gradient(core, near, far, near_halo, far_halo, vol_t):
-    return pl.pallas_call(
-        taps_kernel,
+PLANE = jax.ShapeDtypeStruct((CELLS, C), BF)
+PART = (4 * 32, CHUNK, C)
+SIDE = [
+    pltpu.VMEM((3, PADDED, C), BF),
+    pltpu.VMEM((9 * C, C), BF),
+    pltpu.VMEM((3, PADDED, C), BF),
+    pltpu.VMEM((C, CELLS), BF),
+    pltpu.SemaphoreType.DMA,
+]
+
+
+def near_side(core, halo, weight, inner, upstream, vol_t):
+    return pl.pallas_call(
+        near_kernel,
+        out_shape=[PLANE, jax.ShapeDtypeStruct(PART, F32)],
+        in_specs=[SMEM, VMEM, HBM, VMEM, VMEM, VMEM],
+        out_specs=[VMEM, VMEM],
+        scratch_shapes=SIDE,
+        compiler_params=PARAMS,
+        cost_estimate=cost(2 * CELLS * 3456 * 256, 5 << 20, CELLS * 128),
+        name="near_side",
+    )(core, halo, weight, inner, upstream, vol_t)
+
+
+def far_side(core, halo, weight, inner, upstream, vol_t, near):
+    return pl.pallas_call(
+        far_kernel,
         out_shape=[
+            PLANE,
             jax.ShapeDtypeStruct((64, CHUNK, C), F32),
             jax.ShapeDtypeStruct((64, CHUNK, C), BF),
         ],
-        in_specs=[SMEM] + [VMEM] * 5,
-        out_specs=[VMEM, VMEM],
-        scratch_shapes=[
-            pltpu.VMEM((3, PADDED, 2 * C), BF),
-            pltpu.VMEM((4 * C, CELLS), BF),
-            pltpu.VMEM((4 * 32, CHUNK, C), F32),
-        ],
+        in_specs=[SMEM, VMEM, HBM, VMEM, VMEM, VMEM, VMEM],
+        out_specs=[VMEM] * 3,
+        scratch_shapes=[pltpu.VMEM(PART, F32)] + SIDE,
         compiler_params=PARAMS,
-        cost_estimate=cost(2 * CELLS * 4608 * 256, 5 << 20),
-        name="kernel_gradient",
-    )(core, near, far, near_halo, far_halo, vol_t)
+        cost_estimate=cost(2 * CELLS * 3456 * 256, 5 << 20, CELLS * 128),
+        name="far_side",
+    )(core, halo, weight, inner, upstream, vol_t, near)
 
 
 def inner_back_kernel(
-    core_ref, near, far, weight, later, out, ended, field, mixed, held, made, sem, sems
+    core_ref, near, far, weight, later, out, field, mixed, held, made, sem, sems
 ):
     copy = fetched(weight, held, sem)
-    ended[0] = 0
     shifted_columns(ordered(core_ref[0], near, far), field, 0, False)
     copy.wait()
     for b in range(3):
@@ -308,12 +327,9 @@
 def inner_back(core, near, far, weight, later):
     return pl.pallas_call(
         inner_back_kernel,
-        out_shape=[
-            jax.ShapeDtypeStruct((2, CELLS, C), F32),
-            jax.ShapeDtypeStruct((1,), jnp.int32),
-        ],
+        out_shape=jax.ShapeDtypeStruct((2, CELLS, C), F32),
         in_specs=[SMEM, VMEM, VMEM, HBM, ANY],
-        out_specs=[HBM, SMEM],
+        out_specs=HBM,
         scratch_shapes=[
             pltpu.VMEM((3, PADDED, 2 * C), BF),
             pltpu.VMEM((2 * C, 9 * 256), BF),
@@ -397,12 +413,10 @@
     )(core, near, far, weight, given, inner)
 
 
-def planes_kernel(core_ref, vol, near, far, sems):
+def planes_kernel(core_ref, vol, near, far):
     core = core_ref[0]
-    first = fetched(vol.at[core], far, sems.at[0])
-    second = fetched(vol.at[1 - core], near, sems.at[1])
-    first.wait()
-    second.wait()
+    far[...] = vol[core]
+    near[...] = vol[1 - core]
 
 
 def both_planes(core, vol):
@@ -410,9 +424,8 @@
     return pl.pallas_call(
         planes_kernel,
         out_shape=[plane, plane],
-        in_specs=[SMEM, HBM],
-        out_specs=[HBM, HBM],
-        scratch_shapes=[pltpu.SemaphoreType.DMA((2,))],
+        in_specs=[SMEM, VMEM],
+        out_specs=[VMEM, VMEM],
         compiler_params=SMALL,
         cost_estimate=cost(0, 2 << 20),
         name="both_planes",
@@ -448,9 +461,9 @@
     return pl.pallas_call(
         mix_kernel,
         out_shape=jax.ShapeDtypeStruct((8, CHUNK, C), BF),
-        in_specs=[VMEM, SMEM],
+        in_specs=[VMEM, ANY],
         out_specs=VMEM,
-        compiler_params=SMALL,
+        compiler_params=LARGE,
         cost_estimate=cost(1 << 18, 1 << 20),
         name="mixed_rows",
     )(got, later)
@@ -502,24 +515,19 @@
     vol = volume.reshape(2, CELLS, C)
     up = upstream.reshape(2, CELLS, C)
     core = lax.axis_index("core")
-    at_core, at_near = core.reshape(1), (1 - core).reshape(1)
+    at_core = core.reshape(1)
     near_halo, far_halo = from_neighbours(*both_planes(at_core, vol))
     inner, vol_t = inner_conv(vol, weight)
-    near, ended = outer_conv(
-        "near_conv", at_near, near_halo, weight, inner, up, at_core
-    )
-    far, ended = outer_conv(
-        "far_conv", at_core, far_halo, weight, inner, up, ended
-    )
-    kept, sent = kernel_gradient(at_core, near, far, near_halo, far_halo, vol_t)
+    near, part = near_side(at_core, near_halo, weight, inner, up, vol_t)
+    far, kept, sent = far_side(at_core, far_halo, weight, inner, up, vol_t, part)
 
     rows = first_moment.shape[0]
     other = lax.ppermute(sent, "core", [(0, 1), (1, 0)])
     half = (kept + other.astype(F32)).astype(BF).reshape(16, 4, CHUNK, C)
     got = lax.all_to_all(half, ("x", "y"), 0, 0)
     grad_near, grad_far = from_neighbours(near, far)
-    local, ended = inner_back(at_core, near, far, weight, half)
-    part = mixed_rows(got, ended)
+    local = inner_back(at_core, near, far, weight, half)
+    part = mixed_rows(got, local)
     got = lax.all_to_all(part, ("zl", "sample"), 0, 0)
     owner = core * 16 + lax.axis_index("x") * 4 + lax.axis_index("y")
     at = jnp.minimum(owner * CHUNK, rows - CHUNK).reshape(1)

time: 87.5 us -> 83.2 us (0.951)
  waiting for transfers between devices: 13.6 us -> 10.8 us
  Pallas kernels: 34.9 us -> 33.8 us
    ppermute x2, waiting for transfers between devices: 3.59 us -> 0.55 us  [from_neighbours(): far_halo = lax.ppermute(far, SPACE, pairs + [(j, i) for i, j in pairs])]
    pallas_call x5 -> x4, Pallas kernels: 20.1 us -> 18.6 us  [the longest x1 6.7 us: inner_back(): pl.pallas_call(inner_back_kernel, out_shape=jax.ShapeDtypeStruct((2, CELL...]
    unnamed x18 -> x16, local copies, waits for them, and re-layouts: 3.64 us -> 3.63 us
  transfers between devices with their start and end apart: 8 -> 8, of which waited for: 4 -> 5; matrix products, arithmetic and copies ran while one was open for 0% -> 0% of each run, Pallas kernels for 27% -> 32%
where the time goes in v5:
time: 83.2 us; the launch traced here: 82.6 us
  Pallas kernels  33.8 us (41%)
  starting transfers between devices  32.6 us (39%)
  waiting for transfers between devices  10.8 us (13%)
  local copies, waits for them, and re-layouts  3.63 us (4%)
  other arithmetic  0.96 us (1%)
    all_to_all x1, starting transfers between devices, body(): whole = lax.all_to_all(step, ('core', 'x', 'y'), 0, 0)  8.43 us
    all_to_all x1, starting transfers between devices, body(): got = lax.all_to_all(part, ('zl', 'sample'), 0, 0)  8.39 us
    pallas_call x1, Pallas kernels, outer_back(): pl.pallas_call(outer_back_kernel, out_shape=jax.ShapeDtypeStruct((2, CELL...  7.42 us
    all_to_all x1, starting transfers between devices, body(): got = lax.all_to_all(half, ('x', 'y'), 0, 0)  6.77 us
    pallas_call x1, Pallas kernels, inner_back(): pl.pallas_call(inner_back_kernel, out_shape=jax.ShapeDtypeStruct((2, CELL...  6.7 us
    all_to_all x1, waiting for transfers between devices, body(): got = lax.all_to_all(part, ('zl', 'sample'), 0, 0)  6.63 us
    pallas_call x1, Pallas kernels, far_side(): pl.pallas_call(far_kernel, out_shape=[PLANE, jax.ShapeDtypeStruct((64, CH...  6.49 us
    ppermute x2, starting transfers between devices, from_neighbours(): far_halo = lax.ppermute(far, SPACE, pairs + [(j, i) for i, j in pairs])  5.52 us
  transfers between devices with their start and end apart: 8, of which 5 were waited for; matrix products, arithmetic and copies ran while one was open for 0% of the time, Pallas kernels for 32%

profile of v5, /device:TPU:1, one launch (start us, length us, event | category | flops | bytes accessed | tf_op | source)
XLA Modules:
  0.0 82.6 jit_solution(5415300068986892896)
XLA Ops:
  0.6 1.2 %copy-done = bf16[1,2,32,64,128]{4,3,2,1,0:T(8,128)(2,1)S(1)} copy-done((bf16[1,2,32,64,128]{4,3,2,1,0:T(8,128)(2,1)S(1)}, bf16[1,2,32,64,128]{4,3,2,1,0:T(8,128)(2,1)}, u32[]{:S(2)}) %copy-start) | copy-done | bytes 1048600
  1.9 3.3 %collective-permute-start = (bf16[2048,128]{1,0:T(8,128)(2,1)S(1)}, bf16[2048,128]{1,0:T(8,128)(2,1)S(1)}, u32[]{:S(2)}, u32[]{:S(2)}) collective-permute-start(bf16[2048,128]{1,0:T(8,128)(2,1)S(1)} %get-tuple-element.11), channel_id=1, source_target_pairs={{0,4},{4,0},{1,5},{5,1},{2,6},{6,2},{3,7},{7,3},{8,12},{12,8},{9,1... | collective-permute-start | bytes 1572872 | tf_op jit(solution)/shard_map/ppermute | solution.py:510
  5.3 1.9 %collective-permute-start.2 = (bf16[2048,128]{1,0:T(8,128)(2,1)S(1)}, bf16[2048,128]{1,0:T(8,128)(2,1)S(1)}, u32[]{:S(2)}, u32[]{:S(2)}) collective-permute-start(bf16[2048,128]{1,0:T(8,128)(2,1)S(1)} %get-tuple-element.15), channel_id=1, source_target_pairs={{4,8},{12,16},{20,24},{28,32},{36,40},{44,48},{52,56},{60,64},{68,... | collective-permute-start | bytes 1572872 | tf_op jit(solution)/shard_map/ppermute | solution.py:509
  7.2 1.2 %copy-done.1 = bf16[1,2,32,64,128]{4,3,2,1,0:T(8,128)(2,1)S(1)} copy-done((bf16[1,2,32,64,128]{4,3,2,1,0:T(8,128)(2,1)S(1)}, bf16[1,2,32,64,128]{4,3,2,1,0:T(8,128)(2,1)}, u32[]{:S(2)}) %copy-start.1) | copy-done | bytes 1048600
  8.4 1.2 %copy-done.5 = bf16[3456,128]{1,0:T(8,128)(2,1)S(1)} copy-done((bf16[3456,128]{1,0:T(8,128)(2,1)S(1)}, bf16[3456,128]{1,0:T(8,128)(2,1)}, u32[]{:S(2)}) %copy-start.5) | copy-done | bytes 884760
  9.6 4.5 %inner_conv.1 = (f32[2,2048,128]{2,1,0:T(8,128)S(1)}, bf16[256,2048]{1,0:T(8,128)(2,1)S(1)}) custom-call(bf16[2,2048,128]{2,1,0:T(8,128)(2,1)S(1)} %bitcast.8, bf16[3456,128]{1,0:T(8,128)(2,1)S(1)} %copy-done.5), custom_call_target="tpu_custom_call" | custom-call | flops 2415919104 | bytes 5242880 | tf_op jit(solution)/shard_map/inner_conv/pallas_call | solution.py:138
  14.1 5.3 %near_side.1 = (bf16[2048,128]{1,0:T(8,128)(2,1)S(1)}, f32[128,32,128]{2,1,0:T(8,128)S(1)}) custom-call(s32[1]{0:T(128)} %bitcast.core_ref, bf16[2048,128]{1,0:T(8,128)(2,1)S(1)} %collective-permute-done.halo, bf16[3456,128]{1,0:T(8,128)(2,1)S(1)} %copy-done.6, f32[2,2048,128]{2,1,0:T(8,128)S(1)} %get-tuple-element.12.inner, ...), custom_call_target="tpu_custom_call" | custom-call | flops 3623878656 | bytes 5242880 | tf_op jit(solution)/shard_map/near_side/pallas_call | solution.py:256
  19.4 0.5 collective-permute-done.2.halo
  20.0 6.5 %far_side.1 = (bf16[2048,128]{1,0:T(8,128)(2,1)}, f32[64,32,128]{2,1,0:T(8,128)S(1)}, bf16[64,32,128]{2,1,0:T(8,128)(2,1)S(1)}) custom-call(s32[1]{0:T(128)} %bitcast.core_ref, bf16[2048,128]{1,0:T(8,128)(2,1)S(1)} %collective-permute-done.2.halo, bf16[3456,128]{1,0:T(8,128)(2,1)S(1)} %copy-done.6, f32[2,2048,128]{2,1,0:T(8,128)S(1)} %get-tuple-element.12.inner, ...), custom_call_target="tpu_custom_call" | custom-call | flops 3623878656 | bytes 5242880 | tf_op jit(solution)/shard_map/far_side/pallas_call | solution.py:269
  26.6 1.9 %collective-permute-done.4 = bf16[64,32,128]{2,1,0:T(8,128)(2,1)S(1)} collective-permute-done((bf16[64,32,128]{2,1,0:T(8,128)(2,1)S(1)}, bf16[64,32,128]{2,1,0:T(8,128)(2,1)S(1)}, u32[]{:S(2)}, u32[]{:S(2)}) %collective-permute-start.4) | collective-permute-done | bytes 524320 | tf_op jit(solution)/shard_map/ppermute | solution.py:525
  28.5 1.0 %add_convert_fusion = bf16[64,32,128]{2,1,0:T(8,128)(2,1)} fusion(f32[64,32,128]{2,1,0:T(8,128)S(1)} %get-tuple-element.18, bf16[64,32,128]{2,1,0:T(8,128)(2,1)S(1)} %collective-permute-done.4), kind=kLoop, calls=%fused_computation | loop fusion | flops 786432 | bytes 2097152 | tf_op jit(solution)/shard_map/convert_element_type | solution.py:526
  29.4 6.8 %all-to-all-start = ((bf16[16,4,32,128]{3,2,1,0:T(8,128)(2,1)}), bf16[16,4,32,128]{3,2,1,0:T(8,128)(2,1)}, u32[]{:S(2)}, u32[]{:S(2)}) async-start(bf16[16,4,32,128]{3,2,1,0:T(8,128)(2,1)} %bitcast.3.later), calls=%async_computation | async-start | bytes 1048576 | tf_op jit(solution)/shard_map/all_to_all | solution.py:527
  36.2 3.6 %collective-permute-start.3 = (bf16[2048,128]{1,0:T(8,128)(2,1)}, bf16[2048,128]{1,0:T(8,128)(2,1)}, u32[]{:S(2)}, u32[]{:S(2)}) collective-permute-start(bf16[2048,128]{1,0:T(8,128)(2,1)} %get-tuple-element.17.far), channel_id=1, source_target_pairs={{4,8},{12,16},{20,24},{28,32},{36,40},{44,48},{52,56},{60,64},{68,... | collective-permute-start | bytes 1572872 | tf_op jit(solution)/shard_map/ppermute | solution.py:509
  39.8 0.1 collective-permute-start.1
  39.9 6.7 %inner_back.1.kept.later = f32[2,2048,128]{2,1,0:T(8,128)} custom-call(s32[1]{0:T(128)} %bitcast.core_ref, bf16[2048,128]{1,0:T(8,128)(2,1)} %copy-done.7, bf16[2048,128]{1,0:T(8,128)(2,1)} %get-tuple-element.17.far, bf16[3456,128]{1,0:T(8,128)(2,1)} %weight.9, bf16[16,4,32,128]{3,2,1,0:T(8,128)(2,1)} %bitcast.3.later), custom_call_target="tpu_custom_call" | custom-call | flops 2415919104 | bytes 5242880 | tf_op jit(solution)/shard_map/inner_back/pallas_call | solution.py:328
  46.7 0.3 all-to-all-done.got
  47.0 1.7 %mixed_rows.1 = bf16[8,32,128]{2,1,0:T(8,128)(2,1)} custom-call(bf16[16,4,32,128]{3,2,1,0:T(8,128)(2,1)} %all-to-all-done.got, f32[2,2048,128]{2,1,0:T(8,128)} %inner_back.1.kept.later), custom_call_target="tpu_custom_call" | custom-call | flops 262144 | bytes 1048576 | tf_op jit(solution)/shard_map/mixed_rows/pallas_call | solution.py:461
  48.7 8.4 %all-to-all-start.1 = ((bf16[8,32,128]{2,1,0:T(8,128)(2,1)}), bf16[8,32,128]{2,1,0:T(8,128)(2,1)S(1)}, u32[]{:S(2)}, u32[]{:S(2)}) async-start(bf16[8,32,128]{2,1,0:T(8,128)(2,1)} %mixed_rows.1), calls=%async_computation.1 | async-start | bytes 131072 | tf_op jit(solution)/shard_map/all_to_all | solution.py:531
  57.1 6.6 %all-to-all-done.1.got = bf16[8,32,128]{2,1,0:T(8,128)(2,1)S(1)} async-done(((bf16[8,32,128]{2,1,0:T(8,128)(2,1)}), bf16[8,32,128]{2,1,0:T(8,128)(2,1)S(1)}, u32[]{:S(2)}, u32[]{:S(2)}) %all-to-all-start.1) | async-done | bytes 65568 | tf_op jit(solution)/shard_map/all_to_all | solution.py:531
  63.8 0.8 spread_step.1
  64.5 8.4 %all-to-all-start.2 = ((bf16[32,32,128]{2,1,0:T(8,128)(2,1)}), bf16[32,32,128]{2,1,0:T(8,128)(2,1)S(1)}, u32[]{:S(2)}, u32[]{:S(2)}) async-start(bf16[32,32,128]{2,1,0:T(8,128)(2,1)} %spread_step.1), calls=%async_computation.2 | async-start | bytes 524288 | tf_op jit(solution)/shard_map/all_to_all | solution.py:535
  73.0 7.4 %outer_back.1 = bf16[2,2048,128]{2,1,0:T(8,128)(2,1)} custom-call(s32[1]{0:T(128)} %bitcast.core_ref, bf16[2048,128]{1,0:T(8,128)(2,1)} %collective-permute-done.1.near, bf16[2048,128]{1,0:T(8,128)(2,1)} %collective-permute-done.3.far, bf16[3456,128]{1,0:T(8,128)(2,1)} %weight.9, bf16[2,2048,128]{2,1,0:T(8,128)(2,1)} %bitcast.10, ...), custom_call_target="tpu_custom_call" | custom-call | flops 2415919104 | bytes 5242880 | tf_op jit(solution)/shard_map/outer_back/pallas_call | solution.py:397
  80.4 1.4 %all-to-all-done.2 = bf16[32,32,128]{2,1,0:T(8,128)(2,1)S(1)} async-done(((bf16[32,32,128]{2,1,0:T(8,128)(2,1)}), bf16[32,32,128]{2,1,0:T(8,128)(2,1)S(1)}, u32[]{:S(2)}, u32[]{:S(2)}) %all-to-all-start.2) | async-done | bytes 262176 | tf_op jit(solution)/shard_map/all_to_all | solution.py:535
  81.8 0.8 first_rows.1
  (18 shorter events, 0.2 us)
Async XLA Ops:
  0.6 1.2 %copy-start = (bf16[1,2,32,64,128]{4,3,2,1,0:T(8,128)(2,1)S(1)}, bf16[1,2,32,64,128]{4,3,2,1,0:T(8,128)(2,1)}, u32[]{:S(2)}) copy-start(bf16[1,2,32,64,128]{4,3,2,1,0:T(8,128)(2,1)} %param.5) | copy-start | bytes 3145732
  1.9 12.1 %collective-permute-start = (bf16[2048,128]{1,0:T(8,128)(2,1)S(1)}, bf16[2048,128]{1,0:T(8,128)(2,1)S(1)}, u32[]{:S(2)}, u32[]{:S(2)}) collective-permute-start(bf16[2048,128]{1,0:T(8,128)(2,1)S(1)} %get-tuple-element.11), channel_id=1, source_target_pairs={{0,4},{4,0},{1,5},{5,1},{2,6},{6,2},{3,7},{7,3},{8,12},{12,8},{9,1... | collective-permute-start | bytes 1572872 | tf_op jit(solution)/shard_map/ppermute | solution.py:510
  5.3 14.7 %collective-permute-start.2 = (bf16[2048,128]{1,0:T(8,128)(2,1)S(1)}, bf16[2048,128]{1,0:T(8,128)(2,1)S(1)}, u32[]{:S(2)}, u32[]{:S(2)}) collective-permute-start(bf16[2048,128]{1,0:T(8,128)(2,1)S(1)} %get-tuple-element.15), channel_id=1, source_target_pairs={{4,8},{12,16},{20,24},{28,32},{36,40},{44,48},{52,56},{60,64},{68,... | collective-permute-start | bytes 1572872 | tf_op jit(solution)/shard_map/ppermute | solution.py:509
  7.2 1.2 %copy-start.1 = (bf16[1,2,32,64,128]{4,3,2,1,0:T(8,128)(2,1)S(1)}, bf16[1,2,32,64,128]{4,3,2,1,0:T(8,128)(2,1)}, u32[]{:S(2)}) copy-start(bf16[1,2,32,64,128]{4,3,2,1,0:T(8,128)(2,1)} %param.5) | copy-start | bytes 3145732
  8.4 1.2 %copy-start.5 = (bf16[3456,128]{1,0:T(8,128)(2,1)S(1)}, bf16[3456,128]{1,0:T(8,128)(2,1)}, u32[]{:S(2)}) copy-start(bf16[3456,128]{1,0:T(8,128)(2,1)} %weight.9) | copy-start | bytes 2654212
  9.6 4.5 %copy-start.4 = (bf16[1,2,32,64,128]{4,3,2,1,0:T(8,128)(2,1)S(1)}, bf16[1,2,32,64,128]{4,3,2,1,0:T(8,128)(2,1)}, u32[]{:S(2)}) copy-start(bf16[1,2,32,64,128]{4,3,2,1,0:T(8,128)(2,1)} %param.6) | copy-start | bytes 3145732
  9.6 4.5 %copy-start.6 = (bf16[3456,128]{1,0:T(8,128)(2,1)S(1)}, bf16[3456,128]{1,0:T(8,128)(2,1)}, u32[]{:S(2)}) copy-start(bf16[3456,128]{1,0:T(8,128)(2,1)} %weight.9) | copy-start | bytes 2654212
  19.4 20.4 %copy-start.7 = (bf16[2048,128]{1,0:T(8,128)(2,1)}, bf16[2048,128]{1,0:T(8,128)(2,1)S(1)}, u32[]{:S(2)}) copy-start(bf16[2048,128]{1,0:T(8,128)(2,1)S(1)} %get-tuple-element.14.near) | copy-start | bytes 1572868
  26.5 2.0 %collective-permute-start.4 = (bf16[64,32,128]{2,1,0:T(8,128)(2,1)S(1)}, bf16[64,32,128]{2,1,0:T(8,128)(2,1)S(1)}, u32[]{:S(2)}, u32[]{:S(2)}) collective-permute-start(bf16[64,32,128]{2,1,0:T(8,128)(2,1)S(1)} %get-tuple-element.19), channel_id=1, source_target_pairs={{0,4},{4,0},{1,5},{5,1},{2,6},{6,2},{3,7},{7,3},{8,12},{12,8},{9,1... | collective-permute-start | bytes 1572872 | tf_op jit(solution)/shard_map/ppermute | solution.py:525
  29.4 17.5 %all-to-all-start = ((bf16[16,4,32,128]{3,2,1,0:T(8,128)(2,1)}), bf16[16,4,32,128]{3,2,1,0:T(8,128)(2,1)}, u32[]{:S(2)}, u32[]{:S(2)}) async-start(bf16[16,4,32,128]{3,2,1,0:T(8,128)(2,1)} %bitcast.3.later), calls=%async_computation | async-start | bytes 1048576 | tf_op jit(solution)/shard_map/all_to_all | solution.py:527
  36.2 36.7 %collective-permute-start.3 = (bf16[2048,128]{1,0:T(8,128)(2,1)}, bf16[2048,128]{1,0:T(8,128)(2,1)}, u32[]{:S(2)}, u32[]{:S(2)}) collective-permute-start(bf16[2048,128]{1,0:T(8,128)(2,1)} %get-tuple-element.17.far), channel_id=1, source_target_pairs={{4,8},{12,16},{20,24},{28,32},{36,40},{44,48},{52,56},{60,64},{68,... | collective-permute-start | bytes 1572872 | tf_op jit(solution)/shard_map/ppermute | solution.py:509
  39.8 33.1 %collective-permute-start.1 = (bf16[2048,128]{1,0:T(8,128)(2,1)S(1)}, bf16[2048,128]{1,0:T(8,128)(2,1)}, u32[]{:S(2)}, u32[]{:S(2)}) collective-permute-start(bf16[2048,128]{1,0:T(8,128)(2,1)S(1)} %get-tuple-element.14.near), channel_id=1, source_target_pairs={{0,4},{4,0},{1,5},{5,1},{2,6},{6,2},{3,7},{7,3},{8,12},{12,8},{9,1... | collective-permute-start | bytes 1572872 | tf_op jit(solution)/shard_map/ppermute | solution.py:510
  46.7 17.1 %copy-start.2 = (f32[864,128]{1,0:T(8,128)S(1)}, f32[864,128]{1,0:T(8,128)}, u32[]{:S(2)}) copy-start(f32[864,128]{1,0:T(8,128)} %first.1) | copy-start | bytes 1327108
  46.7 17.1 %copy-start.3 = (f32[864,128]{1,0:T(8,128)S(1)}, f32[864,128]{1,0:T(8,128)}, u32[]{:S(2)}) copy-start(f32[864,128]{1,0:T(8,128)} %second.1) | copy-start | bytes 1327108
  48.7 15.0 %all-to-all-start.1 = ((bf16[8,32,128]{2,1,0:T(8,128)(2,1)}), bf16[8,32,128]{2,1,0:T(8,128)(2,1)S(1)}, u32[]{:S(2)}, u32[]{:S(2)}) async-start(bf16[8,32,128]{2,1,0:T(8,128)(2,1)} %mixed_rows.1), calls=%async_computation.1 | async-start | bytes 131072 | tf_op jit(solution)/shard_map/all_to_all | solution.py:531
  64.5 17.3 %all-to-all-start.2 = ((bf16[32,32,128]{2,1,0:T(8,128)(2,1)}), bf16[32,32,128]{2,1,0:T(8,128)(2,1)S(1)}, u32[]{:S(2)}, u32[]{:S(2)}) async-start(bf16[32,32,128]{2,1,0:T(8,128)(2,1)} %spread_step.1), calls=%async_computation.2 | async-start | bytes 524288 | tf_op jit(solution)/shard_map/all_to_all | solution.py:535

commit v6 on v5

--- a/solution.py
+++ b/solution.py
@@ -344,73 +344,71 @@
     )(core, near, far, weight, later)
 
 
-def outer_back_kernel(
-    core_ref, near, far, weight, given, kept, out, field, mixed, held, upstream, inner, sems
-):
-    copy = fetched(weight, held, sems.at[0])
-    kept_copy = fetched(kept, inner, sems.at[1])
-    given_copy = fetched(given, upstream, sems.at[2])
-    core = core_ref[0]
-    shifted_columns([rows_of(near), rows_of(far)], field, 0, False)
+def outer_back_kernel(at_ref, halo, weight, given, kept, *rest):
+    out, field, mixed, held, upstream, inner, made, sems, leave_sems = rest[-9:]
+    z = at_ref[0]
+    first = pl.multiple_of((2 - 2 * z) * 9 * C, 9 * C)
+    copy = fetched(weight.at[pl.ds(first, 9 * C), :], held, sems.at[0])
+    kept_copy = fetched(kept.at[z], inner, sems.at[1])
+    given_copy = fetched(given.at[z], upstream, sems.at[2])
+    shifted_columns([rows_of(halo)], field, 0, False)
     copy.wait()
-    for k in range(2):
-        z = 1 - core if k == 0 else core
-        first = pl.multiple_of((2 - 2 * z) * 9 * C, C)
-        for b in range(3):
-            for c in range(3):
-                base = (b * 3 + c) * C
-                mixed[k, :, base : base + C] = held[
-                    pl.ds(first + tap(0, 2 - b, 2 - c) * C, C), :
-                ]
+    for b in range(3):
+        for c in range(3):
+            base = (b * 3 + c) * C
+            t = tap(0, 2 - b, 2 - c)
+            mixed[:, base : base + C] = held[t * C : (t + 1) * C, :]
     kept_copy.wait()
     given_copy.wait()
+    tiles = CELLS // TILE
+
+    def leave(i):
+        rows = pl.ds(pl.multiple_of(i * TILE, TILE), TILE)
+        return pltpu.make_async_copy(
+            made.at[rows, :], out.at[z, rows, :], leave_sems.at[i]
+        )
 
     def tile(i, carry):
         at = pl.multiple_of(i * TILE, TILE)
         rows = pl.ds(at, TILE)
-        for k in range(2):
-            z = 1 - core if k == 0 else core
-            lhs = jnp.concatenate(
-                [
-                    field[
-                        c,
-                        pl.ds(pl.multiple_of(at + b * COLS, COLS), TILE),
-                        k * C : (k + 1) * C,
-                    ]
-                    for b in range(3)
-                    for c in range(3)
-                ],
-                axis=1,
-            )
-            got = lax.dot_general(
-                lhs, mixed[k], (((1,), (1,)), ((), ())), preferred_element_type=F32
-            )
-            out[z, rows, :] = (
-                upstream[z, rows, :].astype(F32) + (inner[z, rows, :] + got)
-            ).astype(BF)
+        got = lax.dot_general(
+            taps_of(field, at, TILE),
+            mixed[...],
+            (((1,), (1,)), ((), ())),
+            preferred_element_type=F32,
+        )
+        made[rows, :] = (
+            upstream[rows, :].astype(F32) + (inner[rows, :] + got)
+        ).astype(BF)
+        leave(i).start()
         return carry
 
-    lax.fori_loop(0, CELLS // TILE, tile, 0)
-
-
-def outer_back(core, near, far, weight, given, inner):
+    lax.fori_loop(0, tiles, tile, 0)
+    for i in range(tiles):
+        leave(i).wait()
+
+
+def outer_back(name, z, halo, weight, given, inner, *begun):
     return pl.pallas_call(
         outer_back_kernel,
         out_shape=jax.ShapeDtypeStruct((2, CELLS, C), BF),
-        in_specs=[SMEM, VMEM, VMEM, HBM, HBM, HBM],
-        out_specs=VMEM,
+        in_specs=[SMEM, VMEM] + [HBM] * (3 + len(begun)),
+        out_specs=HBM,
         scratch_shapes=[
-            pltpu.VMEM((3, PADDED, 2 * C), BF),
-            pltpu.VMEM((2, C, 9 * C), BF),
-            pltpu.VMEM((27 * C, C), BF),
-            pltpu.VMEM((2, CELLS, C), BF),
-            pltpu.VMEM((2, CELLS, C), F32),
+            pltpu.VMEM((3, PADDED, C), BF),
+            pltpu.VMEM((C, 9 * C), BF),
+            pltpu.VMEM((9 * C, C), BF),
+            pltpu.VMEM((CELLS, C), BF),
+            pltpu.VMEM((CELLS, C), F32),
+            pltpu.VMEM((CELLS, C), BF),
             pltpu.SemaphoreType.DMA((3,)),
+            pltpu.SemaphoreType.DMA((CELLS // TILE,)),
         ],
+        input_output_aliases={5: 0} if begun else {},
         compiler_params=LARGE,
-        cost_estimate=cost(2 * CELLS * 2304 * 256, 5 << 20),
-        name="outer_back",
-    )(core, near, far, weight, given, inner)
+        cost_estimate=cost(CELLS * 2304 * 256, 3 << 20),
+        name=name,
+    )(z, halo, weight, given, inner, *begun)
 
 
 def planes_kernel(core_ref, vol, near, far):
@@ -432,8 +430,18 @@
     )(core, vol)
 
 
-def first_rows_kernel(whole, out):
-    out[...] = whole[0 : out.shape[0], :].astype(F32)
+def first_rows_kernel(whole, out, wide, sems):
+    rows = out.shape[0]
+    step = rows // 4
+    copies = []
+    for k in range(4):
+        part = slice(k * step, (k + 1) * step)
+        wide[part, :] = whole[part, :].astype(F32)
+        copy = pltpu.make_async_copy(wide.at[part, :], out.at[part, :], sems.at[k])
+        copy.start()
+        copies.append(copy)
+    for copy in copies:
+        copy.wait()
 
 
 def first_rows(whole, rows):
@@ -441,14 +449,15 @@
         first_rows_kernel,
         out_shape=jax.ShapeDtypeStruct((rows, C), F32),
         in_specs=[VMEM],
-        out_specs=VMEM,
+        out_specs=ANY,
+        scratch_shapes=[pltpu.VMEM((rows, C), F32), pltpu.SemaphoreType.DMA((4,))],
         compiler_params=SMALL,
         cost_estimate=cost(0, 1 << 20),
         name="first_rows",
     )(whole)
 
 
-def mix_kernel(got, later, out):
+def mix_kernel(got, out):
     for group in range(4):
         total = got[0, group].astype(F32)
         for k in range(1, 16):
@@ -457,16 +466,16 @@
         out[4 + group] = total.astype(BF)
 
 
-def mixed_rows(got, later):
+def mixed_rows(got):
     return pl.pallas_call(
         mix_kernel,
         out_shape=jax.ShapeDtypeStruct((8, CHUNK, C), BF),
-        in_specs=[VMEM, ANY],
+        in_specs=[VMEM],
         out_specs=VMEM,
-        compiler_params=LARGE,
+        compiler_params=SMALL,
         cost_estimate=cost(1 << 18, 1 << 20),
         name="mixed_rows",
-    )(got, later)
+    )(got)
 
 
 def step_kernel(at_ref, got, first, second, out):
@@ -524,16 +533,23 @@
     rows = first_moment.shape[0]
     other = lax.ppermute(sent, "core", [(0, 1), (1, 0)])
     half = (kept + other.astype(F32)).astype(BF).reshape(16, 4, CHUNK, C)
+    near_sent, half = lax.optimization_barrier((near, half))
     got = lax.all_to_all(half, ("x", "y"), 0, 0)
-    grad_near, grad_far = from_neighbours(near, far)
+    grad_near, grad_far = from_neighbours(near_sent, far)
     local = inner_back(at_core, near, far, weight, half)
-    part = mixed_rows(got, local)
+    got, local = lax.optimization_barrier((got, local))
+    part = mixed_rows(got)
+    grad_near, part = lax.optimization_barrier((grad_near, part))
     got = lax.all_to_all(part, ("zl", "sample"), 0, 0)
+    half_done = outer_back("near_back", 1 - at_core, grad_near, weight, up, local)
+    got, half_done = lax.optimization_barrier((got, half_done))
     owner = core * 16 + lax.axis_index("x") * 4 + lax.axis_index("y")
     at = jnp.minimum(owner * CHUNK, rows - CHUNK).reshape(1)
     step = spread_step(at, got, first_moment, second_moment)
     whole = lax.all_to_all(step, ("core", "x", "y"), 0, 0)
-    grad_volume = outer_back(at_core, grad_near, grad_far, weight, up, local)
+    grad_volume = outer_back(
+        "far_back", at_core, grad_far, weight, up, local, half_done
+    )
     direction = first_rows(whole.reshape(OWNERS * CHUNK, C), rows)
     return (grad_volume.reshape(volume.shape), direction)
 

time: 83.2 us -> 81.9 us (0.984)
  waiting for transfers between devices: 10.8 us -> 7.68 us
  Pallas kernels: 33.8 us -> 35.7 us
    all_to_all x1, waiting for transfers between devices: 6.63 us -> 1.42 us  [body(): got = lax.all_to_all(part, ('zl', 'sample'), 0, 0)]
    pallas_call x1 -> x2, Pallas kernels: 7.42 us -> 10.3 us  [outer_back(): pl.pallas_call(outer_back_kernel, out_shape=jax.ShapeDtypeStruct((2, CELL...]
    all_to_all x1, waiting for transfers between devices: 1.37 us -> 3.72 us  [body(): whole = lax.all_to_all(step, ('core', 'x', 'y'), 0, 0)]
    pallas_call x1, Pallas kernels: 1.74 us -> 0.7 us  [mixed_rows(): pl.pallas_call(mix_kernel, out_shape=jax.ShapeDtypeStruct((8, CHUNK, C),...]
    unnamed x16 -> x18, local copies, waits for them, and re-layouts: 3.63 us -> 3.64 us
  transfers between devices with their start and end apart: 8 -> 8, of which waited for: 5 -> 5; matrix products, arithmetic and copies ran while one was open for 0% -> 0% of each run, Pallas kernels for 32% -> 35%
where the time goes in v6:
time: 81.9 us; the launch traced here: 81.1 us
  Pallas kernels  35.7 us (44%)
  starting transfers between devices  32.4 us (40%)
  waiting for transfers between devices  7.68 us (9%)
  local copies, waits for them, and re-layouts  3.64 us (4%)
  other arithmetic  0.93 us (1%)
    pallas_call x2, Pallas kernels, outer_back(): pl.pallas_call(outer_back_kernel, out_shape=jax.ShapeDtypeStruct((2, CELL...  10.3 us
    all_to_all x1, starting transfers between devices, body(): got = lax.all_to_all(part, ('zl', 'sample'), 0, 0)  8.36 us
    all_to_all x1, starting transfers between devices, body(): whole = lax.all_to_all(step, ('core', 'x', 'y'), 0, 0)  7.91 us
    all_to_all x1, starting transfers between devices, body(): got = lax.all_to_all(half, ('x', 'y'), 0, 0)  6.95 us
    pallas_call x1, Pallas kernels, inner_back(): pl.pallas_call(inner_back_kernel, out_shape=jax.ShapeDtypeStruct((2, CELL...  6.7 us
    pallas_call x1, Pallas kernels, far_side(): pl.pallas_call(far_kernel, out_shape=[PLANE, jax.ShapeDtypeStruct((64, CH...  6.56 us
    ppermute x2, starting transfers between devices, from_neighbours(): far_halo = lax.ppermute(far, SPACE, pairs + [(j, i) for i, j in pairs])  5.63 us
    pallas_call x1, Pallas kernels, near_side(): pl.pallas_call(near_kernel, out_shape=[PLANE, jax.ShapeDtypeStruct(PART,...  5.36 us
  transfers between devices with their start and end apart: 8, of which 5 were waited for; matrix products, arithmetic and copies ran while one was open for 0% of the time, Pallas kernels for 35%

profile of v6, /device:TPU:1, one launch (start us, length us, event | category | flops | bytes accessed | tf_op | source)
XLA Modules:
  0.0 81.1 jit_solution(3582470861909246989)
XLA Ops:
  0.6 1.2 %copy-done.3 = bf16[1,2,32,64,128]{4,3,2,1,0:T(8,128)(2,1)S(1)} copy-done((bf16[1,2,32,64,128]{4,3,2,1,0:T(8,128)(2,1)S(1)}, bf16[1,2,32,64,128]{4,3,2,1,0:T(8,128)(2,1)}, u32[]{:S(2)}) %copy-start.3) | copy-done | bytes 1048600
  1.9 3.3 %collective-permute-start.1 = (bf16[2048,128]{1,0:T(8,128)(2,1)S(1)}, bf16[2048,128]{1,0:T(8,128)(2,1)S(1)}, u32[]{:S(2)}, u32[]{:S(2)}) collective-permute-start(bf16[2048,128]{1,0:T(8,128)(2,1)S(1)} %get-tuple-element.22), channel_id=1, source_target_pairs={{0,4},{4,0},{1,5},{5,1},{2,6},{6,2},{3,7},{7,3},{8,12},{12,8},{9,1... | collective-permute-start | bytes 1572872 | tf_op jit(solution)/shard_map/ppermute | solution.py:519
  5.3 2.0 %collective-permute-start = (bf16[2048,128]{1,0:T(8,128)(2,1)S(1)}, bf16[2048,128]{1,0:T(8,128)(2,1)S(1)}, u32[]{:S(2)}, u32[]{:S(2)}) collective-permute-start(bf16[2048,128]{1,0:T(8,128)(2,1)S(1)} %get-tuple-element.19), channel_id=1, source_target_pairs={{4,8},{12,16},{20,24},{28,32},{36,40},{44,48},{52,56},{60,64},{68,... | collective-permute-start | bytes 1572872 | tf_op jit(solution)/shard_map/ppermute | solution.py:518
  7.3 1.2 %copy-done.1 = bf16[3456,128]{1,0:T(8,128)(2,1)S(1)} copy-done((bf16[3456,128]{1,0:T(8,128)(2,1)S(1)}, bf16[3456,128]{1,0:T(8,128)(2,1)}, u32[]{:S(2)}) %copy-start.1) | copy-done | bytes 884760
  8.5 1.2 %copy-done.4 = bf16[1,2,32,64,128]{4,3,2,1,0:T(8,128)(2,1)S(1)} copy-done((bf16[1,2,32,64,128]{4,3,2,1,0:T(8,128)(2,1)S(1)}, bf16[1,2,32,64,128]{4,3,2,1,0:T(8,128)(2,1)}, u32[]{:S(2)}) %copy-start.4) | copy-done | bytes 1048600
  9.7 4.5 %inner_conv.1 = (f32[2,2048,128]{2,1,0:T(8,128)S(1)}, bf16[256,2048]{1,0:T(8,128)(2,1)S(1)}) custom-call(bf16[2,2048,128]{2,1,0:T(8,128)(2,1)S(1)} %bitcast.12, bf16[3456,128]{1,0:T(8,128)(2,1)S(1)} %copy-done.1), custom_call_target="tpu_custom_call" | custom-call | flops 2415919104 | bytes 5242880 | tf_op jit(solution)/shard_map/inner_conv/pallas_call | solution.py:138
  14.2 5.4 %near_side.1 = (bf16[2048,128]{1,0:T(8,128)(2,1)S(1)}, f32[128,32,128]{2,1,0:T(8,128)S(1)}) custom-call(s32[1]{0:T(128)} %bitcast.core_ref.at_ref, bf16[2048,128]{1,0:T(8,128)(2,1)S(1)} %collective-permute-done.1.halo, bf16[3456,128]{1,0:T(8,128)(2,1)S(1)} %copy-done.2, f32[2,2048,128]{2,1,0:T(8,128)S(1)} %get-tuple-element.20.inner, ...), custom_call_target="tpu_custom_call" | custom-call | flops 3623878656 | bytes 5242880 | tf_op jit(solution)/shard_map/near_side/pallas_call | solution.py:256
  19.6 0.5 collective-permute-done.halo
  20.1 6.6 %far_side.1 = (bf16[2048,128]{1,0:T(8,128)(2,1)}, f32[64,32,128]{2,1,0:T(8,128)S(1)}, bf16[64,32,128]{2,1,0:T(8,128)(2,1)S(1)}) custom-call(s32[1]{0:T(128)} %bitcast.core_ref.at_ref, bf16[2048,128]{1,0:T(8,128)(2,1)S(1)} %collective-permute-done.halo, bf16[3456,128]{1,0:T(8,128)(2,1)S(1)} %copy-done.2, f32[2,2048,128]{2,1,0:T(8,128)S(1)} %get-tuple-element.20.inner, ...), custom_call_target="tpu_custom_call" | custom-call | flops 3623878656 | bytes 5242880 | tf_op jit(solution)/shard_map/far_side/pallas_call | solution.py:269
  26.8 1.9 %collective-permute-done.3 = bf16[64,32,128]{2,1,0:T(8,128)(2,1)S(1)} collective-permute-done((bf16[64,32,128]{2,1,0:T(8,128)(2,1)S(1)}, bf16[64,32,128]{2,1,0:T(8,128)(2,1)S(1)}, u32[]{:S(2)}, u32[]{:S(2)}) %collective-permute-start.3) | collective-permute-done | bytes 524320 | tf_op jit(solution)/shard_map/ppermute | solution.py:534
  28.7 0.9 %add_convert_fusion = bf16[64,32,128]{2,1,0:T(8,128)(2,1)} fusion(f32[64,32,128]{2,1,0:T(8,128)S(1)} %get-tuple-element.26, bf16[64,32,128]{2,1,0:T(8,128)(2,1)S(1)} %collective-permute-done.3), kind=kLoop, calls=%fused_computation | loop fusion | flops 786432 | bytes 2097152 | tf_op jit(solution)/shard_map/convert_element_type | solution.py:535
  29.6 0.1 collective-permute-start.4
  29.8 6.9 %all-to-all-start = ((bf16[16,4,32,128]{3,2,1,0:T(8,128)(2,1)}), bf16[16,4,32,128]{3,2,1,0:T(8,128)(2,1)S(1)}, u32[]{:S(2)}, u32[]{:S(2)}) async-start(bf16[16,4,32,128]{3,2,1,0:T(8,128)(2,1)} %bitcast.3.later), calls=%async_computation | async-start | bytes 1048576 | tf_op jit(solution)/shard_map/all_to_all | solution.py:537
  36.7 3.6 %collective-permute-start.2 = (bf16[2048,128]{1,0:T(8,128)(2,1)}, bf16[2048,128]{1,0:T(8,128)(2,1)}, u32[]{:S(2)}, u32[]{:S(2)}) collective-permute-start(bf16[2048,128]{1,0:T(8,128)(2,1)} %get-tuple-element.24.far), channel_id=1, source_target_pairs={{4,8},{12,16},{20,24},{28,32},{36,40},{44,48},{52,56},{60,64},{68,... | collective-permute-start | bytes 1572872 | tf_op jit(solution)/shard_map/ppermute | solution.py:518
  40.3 6.7 %inner_back.1.kept = f32[2,2048,128]{2,1,0:T(8,128)} custom-call(s32[1]{0:T(128)} %bitcast.core_ref.at_ref, bf16[2048,128]{1,0:T(8,128)(2,1)} %copy-done.7, bf16[2048,128]{1,0:T(8,128)(2,1)} %get-tuple-element.24.far, bf16[3456,128]{1,0:T(8,128)(2,1)} %weight.11, bf16[16,4,32,128]{3,2,1,0:T(8,128)(2,1)} %bitcast.3.later), custom_call_target="tpu_custom_call" | custom-call | flops 2415919104 | bytes 5242880 | tf_op jit(solution)/shard_map/inner_back/pallas_call | solution.py:328
  47.1 0.7 mixed_rows.1
  47.9 8.4 %all-to-all-start.1 = ((bf16[8,32,128]{2,1,0:T(8,128)(2,1)}), bf16[8,32,128]{2,1,0:T(8,128)(2,1)S(1)}, u32[]{:S(2)}, u32[]{:S(2)}) async-start(bf16[8,32,128]{2,1,0:T(8,128)(2,1)} %mixed_rows.1), calls=%async_computation.1 | async-start | bytes 131072 | tf_op jit(solution)/shard_map/all_to_all | solution.py:543
  56.2 5.2 %near_back.1.rest_0_ = bf16[2,2048,128]{2,1,0:T(8,128)(2,1)} custom-call(s32[1]{0:T(128)S(6)} %sub.3.at_ref, bf16[2048,128]{1,0:T(8,128)(2,1)} %copy-done.8, bf16[3456,128]{1,0:T(8,128)(2,1)} %weight.11, bf16[2,2048,128]{2,1,0:T(8,128)(2,1)} %bitcast.7, f32[2,2048,128]{2,1,0:T(8,128)} %inner_back.1.kept), custom_call_target="tpu_custom_call" | custom-call | flops 1207959552 | bytes 3145728 | tf_op jit(solution)/shard_map/near_back/pallas_call | solution.py:392
  61.4 1.4 %all-to-all-done.1.got = bf16[8,32,128]{2,1,0:T(8,128)(2,1)S(1)} async-done(((bf16[8,32,128]{2,1,0:T(8,128)(2,1)}), bf16[8,32,128]{2,1,0:T(8,128)(2,1)S(1)}, u32[]{:S(2)}, u32[]{:S(2)}) %all-to-all-start.1) | async-done | bytes 65568 | tf_op jit(solution)/shard_map/all_to_all | solution.py:543
  62.8 0.8 spread_step.1
  63.6 7.9 %all-to-all-start.2 = ((bf16[32,32,128]{2,1,0:T(8,128)(2,1)}), bf16[32,32,128]{2,1,0:T(8,128)(2,1)S(1)}, u32[]{:S(2)}, u32[]{:S(2)}) async-start(bf16[32,32,128]{2,1,0:T(8,128)(2,1)} %spread_step.1), calls=%async_computation.2 | async-start | bytes 524288 | tf_op jit(solution)/shard_map/all_to_all | solution.py:549
  71.5 5.1 %far_back.1 = bf16[2,2048,128]{2,1,0:T(8,128)(2,1)} custom-call(s32[1]{0:T(128)} %bitcast.core_ref.at_ref, bf16[2048,128]{1,0:T(8,128)(2,1)} %collective-permute-done.2.halo, bf16[3456,128]{1,0:T(8,128)(2,1)} %weight.11, bf16[2,2048,128]{2,1,0:T(8,128)(2,1)} %bitcast.8, f32[2,2048,128]{2,1,0:T(8,128)} %inner_back.1.kept, ...), custom_call_target="tpu_custom_call", output_to_operand_aliasing={{}: (5, {})} | custom-call | flops 1207959552 | bytes 3145728 | tf_op jit(solution)/shard_map/far_back/pallas_call | solution.py:392
  76.6 3.7 %all-to-all-done.2 = bf16[32,32,128]{2,1,0:T(8,128)(2,1)S(1)} async-done(((bf16[32,32,128]{2,1,0:T(8,128)(2,1)}), bf16[32,32,128]{2,1,0:T(8,128)(2,1)S(1)}, u32[]{:S(2)}, u32[]{:S(2)}) %all-to-all-start.2) | async-done | bytes 262176 | tf_op jit(solution)/shard_map/all_to_all | solution.py:549
  80.3 0.8 first_rows.1
  (21 shorter events, 0.3 us)
Async XLA Ops:
  0.6 1.2 %copy-start.3 = (bf16[1,2,32,64,128]{4,3,2,1,0:T(8,128)(2,1)S(1)}, bf16[1,2,32,64,128]{4,3,2,1,0:T(8,128)(2,1)}, u32[]{:S(2)}) copy-start(bf16[1,2,32,64,128]{4,3,2,1,0:T(8,128)(2,1)} %param.5) | copy-start | bytes 3145732
  1.9 12.3 %collective-permute-start.1 = (bf16[2048,128]{1,0:T(8,128)(2,1)S(1)}, bf16[2048,128]{1,0:T(8,128)(2,1)S(1)}, u32[]{:S(2)}, u32[]{:S(2)}) collective-permute-start(bf16[2048,128]{1,0:T(8,128)(2,1)S(1)} %get-tuple-element.22), channel_id=1, source_target_pairs={{0,4},{4,0},{1,5},{5,1},{2,6},{6,2},{3,7},{7,3},{8,12},{12,8},{9,1... | collective-permute-start | bytes 1572872 | tf_op jit(solution)/shard_map/ppermute | solution.py:519
  5.3 8.9 %copy-start = (bf16[1,2,32,64,128]{4,3,2,1,0:T(8,128)(2,1)S(1)}, bf16[1,2,32,64,128]{4,3,2,1,0:T(8,128)(2,1)}, u32[]{:S(2)}) copy-start(bf16[1,2,32,64,128]{4,3,2,1,0:T(8,128)(2,1)} %param.6) | copy-start | bytes 3145732
  5.3 14.9 %collective-permute-start = (bf16[2048,128]{1,0:T(8,128)(2,1)S(1)}, bf16[2048,128]{1,0:T(8,128)(2,1)S(1)}, u32[]{:S(2)}, u32[]{:S(2)}) collective-permute-start(bf16[2048,128]{1,0:T(8,128)(2,1)S(1)} %get-tuple-element.19), channel_id=1, source_target_pairs={{4,8},{12,16},{20,24},{28,32},{36,40},{44,48},{52,56},{60,64},{68,... | collective-permute-start | bytes 1572872 | tf_op jit(solution)/shard_map/ppermute | solution.py:518
  7.3 1.2 %copy-start.1 = (bf16[3456,128]{1,0:T(8,128)(2,1)S(1)}, bf16[3456,128]{1,0:T(8,128)(2,1)}, u32[]{:S(2)}) copy-start(bf16[3456,128]{1,0:T(8,128)(2,1)} %weight.11) | copy-start | bytes 2654212
  8.5 1.2 %copy-start.4 = (bf16[1,2,32,64,128]{4,3,2,1,0:T(8,128)(2,1)S(1)}, bf16[1,2,32,64,128]{4,3,2,1,0:T(8,128)(2,1)}, u32[]{:S(2)}) copy-start(bf16[1,2,32,64,128]{4,3,2,1,0:T(8,128)(2,1)} %param.5) | copy-start | bytes 3145732
  9.7 4.5 %copy-start.2 = (bf16[3456,128]{1,0:T(8,128)(2,1)S(1)}, bf16[3456,128]{1,0:T(8,128)(2,1)}, u32[]{:S(2)}) copy-start(bf16[3456,128]{1,0:T(8,128)(2,1)} %weight.11) | copy-start | bytes 2654212
  19.6 10.0 %copy-start.7 = (bf16[2048,128]{1,0:T(8,128)(2,1)}, bf16[2048,128]{1,0:T(8,128)(2,1)S(1)}, u32[]{:S(2)}) copy-start(bf16[2048,128]{1,0:T(8,128)(2,1)S(1)} %get-tuple-element.30.near) | copy-start | bytes 1572868
  26.7 2.0 %collective-permute-start.3 = (bf16[64,32,128]{2,1,0:T(8,128)(2,1)S(1)}, bf16[64,32,128]{2,1,0:T(8,128)(2,1)S(1)}, u32[]{:S(2)}, u32[]{:S(2)}) collective-permute-start(bf16[64,32,128]{2,1,0:T(8,128)(2,1)S(1)} %get-tuple-element.27), channel_id=1, source_target_pairs={{0,4},{4,0},{1,5},{5,1},{2,6},{6,2},{3,7},{7,3},{8,12},{12,8},{9,1... | collective-permute-start | bytes 1572872 | tf_op jit(solution)/shard_map/ppermute | solution.py:534
  29.6 18.2 %collective-permute-start.4 = (bf16[2048,128]{1,0:T(8,128)(2,1)S(1)}, bf16[2048,128]{1,0:T(8,128)(2,1)S(1)}, u32[]{:S(2)}, u32[]{:S(2)}) collective-permute-start(bf16[2048,128]{1,0:T(8,128)(2,1)S(1)} %get-tuple-element.30.near), channel_id=1, source_target_pairs={{0,4},{4,0},{1,5},{5,1},{2,6},{6,2},{3,7},{7,3},{8,12},{12,8},{9,1... | collective-permute-start | bytes 1572872 | tf_op jit(solution)/shard_map/ppermute | solution.py:519
  29.8 17.4 %all-to-all-start = ((bf16[16,4,32,128]{3,2,1,0:T(8,128)(2,1)}), bf16[16,4,32,128]{3,2,1,0:T(8,128)(2,1)S(1)}, u32[]{:S(2)}, u32[]{:S(2)}) async-start(bf16[16,4,32,128]{3,2,1,0:T(8,128)(2,1)} %bitcast.3.later), calls=%async_computation | async-start | bytes 1048576 | tf_op jit(solution)/shard_map/all_to_all | solution.py:537
  36.7 34.8 %collective-permute-start.2 = (bf16[2048,128]{1,0:T(8,128)(2,1)}, bf16[2048,128]{1,0:T(8,128)(2,1)}, u32[]{:S(2)}, u32[]{:S(2)}) collective-permute-start(bf16[2048,128]{1,0:T(8,128)(2,1)} %get-tuple-element.24.far), channel_id=1, source_target_pairs={{4,8},{12,16},{20,24},{28,32},{36,40},{44,48},{52,56},{60,64},{68,... | collective-permute-start | bytes 1572872 | tf_op jit(solution)/shard_map/ppermute | solution.py:518
  47.8 8.4 %copy-start.8 = (bf16[2048,128]{1,0:T(8,128)(2,1)}, bf16[2048,128]{1,0:T(8,128)(2,1)S(1)}, u32[]{:S(2)}) copy-start(bf16[2048,128]{1,0:T(8,128)(2,1)S(1)} %collective-permute-done.4.halo) | copy-start | bytes 1572868
  47.9 15.0 %all-to-all-start.1 = ((bf16[8,32,128]{2,1,0:T(8,128)(2,1)}), bf16[8,32,128]{2,1,0:T(8,128)(2,1)S(1)}, u32[]{:S(2)}, u32[]{:S(2)}) async-start(bf16[8,32,128]{2,1,0:T(8,128)(2,1)} %mixed_rows.1), calls=%async_computation.1 | async-start | bytes 131072 | tf_op jit(solution)/shard_map/all_to_all | solution.py:543
  56.2 6.6 %copy-start.5 = (f32[864,128]{1,0:T(8,128)S(1)}, f32[864,128]{1,0:T(8,128)}, u32[]{:S(2)}) copy-start(f32[864,128]{1,0:T(8,128)} %first.1) | copy-start | bytes 1327108
  56.2 6.6 %copy-start.6 = (f32[864,128]{1,0:T(8,128)S(1)}, f32[864,128]{1,0:T(8,128)}, u32[]{:S(2)}) copy-start(f32[864,128]{1,0:T(8,128)} %second.1) | copy-start | bytes 1327108
  63.6 16.8 %all-to-all-start.2 = ((bf16[32,32,128]{2,1,0:T(8,128)(2,1)}), bf16[32,32,128]{2,1,0:T(8,128)(2,1)S(1)}, u32[]{:S(2)}, u32[]{:S(2)}) async-start(bf16[32,32,128]{2,1,0:T(8,128)(2,1)} %spread_step.1), calls=%async_computation.2 | async-start | bytes 524288 | tf_op jit(solution)/shard_map/all_to_all | solution.py:549

commit v7 on v6

--- a/solution.py
+++ b/solution.py
@@ -31,6 +31,7 @@
 SMEM = pl.BlockSpec(memory_space=pltpu.SMEM)
 WHOLE = pltpu.CompilerParams(vmem_limit_bytes=60 * 1024 * 1024)
 LARGE = pltpu.CompilerParams(vmem_limit_bytes=62 * 1024 * 1024 + 512 * 1024)
+INNER = pltpu.CompilerParams(vmem_limit_bytes=44 * 1024 * 1024)
 SMALL = pltpu.CompilerParams(vmem_limit_bytes=4 * 1024 * 1024)
 PARAMS = pltpu.CompilerParams(vmem_limit_bytes=32 * 1024 * 1024)
 
@@ -107,9 +108,9 @@
     )
 
 
-def inner_kernel(vol, weight, out, vol_t, field, mixed, held, sem):
+def inner_kernel(core_ref, near, far, weight, out, vol_t, field, mixed, held, sem):
     copy = fetched(weight, held, sem)
-    planes = [rows_of(vol.at[0]), rows_of(vol.at[1])]
+    planes = ordered(core_ref[0], near, far)
     shifted_columns(planes, field, 0, False)
     copy.wait()
     for b in range(3):
@@ -134,14 +135,14 @@
         transposed(planes[p], vol_t, p * C)
 
 
-def inner_conv(vol, weight):
+def inner_conv(core, near, far, weight):
     return pl.pallas_call(
         inner_kernel,
         out_shape=[
             jax.ShapeDtypeStruct((2, CELLS, C), F32),
             jax.ShapeDtypeStruct((2 * C, CELLS), BF),
         ],
-        in_specs=[VMEM, HBM],
+        in_specs=[SMEM, VMEM, VMEM, HBM],
         out_specs=[VMEM] * 2,
         scratch_shapes=[
             pltpu.VMEM((3, PADDED, 2 * C), BF),
@@ -149,13 +150,35 @@
             pltpu.VMEM((27 * C, C), BF),
             pltpu.SemaphoreType.DMA,
         ],
-        compiler_params=PARAMS,
+        compiler_params=INNER,
         cost_estimate=cost(2 * CELLS * 2304 * 256, 5 << 20),
         name="inner_conv",
-    )(vol, weight)
-
-
-def side(z, halo, weight, inner, upstream, vol_t, grad, part, field, held, shifts, turned, sem):
+    )(core, near, far, weight)
+
+
+def place(core, group, owner):
+    half = jnp.where(owner // 16 == core, 0, 64)
+    return half + (owner % 16) * 4 + group
+
+
+def side(
+    core,
+    z,
+    begun,
+    halo,
+    weight,
+    inner,
+    upstream,
+    vol_t,
+    grad,
+    part,
+    field,
+    held,
+    shifts,
+    turned,
+    sem,
+    leave_sems,
+):
     first = pl.multiple_of(z * 18 * C, 18 * C)
     copy = fetched(weight.at[pl.ds(first, 9 * C), :], held, sem)
     shifted_columns([rows_of(halo)], field, 0, False)
@@ -165,6 +188,16 @@
         shifts[c, 0:COLS, :] = blank
         shifts[c, PADDED - COLS : PADDED, :] = blank
     copy.wait()
+    for owner in range(27, 32):
+        for group in range(4):
+            part[place(core, group, owner)] = jnp.zeros((CHUNK, C), F32)
+
+    def leave(i):
+        at = pl.multiple_of(i * TILE, TILE)
+        held_at = pl.ds(pl.multiple_of(at + COLS, COLS), TILE)
+        return pltpu.make_async_copy(
+            shifts.at[1, held_at, :], grad.at[pl.ds(at, TILE), :], leave_sems.at[i]
+        )
 
     def tile(i, carry):
         at = pl.multiple_of(i * TILE, TILE)
@@ -176,10 +209,10 @@
         s = jax.nn.sigmoid(preact)
         slopes = s * (1.0 + preact * (1.0 - s))
         here = (upstream[z, rows, :].astype(F32) * slopes).astype(BF)
-        grad[rows, :] = here
         wide = here.astype(F32)
         col = lax.broadcasted_iota(jnp.int32, (TILE, C), 0) & (COLS - 1)
         shifts[1, to, :] = here
+        leave(i).start()
         shifts[0, to, :] = jnp.where(col == 0, 0.0, pltpu.roll(wide, 1, 0)).astype(BF)
         shifts[2, to, :] = jnp.where(
             col == COLS - 1, 0.0, pltpu.roll(wide, TILE - 1, 0)
@@ -204,41 +237,28 @@
             for p in range(3):
                 for i in range(4):
                     chunk = 4 * tap(offset_of[p], b, c) + i
-                    at = p * C + i * CHUNK
-                    part[chunk + 5 * (chunk // 27)] = got[
-                        at : at + CHUNK, k * C : (k + 1) * C
-                    ]
-
-
-def near_kernel(
-    core_ref, halo, weight, inner, upstream, vol_t, grad, part, *scratch
-):
-    side(
-        1 - core_ref[0], halo, weight, inner, upstream, vol_t, grad, part, *scratch
-    )
-    for owner in range(27, 32):
-        for group in range(4):
-            part[group * 32 + owner] = jnp.zeros((CHUNK, C), F32)
+                    group = chunk // 27
+                    at = place(core, group, chunk - 27 * group)
+                    first = p * C + i * CHUNK
+                    block = got[first : first + CHUNK, k * C : (k + 1) * C]
+                    part[at] = block if begun is None else begun[at] + block
+    for i in range(CELLS // TILE):
+        leave(i).wait()
+
+
+def near_kernel(core_ref, *refs):
+    core = core_ref[0]
+    side(core, 1 - core, None, *refs)
 
 
 def far_kernel(
-    core_ref, halo, weight, inner, upstream, vol_t, near, grad, kept, sent, part, *scratch
+    core_ref, begun, halo, weight, inner, upstream, vol_t, grad, part, sent, *scratch
 ):
     core = core_ref[0]
-    side(core, halo, weight, inner, upstream, vol_t, grad, part, *scratch)
-    for owner in range(27, 32):
-        for group in range(4):
-            part[group * 32 + owner] = jnp.zeros((CHUNK, C), F32)
-
-    def share(owner, carry):
-        for group in range(4):
-            mine = group * 32 + core * 16 + owner
-            other = group * 32 + (1 - core) * 16 + owner
-            kept[owner * 4 + group] = part[mine] + near[mine]
-            sent[owner * 4 + group] = (part[other] + near[other]).astype(BF)
-        return carry
-
-    lax.fori_loop(0, 16, share, 0)
+    side(
+        core, core, begun, halo, weight, inner, upstream, vol_t, grad, part, *scratch
+    )
+    sent[...] = part[64:128].astype(BF)
 
 
 PLANE = jax.ShapeDtypeStruct((CELLS, C), BF)
@@ -249,6 +269,7 @@
     pltpu.VMEM((3, PADDED, C), BF),
     pltpu.VMEM((C, CELLS), BF),
     pltpu.SemaphoreType.DMA,
+    pltpu.SemaphoreType.DMA((CELLS // TILE,)),
 ]
 
 
@@ -257,7 +278,7 @@
         near_kernel,
         out_shape=[PLANE, jax.ShapeDtypeStruct(PART, F32)],
         in_specs=[SMEM, VMEM, HBM, VMEM, VMEM, VMEM],
-        out_specs=[VMEM, VMEM],
+        out_specs=[HBM, VMEM],
         scratch_shapes=SIDE,
         compiler_params=PARAMS,
         cost_estimate=cost(2 * CELLS * 3456 * 256, 5 << 20, CELLS * 128),
@@ -265,21 +286,37 @@
     )(core, halo, weight, inner, upstream, vol_t)
 
 
-def far_side(core, halo, weight, inner, upstream, vol_t, near):
+def far_side(core, begun, halo, weight, inner, upstream, vol_t):
     return pl.pallas_call(
         far_kernel,
         out_shape=[
             PLANE,
-            jax.ShapeDtypeStruct((64, CHUNK, C), F32),
+            jax.ShapeDtypeStruct(PART, F32),
             jax.ShapeDtypeStruct((64, CHUNK, C), BF),
         ],
-        in_specs=[SMEM, VMEM, HBM, VMEM, VMEM, VMEM, VMEM],
-        out_specs=[VMEM] * 3,
-        scratch_shapes=[pltpu.VMEM(PART, F32)] + SIDE,
+        in_specs=[SMEM, VMEM, VMEM, HBM, VMEM, VMEM, VMEM],
+        out_specs=[HBM, VMEM, VMEM],
+        scratch_shapes=SIDE,
         compiler_params=PARAMS,
         cost_estimate=cost(2 * CELLS * 3456 * 256, 5 << 20, CELLS * 128),
         name="far_side",
-    )(core, halo, weight, inner, upstream, vol_t, near)
+    )(core, begun, halo, weight, inner, upstream, vol_t)
+
+
+def halves_kernel(part, other, half):
+    half[...] = (part[0:64] + other[...].astype(F32)).astype(BF)
+
+
+def both_halves(part, other):
+    return pl.pallas_call(
+        halves_kernel,
+        out_shape=jax.ShapeDtypeStruct((64, CHUNK, C), BF),
+        in_specs=[VMEM, VMEM],
+        out_specs=VMEM,
+        compiler_params=SMALL,
+        cost_estimate=cost(1 << 18, 2 << 20),
+        name="both_halves",
+    )(part, other)
 
 
 def inner_back_kernel(
@@ -525,17 +562,17 @@
     up = upstream.reshape(2, CELLS, C)
     core = lax.axis_index("core")
     at_core = core.reshape(1)
-    near_halo, far_halo = from_neighbours(*both_planes(at_core, vol))
-    inner, vol_t = inner_conv(vol, weight)
+    near, far = both_planes(at_core, vol)
+    near_halo, far_halo = from_neighbours(near, far)
+    inner, vol_t = inner_conv(at_core, near, far, weight)
     near, part = near_side(at_core, near_halo, weight, inner, up, vol_t)
-    far, kept, sent = far_side(at_core, far_halo, weight, inner, up, vol_t, part)
+    far, part, sent = far_side(at_core, part, far_halo, weight, inner, up, vol_t)
 
     rows = first_moment.shape[0]
     other = lax.ppermute(sent, "core", [(0, 1), (1, 0)])
-    half = (kept + other.astype(F32)).astype(BF).reshape(16, 4, CHUNK, C)
-    near_sent, half = lax.optimization_barrier((near, half))
+    half = both_halves(part, other).reshape(16, 4, CHUNK, C)
     got = lax.all_to_all(half, ("x", "y"), 0, 0)
-    grad_near, grad_far = from_neighbours(near_sent, far)
+    grad_near, grad_far = from_neighbours(near, far)
     local = inner_back(at_core, near, far, weight, half)
     got, local = lax.optimization_barrier((got, local))
     part = mixed_rows(got)

time: 81.9 us -> 80.8 us (0.987)
  Pallas kernels: 35.7 us -> 37.2 us
  local copies, waits for them, and re-layouts: 3.64 us -> 2.41 us
  other arithmetic: 0.93 us -> 0 us
    unnamed x18 -> x14, local copies, waits for them, and re-layouts: 3.64 us -> 2.41 us
    pallas_call x1, Pallas kernels: 5.36 us -> 6.39 us  [near_side(): pl.pallas_call(near_kernel, out_shape=[PLANE, jax.ShapeDtypeStruct(PART,...]
    convert_element_type x1 -> x0, other arithmetic: 0.93 us -> none  [body(): half = (kept + other.astype(F32)).astype(BF).reshape(16, 4, CHUNK, C)]
    pallas_call x1 -> x2, Pallas kernels: 6.56 us -> 6.91 us  [the longest x1 6.02 us: far_side(): pl.pallas_call(far_kernel, out_shape=[PLANE, jax.ShapeDtypeStruct(PART, F...]
  transfers between devices with their start and end apart: 8 -> 8, of which waited for: 5 -> 5; matrix products, arithmetic and copies ran while one was open for 0% -> 0% of each run, Pallas kernels for 35% -> 38%
where the time goes in v7:
time: 80.8 us; the launch traced here: 80.2 us
  Pallas kernels  37.2 us (46%)
  starting transfers between devices  32.2 us (40%)
  waiting for transfers between devices  7.58 us (9%)
  local copies, waits for them, and re-layouts  2.41 us (3%)
  between operations  0.81 us (1%)
    pallas_call x2, Pallas kernels, outer_back(): pl.pallas_call(outer_back_kernel, out_shape=jax.ShapeDtypeStruct((2, CELL...  10.3 us
    all_to_all x1, starting transfers between devices, body(): got = lax.all_to_all(part, ('zl', 'sample'), 0, 0)  8.29 us
    all_to_all x1, starting transfers between devices, body(): whole = lax.all_to_all(step, ('core', 'x', 'y'), 0, 0)  7.66 us
    all_to_all x1, starting transfers between devices, body(): got = lax.all_to_all(half, ('x', 'y'), 0, 0)  6.71 us
    pallas_call x1, Pallas kernels, inner_back(): pl.pallas_call(inner_back_kernel, out_shape=jax.ShapeDtypeStruct((2, CELL...  6.7 us
    pallas_call x1, Pallas kernels, near_side(): pl.pallas_call(near_kernel, out_shape=[PLANE, jax.ShapeDtypeStruct(PART,...  6.39 us
    pallas_call x1, Pallas kernels, far_side(): pl.pallas_call(far_kernel, out_shape=[PLANE, jax.ShapeDtypeStruct(PART, F...  6.02 us
    ppermute x2, starting transfers between devices, from_neighbours(): far_halo = lax.ppermute(far, SPACE, pairs + [(j, i) for i, j in pairs])  5.65 us
  transfers between devices with their start and end apart: 8, of which 5 were waited for; matrix products, arithmetic and copies ran while one was open for 0% of the time, Pallas kernels for 38%

profile of v7, /device:TPU:1, one launch (start us, length us, event | category | flops | bytes accessed | tf_op | source)
XLA Modules:
  0.0 80.2 jit_solution(12899607638892902945)
XLA Ops:
  0.6 1.2 %copy-done.2 = bf16[1,2,32,64,128]{4,3,2,1,0:T(8,128)(2,1)S(1)} copy-done((bf16[1,2,32,64,128]{4,3,2,1,0:T(8,128)(2,1)S(1)}, bf16[1,2,32,64,128]{4,3,2,1,0:T(8,128)(2,1)}, u32[]{:S(2)}) %copy-start.2) | copy-done | bytes 1048600
  1.9 3.3 %collective-permute-start = (bf16[2048,128]{1,0:T(8,128)(2,1)S(1)}, bf16[2048,128]{1,0:T(8,128)(2,1)S(1)}, u32[]{:S(2)}, u32[]{:S(2)}) collective-permute-start(bf16[2048,128]{1,0:T(8,128)(2,1)S(1)} %get-tuple-element.17.near), channel_id=1, source_target_pairs={{0,4},{4,0},{1,5},{5,1},{2,6},{6,2},{3,7},{7,3},{8,12},{12,8},{9,1... | collective-permute-start | bytes 1572872 | tf_op jit(solution)/shard_map/ppermute | solution.py:556
  5.3 2.0 %collective-permute-start.1 = (bf16[2048,128]{1,0:T(8,128)(2,1)S(1)}, bf16[2048,128]{1,0:T(8,128)(2,1)S(1)}, u32[]{:S(2)}, u32[]{:S(2)}) collective-permute-start(bf16[2048,128]{1,0:T(8,128)(2,1)S(1)} %get-tuple-element.18.far), channel_id=1, source_target_pairs={{4,8},{12,16},{20,24},{28,32},{36,40},{44,48},{52,56},{60,64},{68,... | collective-permute-start | bytes 1572872 | tf_op jit(solution)/shard_map/ppermute | solution.py:555
  7.3 1.2 %copy-done.1 = bf16[3456,128]{1,0:T(8,128)(2,1)S(1)} copy-done((bf16[3456,128]{1,0:T(8,128)(2,1)S(1)}, bf16[3456,128]{1,0:T(8,128)(2,1)}, u32[]{:S(2)}) %copy-start.1) | copy-done | bytes 884760
  8.5 4.6 %inner_conv.1 = (f32[2,2048,128]{2,1,0:T(8,128)S(1)}, bf16[256,2048]{1,0:T(8,128)(2,1)S(1)}) custom-call(s32[1]{0:T(128)} %bitcast.core_ref.at_ref, bf16[2048,128]{1,0:T(8,128)(2,1)S(1)} %get-tuple-element.17.near, bf16[2048,128]{1,0:T(8,128)(2,1)S(1)} %get-tuple-element.18.far, bf16[3456,128]{1,0:T(8,128)(2,1)S(1)} %copy-done.1), custom_call_target="tpu_custom_call" | custom-call | flops 2415919104 | bytes 5242880 | tf_op jit(solution)/shard_map/inner_conv/pallas_call | solution.py:139
  13.1 6.4 %near_side.1 = (bf16[2048,128]{1,0:T(8,128)(2,1)S(1)}, f32[128,32,128]{2,1,0:T(8,128)S(1)}) custom-call(s32[1]{0:T(128)} %bitcast.core_ref.at_ref, bf16[2048,128]{1,0:T(8,128)(2,1)S(1)} %collective-permute-done.refs_0_, bf16[3456,128]{1,0:T(8,128)(2,1)S(1)} %copy-done.1, f32[2,2048,128]{2,1,0:T(8,128)S(1)} %get-tuple-element.19.refs_2_.inner, ...), custom_call_target="tpu_custom_call" | custom-call | flops 3623878656 | bytes 5242880 | tf_op jit(solution)/shard_map/near_side/pallas_call | solution.py:277
  19.5 0.7 collective-permute-done.1.halo
  20.1 6.0 %far_side.1 = (bf16[2048,128]{1,0:T(8,128)(2,1)}, f32[128,32,128]{2,1,0:T(8,128)S(1)}, bf16[64,32,128]{2,1,0:T(8,128)(2,1)S(1)}) custom-call(s32[1]{0:T(128)} %bitcast.core_ref.at_ref, f32[128,32,128]{2,1,0:T(8,128)S(1)} %get-tuple-element.21.begun, bf16[2048,128]{1,0:T(8,128)(2,1)S(1)} %collective-permute-done.1.halo, bf16[3456,128]{1,0:T(8,128)(2,1)S(1)} %copy-done.1, ...), custom_call_target="tpu_custom_call" | custom-call | flops 3623878656 | bytes 5242880 | tf_op jit(solution)/shard_map/far_side/pallas_call | solution.py:290
  26.3 0.5 collective-permute-start.4
  26.7 1.4 %collective-permute-done.3.other = bf16[64,32,128]{2,1,0:T(8,128)(2,1)S(1)} collective-permute-done((bf16[64,32,128]{2,1,0:T(8,128)(2,1)S(1)}, bf16[64,32,128]{2,1,0:T(8,128)(2,1)S(1)}, u32[]{:S(2)}, u32[]{:S(2)}) %collective-permute-start.3) | collective-permute-done | bytes 524320 | tf_op jit(solution)/shard_map/ppermute | solution.py:572
  28.1 0.9 %both_halves.1 = bf16[64,32,128]{2,1,0:T(8,128)(2,1)} custom-call(f32[128,32,128]{2,1,0:T(8,128)S(1)} %get-tuple-element.23.part, bf16[64,32,128]{2,1,0:T(8,128)(2,1)S(1)} %collective-permute-done.3.other), custom_call_target="tpu_custom_call" | custom-call | flops 262144 | bytes 2097152 | tf_op jit(solution)/shard_map/both_halves/pallas_call | solution.py:311
  29.0 6.7 %all-to-all-start = ((bf16[16,4,32,128]{3,2,1,0:T(8,128)(2,1)}), bf16[16,4,32,128]{3,2,1,0:T(8,128)(2,1)S(1)}, u32[]{:S(2)}, u32[]{:S(2)}) async-start(bf16[16,4,32,128]{3,2,1,0:T(8,128)(2,1)} %bitcast.3.later), calls=%async_computation | async-start | bytes 1048576 | tf_op jit(solution)/shard_map/all_to_all | solution.py:574
  35.8 3.6 %collective-permute-start.2 = (bf16[2048,128]{1,0:T(8,128)(2,1)}, bf16[2048,128]{1,0:T(8,128)(2,1)}, u32[]{:S(2)}, u32[]{:S(2)}) collective-permute-start(bf16[2048,128]{1,0:T(8,128)(2,1)} %get-tuple-element.22.far), channel_id=1, source_target_pairs={{4,8},{12,16},{20,24},{28,32},{36,40},{44,48},{52,56},{60,64},{68,... | collective-permute-start | bytes 1572872 | tf_op jit(solution)/shard_map/ppermute | solution.py:555
  39.4 6.7 %inner_back.1.kept = f32[2,2048,128]{2,1,0:T(8,128)} custom-call(s32[1]{0:T(128)} %bitcast.core_ref.at_ref, bf16[2048,128]{1,0:T(8,128)(2,1)} %copy-done.5, bf16[2048,128]{1,0:T(8,128)(2,1)} %get-tuple-element.22.far, bf16[3456,128]{1,0:T(8,128)(2,1)} %weight.9, bf16[16,4,32,128]{3,2,1,0:T(8,128)(2,1)} %bitcast.3.later), custom_call_target="tpu_custom_call" | custom-call | flops 2415919104 | bytes 5242880 | tf_op jit(solution)/shard_map/inner_back/pallas_call | solution.py:365
  46.1 0.4 all-to-all-done.got
  46.5 0.7 mixed_rows.1
  47.2 8.3 %all-to-all-start.1 = ((bf16[8,32,128]{2,1,0:T(8,128)(2,1)}), bf16[8,32,128]{2,1,0:T(8,128)(2,1)S(1)}, u32[]{:S(2)}, u32[]{:S(2)}) async-start(bf16[8,32,128]{2,1,0:T(8,128)(2,1)} %mixed_rows.1), calls=%async_computation.1 | async-start | bytes 131072 | tf_op jit(solution)/shard_map/all_to_all | solution.py:580
  55.5 5.2 %near_back.1.rest_0_ = bf16[2,2048,128]{2,1,0:T(8,128)(2,1)} custom-call(s32[1]{0:T(128)S(6)} %sub.3.at_ref, bf16[2048,128]{1,0:T(8,128)(2,1)} %copy-done.6, bf16[3456,128]{1,0:T(8,128)(2,1)} %weight.9, bf16[2,2048,128]{2,1,0:T(8,128)(2,1)} %bitcast.7, f32[2,2048,128]{2,1,0:T(8,128)} %inner_back.1.kept), custom_call_target="tpu_custom_call" | custom-call | flops 1207959552 | bytes 3145728 | tf_op jit(solution)/shard_map/near_back/pallas_call | solution.py:429
  60.7 1.4 %all-to-all-done.1.got = bf16[8,32,128]{2,1,0:T(8,128)(2,1)S(1)} async-done(((bf16[8,32,128]{2,1,0:T(8,128)(2,1)}), bf16[8,32,128]{2,1,0:T(8,128)(2,1)S(1)}, u32[]{:S(2)}, u32[]{:S(2)}) %all-to-all-start.1) | async-done | bytes 65568 | tf_op jit(solution)/shard_map/all_to_all | solution.py:580
  62.1 0.8 spread_step.1
  62.9 7.7 %all-to-all-start.2 = ((bf16[32,32,128]{2,1,0:T(8,128)(2,1)}), bf16[32,32,128]{2,1,0:T(8,128)(2,1)S(1)}, u32[]{:S(2)}, u32[]{:S(2)}) async-start(bf16[32,32,128]{2,1,0:T(8,128)(2,1)} %spread_step.1), calls=%async_computation.2 | async-start | bytes 524288 | tf_op jit(solution)/shard_map/all_to_all | solution.py:586
  70.5 5.1 %far_back.1 = bf16[2,2048,128]{2,1,0:T(8,128)(2,1)} custom-call(s32[1]{0:T(128)} %bitcast.core_ref.at_ref, bf16[2048,128]{1,0:T(8,128)(2,1)} %collective-permute-done.2.halo, bf16[3456,128]{1,0:T(8,128)(2,1)} %weight.9, bf16[2,2048,128]{2,1,0:T(8,128)(2,1)} %bitcast.8, f32[2,2048,128]{2,1,0:T(8,128)} %inner_back.1.kept, ...), custom_call_target="tpu_custom_call", output_to_operand_aliasing={{}: (5, {})} | custom-call | flops 1207959552 | bytes 3145728 | tf_op jit(solution)/shard_map/far_back/pallas_call | solution.py:429
  75.7 3.7 %all-to-all-done.2 = bf16[32,32,128]{2,1,0:T(8,128)(2,1)S(1)} async-done(((bf16[32,32,128]{2,1,0:T(8,128)(2,1)}), bf16[32,32,128]{2,1,0:T(8,128)(2,1)S(1)}, u32[]{:S(2)}, u32[]{:S(2)}) %all-to-all-start.2) | async-done | bytes 262176 | tf_op jit(solution)/shard_map/all_to_all | solution.py:586
  79.4 0.8 first_rows.1
  (17 shorter events, 0.2 us)
Async XLA Ops:
  0.6 1.2 %copy-start.2 = (bf16[1,2,32,64,128]{4,3,2,1,0:T(8,128)(2,1)S(1)}, bf16[1,2,32,64,128]{4,3,2,1,0:T(8,128)(2,1)}, u32[]{:S(2)}) copy-start(bf16[1,2,32,64,128]{4,3,2,1,0:T(8,128)(2,1)} %param.5) | copy-start | bytes 3145732
  1.9 11.1 %collective-permute-start = (bf16[2048,128]{1,0:T(8,128)(2,1)S(1)}, bf16[2048,128]{1,0:T(8,128)(2,1)S(1)}, u32[]{:S(2)}, u32[]{:S(2)}) collective-permute-start(bf16[2048,128]{1,0:T(8,128)(2,1)S(1)} %get-tuple-element.17.near), channel_id=1, source_target_pairs={{0,4},{4,0},{1,5},{5,1},{2,6},{6,2},{3,7},{7,3},{8,12},{12,8},{9,1... | collective-permute-start | bytes 1572872 | tf_op jit(solution)/shard_map/ppermute | solution.py:556
  5.3 7.8 %copy-start = (bf16[1,2,32,64,128]{4,3,2,1,0:T(8,128)(2,1)S(1)}, bf16[1,2,32,64,128]{4,3,2,1,0:T(8,128)(2,1)}, u32[]{:S(2)}) copy-start(bf16[1,2,32,64,128]{4,3,2,1,0:T(8,128)(2,1)} %param.6) | copy-start | bytes 3145732
  5.3 14.9 %collective-permute-start.1 = (bf16[2048,128]{1,0:T(8,128)(2,1)S(1)}, bf16[2048,128]{1,0:T(8,128)(2,1)S(1)}, u32[]{:S(2)}, u32[]{:S(2)}) collective-permute-start(bf16[2048,128]{1,0:T(8,128)(2,1)S(1)} %get-tuple-element.18.far), channel_id=1, source_target_pairs={{4,8},{12,16},{20,24},{28,32},{36,40},{44,48},{52,56},{60,64},{68,... | collective-permute-start | bytes 1572872 | tf_op jit(solution)/shard_map/ppermute | solution.py:555
  7.3 1.2 %copy-start.1 = (bf16[3456,128]{1,0:T(8,128)(2,1)S(1)}, bf16[3456,128]{1,0:T(8,128)(2,1)}, u32[]{:S(2)}) copy-start(bf16[3456,128]{1,0:T(8,128)(2,1)} %weight.9) | copy-start | bytes 2654212
  19.5 6.8 %copy-start.5 = (bf16[2048,128]{1,0:T(8,128)(2,1)}, bf16[2048,128]{1,0:T(8,128)(2,1)S(1)}, u32[]{:S(2)}) copy-start(bf16[2048,128]{1,0:T(8,128)(2,1)S(1)} %get-tuple-element.25.near) | copy-start | bytes 1572868
  26.1 2.0 %collective-permute-start.3 = (bf16[64,32,128]{2,1,0:T(8,128)(2,1)S(1)}, bf16[64,32,128]{2,1,0:T(8,128)(2,1)S(1)}, u32[]{:S(2)}, u32[]{:S(2)}) collective-permute-start(bf16[64,32,128]{2,1,0:T(8,128)(2,1)S(1)} %get-tuple-element.24), channel_id=1, source_target_pairs={{0,4},{4,0},{1,5},{5,1},{2,6},{6,2},{3,7},{7,3},{8,12},{12,8},{9,1... | collective-permute-start | bytes 1572872 | tf_op jit(solution)/shard_map/ppermute | solution.py:572
  26.3 20.9 %collective-permute-start.4 = (bf16[2048,128]{1,0:T(8,128)(2,1)S(1)}, bf16[2048,128]{1,0:T(8,128)(2,1)S(1)}, u32[]{:S(2)}, u32[]{:S(2)}) collective-permute-start(bf16[2048,128]{1,0:T(8,128)(2,1)S(1)} %get-tuple-element.25.near), channel_id=1, source_target_pairs={{0,4},{4,0},{1,5},{5,1},{2,6},{6,2},{3,7},{7,3},{8,12},{12,8},{9,1... | collective-permute-start | bytes 1572872 | tf_op jit(solution)/shard_map/ppermute | solution.py:556
  29.0 17.4 %all-to-all-start = ((bf16[16,4,32,128]{3,2,1,0:T(8,128)(2,1)}), bf16[16,4,32,128]{3,2,1,0:T(8,128)(2,1)S(1)}, u32[]{:S(2)}, u32[]{:S(2)}) async-start(bf16[16,4,32,128]{3,2,1,0:T(8,128)(2,1)} %bitcast.3.later), calls=%async_computation | async-start | bytes 1048576 | tf_op jit(solution)/shard_map/all_to_all | solution.py:574
  35.8 34.8 %collective-permute-start.2 = (bf16[2048,128]{1,0:T(8,128)(2,1)}, bf16[2048,128]{1,0:T(8,128)(2,1)}, u32[]{:S(2)}, u32[]{:S(2)}) collective-permute-start(bf16[2048,128]{1,0:T(8,128)(2,1)} %get-tuple-element.22.far), channel_id=1, source_target_pairs={{4,8},{12,16},{20,24},{28,32},{36,40},{44,48},{52,56},{60,64},{68,... | collective-permute-start | bytes 1572872 | tf_op jit(solution)/shard_map/ppermute | solution.py:555
  47.2 8.3 %copy-start.6 = (bf16[2048,128]{1,0:T(8,128)(2,1)}, bf16[2048,128]{1,0:T(8,128)(2,1)S(1)}, u32[]{:S(2)}) copy-start(bf16[2048,128]{1,0:T(8,128)(2,1)S(1)} %collective-permute-done.4.halo) | copy-start | bytes 1572868
  47.2 14.9 %all-to-all-start.1 = ((bf16[8,32,128]{2,1,0:T(8,128)(2,1)}), bf16[8,32,128]{2,1,0:T(8,128)(2,1)S(1)}, u32[]{:S(2)}, u32[]{:S(2)}) async-start(bf16[8,32,128]{2,1,0:T(8,128)(2,1)} %mixed_rows.1), calls=%async_computation.1 | async-start | bytes 131072 | tf_op jit(solution)/shard_map/all_to_all | solution.py:580
  55.5 6.6 %copy-start.3 = (f32[864,128]{1,0:T(8,128)S(1)}, f32[864,128]{1,0:T(8,128)}, u32[]{:S(2)}) copy-start(f32[864,128]{1,0:T(8,128)} %first.1) | copy-start | bytes 1327108
  55.5 6.6 %copy-start.4 = (f32[864,128]{1,0:T(8,128)S(1)}, f32[864,128]{1,0:T(8,128)}, u32[]{:S(2)}) copy-start(f32[864,128]{1,0:T(8,128)} %second.1) | copy-start | bytes 1327108
  62.9 16.5 %all-to-all-start.2 = ((bf16[32,32,128]{2,1,0:T(8,128)(2,1)}), bf16[32,32,128]{2,1,0:T(8,128)(2,1)S(1)}, u32[]{:S(2)}, u32[]{:S(2)}) async-start(bf16[32,32,128]{2,1,0:T(8,128)(2,1)} %spread_step.1), calls=%async_computation.2 | async-start | bytes 524288 | tf_op jit(solution)/shard_map/all_to_all | solution.py:586

commit v8 on v7

--- a/solution.py
+++ b/solution.py
@@ -130,7 +130,7 @@
         out[1, pl.ds(at, TILE), :] = got[:, C : 2 * C]
         return carry
 
-    lax.fori_loop(0, CELLS // TILE, tile, 0)
+    lax.fori_loop(0, CELLS // TILE, tile, 0, unroll=True)
     for p in range(2):
         transposed(planes[p], vol_t, p * C)
 
@@ -157,7 +157,7 @@
 
 
 def place(core, group, owner):
-    half = jnp.where(owner // 16 == core, 0, 64)
+    half = 0 if owner // 16 == core else 64
     return half + (owner % 16) * 4 + group
 
 
@@ -179,8 +179,8 @@
     sem,
     leave_sems,
 ):
-    first = pl.multiple_of(z * 18 * C, 18 * C)
-    copy = fetched(weight.at[pl.ds(first, 9 * C), :], held, sem)
+    first = z * 18 * C
+    copy = fetched(weight.at[first : first + 9 * C, :], held, sem)
     shifted_columns([rows_of(halo)], field, 0, False)
     transposed(rows_of(halo), turned, 0)
     blank = jnp.zeros((COLS, C), BF)
@@ -247,17 +247,34 @@
 
 
 def near_kernel(core_ref, *refs):
-    core = core_ref[0]
-    side(core, 1 - core, None, *refs)
+    for core in range(2):
+
+        @pl.when(core_ref[0] == core)
+        def _():
+            side(core, 1 - core, None, *refs)
 
 
 def far_kernel(
     core_ref, begun, halo, weight, inner, upstream, vol_t, grad, part, sent, *scratch
 ):
-    core = core_ref[0]
-    side(
-        core, core, begun, halo, weight, inner, upstream, vol_t, grad, part, *scratch
-    )
+    for core in range(2):
+
+        @pl.when(core_ref[0] == core)
+        def _():
+            side(
+                core,
+                core,
+                begun,
+                halo,
+                weight,
+                inner,
+                upstream,
+                vol_t,
+                grad,
+                part,
+                *scratch,
+            )
+
     sent[...] = part[64:128].astype(BF)
 
 
@@ -355,7 +372,7 @@
             leave(i, z).start()
         return carry
 
-    lax.fori_loop(0, tiles, tile, 0)
+    lax.fori_loop(0, tiles, tile, 0, unroll=True)
     for i in range(tiles):
         for z in range(2):
             leave(i, z).wait()
@@ -420,7 +437,7 @@
         leave(i).start()
         return carry
 
-    lax.fori_loop(0, tiles, tile, 0)
+    lax.fori_loop(0, tiles, tile, 0, unroll=True)
     for i in range(tiles):
         leave(i).wait()
 

time: 80.8 us -> 80.5 us (level)
  Pallas kernels: 37.2 us -> 33.4 us
  waiting for transfers between devices: 7.58 us -> 10.6 us
    ppermute x2, waiting for transfers between devices: 0.65 us -> 2.12 us  [from_neighbours(): far_halo = lax.ppermute(far, SPACE, pairs + [(j, i) for i, j in pairs])]
    pallas_call x2, Pallas kernels: 10.3 us -> 9.27 us  [outer_back(): pl.pallas_call(outer_back_kernel, out_shape=jax.ShapeDtypeStruct((2, CELL...]
    pallas_call x1, Pallas kernels: 4.55 us -> 3.66 us  [inner_conv(): pl.pallas_call(inner_kernel, out_shape=[jax.ShapeDtypeStruct((2, CELLS, C...]
  transfers between devices with their start and end apart: 8 -> 8, of which waited for: 5 -> 5; matrix products, arithmetic and copies ran while one was open for 0% -> 0% of each run, Pallas kernels for 38% -> 34%
where the time goes in v8:
time: 80.5 us; the launch traced here: 79.8 us
  Pallas kernels  33.4 us (41%)
  starting transfers between devices  32.4 us (40%)
  waiting for transfers between devices  10.6 us (13%)
  local copies, waits for them, and re-layouts  2.41 us (3%)
  between operations  0.97 us (1%)
    pallas_call x2, Pallas kernels, outer_back(): pl.pallas_call(outer_back_kernel, out_shape=jax.ShapeDtypeStruct((2, CELL...  9.27 us
    all_to_all x1, starting transfers between devices, body(): got = lax.all_to_all(part, ('zl', 'sample'), 0, 0)  8.17 us
    all_to_all x1, starting transfers between devices, body(): whole = lax.all_to_all(step, ('core', 'x', 'y'), 0, 0)  7.77 us
    all_to_all x1, starting transfers between devices, body(): got = lax.all_to_all(half, ('x', 'y'), 0, 0)  6.71 us
    pallas_call x1, Pallas kernels, inner_back(): pl.pallas_call(inner_back_kernel, out_shape=jax.ShapeDtypeStruct((2, CELL...  6.12 us
    pallas_call x1, Pallas kernels, near_side(): pl.pallas_call(near_kernel, out_shape=[PLANE, jax.ShapeDtypeStruct(PART,...  5.82 us
    ppermute x2, starting transfers between devices, from_neighbours(): far_halo = lax.ppermute(far, SPACE, pairs + [(j, i) for i, j in pairs])  5.65 us
    pallas_call x1, Pallas kernels, far_side(): pl.pallas_call(far_kernel, out_shape=[PLANE, jax.ShapeDtypeStruct(PART, F...  5.29 us
  transfers between devices with their start and end apart: 8, of which 5 were waited for; matrix products, arithmetic and copies ran while one was open for 0% of the time, Pallas kernels for 34%

profile of v8, /device:TPU:1, one launch (start us, length us, event | category | flops | bytes accessed | tf_op | source)
XLA Modules:
  0.0 79.8 jit_solution(11724991532676045145)
XLA Ops:
  0.6 1.2 %copy-done.2 = bf16[1,2,32,64,128]{4,3,2,1,0:T(8,128)(2,1)S(1)} copy-done((bf16[1,2,32,64,128]{4,3,2,1,0:T(8,128)(2,1)S(1)}, bf16[1,2,32,64,128]{4,3,2,1,0:T(8,128)(2,1)}, u32[]{:S(2)}) %copy-start.2) | copy-done | bytes 1048600
  1.9 3.3 %collective-permute-start = (bf16[2048,128]{1,0:T(8,128)(2,1)S(1)}, bf16[2048,128]{1,0:T(8,128)(2,1)S(1)}, u32[]{:S(2)}, u32[]{:S(2)}) collective-permute-start(bf16[2048,128]{1,0:T(8,128)(2,1)S(1)} %get-tuple-element.17.near), channel_id=1, source_target_pairs={{0,4},{4,0},{1,5},{5,1},{2,6},{6,2},{3,7},{7,3},{8,12},{12,8},{9,1... | collective-permute-start | bytes 1572872 | tf_op jit(solution)/shard_map/ppermute | solution.py:573
  5.3 2.0 %collective-permute-start.1 = (bf16[2048,128]{1,0:T(8,128)(2,1)S(1)}, bf16[2048,128]{1,0:T(8,128)(2,1)S(1)}, u32[]{:S(2)}, u32[]{:S(2)}) collective-permute-start(bf16[2048,128]{1,0:T(8,128)(2,1)S(1)} %get-tuple-element.18.far), channel_id=1, source_target_pairs={{4,8},{12,16},{20,24},{28,32},{36,40},{44,48},{52,56},{60,64},{68,... | collective-permute-start | bytes 1572872 | tf_op jit(solution)/shard_map/ppermute | solution.py:572
  7.3 1.2 %copy-done.1 = bf16[3456,128]{1,0:T(8,128)(2,1)S(1)} copy-done((bf16[3456,128]{1,0:T(8,128)(2,1)S(1)}, bf16[3456,128]{1,0:T(8,128)(2,1)}, u32[]{:S(2)}) %copy-start.1) | copy-done | bytes 884760
  8.5 3.7 %inner_conv.1 = (f32[2,2048,128]{2,1,0:T(8,128)S(1)}, bf16[256,2048]{1,0:T(8,128)(2,1)S(1)}) custom-call(s32[1]{0:T(128)} %bitcast.core_ref.at_ref, bf16[2048,128]{1,0:T(8,128)(2,1)S(1)} %get-tuple-element.17.near, bf16[2048,128]{1,0:T(8,128)(2,1)S(1)} %get-tuple-element.18.far, bf16[3456,128]{1,0:T(8,128)(2,1)S(1)} %copy-done.1), custom_call_target="tpu_custom_call" | custom-call | flops 2415919104 | bytes 5242880 | tf_op jit(solution)/shard_map/inner_conv/pallas_call | solution.py:139
  12.2 5.8 %near_side.1 = (bf16[2048,128]{1,0:T(8,128)(2,1)S(1)}, f32[128,32,128]{2,1,0:T(8,128)S(1)}) custom-call(s32[1]{0:T(128)} %bitcast.core_ref.at_ref, bf16[2048,128]{1,0:T(8,128)(2,1)S(1)} %collective-permute-done.refs_0_, bf16[3456,128]{1,0:T(8,128)(2,1)S(1)} %copy-done.1, f32[2,2048,128]{2,1,0:T(8,128)S(1)} %get-tuple-element.19.refs_2_.inner, ...), custom_call_target="tpu_custom_call" | custom-call | flops 3623878656 | bytes 5242880 | tf_op jit(solution)/shard_map/near_side/pallas_call | solution.py:294
  18.0 2.1 %collective-permute-done.1.halo = bf16[2048,128]{1,0:T(8,128)(2,1)S(1)} collective-permute-done((bf16[2048,128]{1,0:T(8,128)(2,1)S(1)}, bf16[2048,128]{1,0:T(8,128)(2,1)S(1)}, u32[]{:S(2)}, u32[]{:S(2)}) %collective-permute-start.1) | collective-permute-done | bytes 524320 | tf_op jit(solution)/shard_map/ppermute | solution.py:572
  20.1 5.3 %far_side.1 = (bf16[2048,128]{1,0:T(8,128)(2,1)}, f32[128,32,128]{2,1,0:T(8,128)S(1)}, bf16[64,32,128]{2,1,0:T(8,128)(2,1)S(1)}) custom-call(s32[1]{0:T(128)} %bitcast.core_ref.at_ref, f32[128,32,128]{2,1,0:T(8,128)S(1)} %get-tuple-element.21.begun, bf16[2048,128]{1,0:T(8,128)(2,1)S(1)} %collective-permute-done.1.halo, bf16[3456,128]{1,0:T(8,128)(2,1)S(1)} %copy-done.1, ...), custom_call_target="tpu_custom_call" | custom-call | flops 3623878656 | bytes 5242880 | tf_op jit(solution)/shard_map/far_side/pallas_call | solution.py:307
  25.7 0.5 collective-permute-start.4
  26.2 1.4 %collective-permute-done.3.other = bf16[64,32,128]{2,1,0:T(8,128)(2,1)S(1)} collective-permute-done((bf16[64,32,128]{2,1,0:T(8,128)(2,1)S(1)}, bf16[64,32,128]{2,1,0:T(8,128)(2,1)S(1)}, u32[]{:S(2)}, u32[]{:S(2)}) %collective-permute-start.3) | collective-permute-done | bytes 524320 | tf_op jit(solution)/shard_map/ppermute | solution.py:589
  27.6 0.9 %both_halves.1 = bf16[64,32,128]{2,1,0:T(8,128)(2,1)} custom-call(f32[128,32,128]{2,1,0:T(8,128)S(1)} %get-tuple-element.23.part, bf16[64,32,128]{2,1,0:T(8,128)(2,1)S(1)} %collective-permute-done.3.other), custom_call_target="tpu_custom_call" | custom-call | flops 262144 | bytes 2097152 | tf_op jit(solution)/shard_map/both_halves/pallas_call | solution.py:328
  28.5 6.7 %all-to-all-start = ((bf16[16,4,32,128]{3,2,1,0:T(8,128)(2,1)}), bf16[16,4,32,128]{3,2,1,0:T(8,128)(2,1)S(1)}, u32[]{:S(2)}, u32[]{:S(2)}) async-start(bf16[16,4,32,128]{3,2,1,0:T(8,128)(2,1)} %bitcast.3.later), calls=%async_computation | async-start | bytes 1048576 | tf_op jit(solution)/shard_map/all_to_all | solution.py:591
  35.2 3.6 %collective-permute-start.2 = (bf16[2048,128]{1,0:T(8,128)(2,1)}, bf16[2048,128]{1,0:T(8,128)(2,1)}, u32[]{:S(2)}, u32[]{:S(2)}) collective-permute-start(bf16[2048,128]{1,0:T(8,128)(2,1)} %get-tuple-element.22.far), channel_id=1, source_target_pairs={{4,8},{12,16},{20,24},{28,32},{36,40},{44,48},{52,56},{60,64},{68,... | collective-permute-start | bytes 1572872 | tf_op jit(solution)/shard_map/ppermute | solution.py:572
  38.8 6.1 %inner_back.1.kept = f32[2,2048,128]{2,1,0:T(8,128)} custom-call(s32[1]{0:T(128)} %bitcast.core_ref.at_ref, bf16[2048,128]{1,0:T(8,128)(2,1)} %copy-done.5, bf16[2048,128]{1,0:T(8,128)(2,1)} %get-tuple-element.22.far, bf16[3456,128]{1,0:T(8,128)(2,1)} %weight.9, bf16[16,4,32,128]{3,2,1,0:T(8,128)(2,1)} %bitcast.3.later), custom_call_target="tpu_custom_call" | custom-call | flops 2415919104 | bytes 5242880 | tf_op jit(solution)/shard_map/inner_back/pallas_call | solution.py:382
  45.0 1.0 %all-to-all-done.got = bf16[16,4,32,128]{3,2,1,0:T(8,128)(2,1)S(1)} async-done(((bf16[16,4,32,128]{3,2,1,0:T(8,128)(2,1)}), bf16[16,4,32,128]{3,2,1,0:T(8,128)(2,1)S(1)}, u32[]{:S(2)}, u32[]{:S(2)}) %all-to-all-start) | async-done | bytes 524320 | tf_op jit(solution)/shard_map/all_to_all | solution.py:591
  45.9 0.7 mixed_rows.1
  46.6 8.2 %all-to-all-start.1 = ((bf16[8,32,128]{2,1,0:T(8,128)(2,1)}), bf16[8,32,128]{2,1,0:T(8,128)(2,1)S(1)}, u32[]{:S(2)}, u32[]{:S(2)}) async-start(bf16[8,32,128]{2,1,0:T(8,128)(2,1)} %mixed_rows.1), calls=%async_computation.1 | async-start | bytes 131072 | tf_op jit(solution)/shard_map/all_to_all | solution.py:597
  54.8 4.7 %near_back.1.rest_0_ = bf16[2,2048,128]{2,1,0:T(8,128)(2,1)} custom-call(s32[1]{0:T(128)S(6)} %sub.3.at_ref, bf16[2048,128]{1,0:T(8,128)(2,1)} %copy-done.6, bf16[3456,128]{1,0:T(8,128)(2,1)} %weight.9, bf16[2,2048,128]{2,1,0:T(8,128)(2,1)} %bitcast.7, f32[2,2048,128]{2,1,0:T(8,128)} %inner_back.1.kept), custom_call_target="tpu_custom_call" | custom-call | flops 1207959552 | bytes 3145728 | tf_op jit(solution)/shard_map/near_back/pallas_call | solution.py:446
  59.5 1.9 %all-to-all-done.1.got = bf16[8,32,128]{2,1,0:T(8,128)(2,1)S(1)} async-done(((bf16[8,32,128]{2,1,0:T(8,128)(2,1)}), bf16[8,32,128]{2,1,0:T(8,128)(2,1)S(1)}, u32[]{:S(2)}, u32[]{:S(2)}) %all-to-all-start.1) | async-done | bytes 65568 | tf_op jit(solution)/shard_map/all_to_all | solution.py:597
  61.5 0.8 spread_step.1
  62.2 7.8 %all-to-all-start.2 = ((bf16[32,32,128]{2,1,0:T(8,128)(2,1)}), bf16[32,32,128]{2,1,0:T(8,128)(2,1)S(1)}, u32[]{:S(2)}, u32[]{:S(2)}) async-start(bf16[32,32,128]{2,1,0:T(8,128)(2,1)} %spread_step.1), calls=%async_computation.2 | async-start | bytes 524288 | tf_op jit(solution)/shard_map/all_to_all | solution.py:603
  70.0 4.6 %far_back.1 = bf16[2,2048,128]{2,1,0:T(8,128)(2,1)} custom-call(s32[1]{0:T(128)} %bitcast.core_ref.at_ref, bf16[2048,128]{1,0:T(8,128)(2,1)} %collective-permute-done.2.halo, bf16[3456,128]{1,0:T(8,128)(2,1)} %weight.9, bf16[2,2048,128]{2,1,0:T(8,128)(2,1)} %bitcast.8, f32[2,2048,128]{2,1,0:T(8,128)} %inner_back.1.kept, ...), custom_call_target="tpu_custom_call", output_to_operand_aliasing={{}: (5, {})} | custom-call | flops 1207959552 | bytes 3145728 | tf_op jit(solution)/shard_map/far_back/pallas_call | solution.py:446
  74.6 4.2 %all-to-all-done.2 = bf16[32,32,128]{2,1,0:T(8,128)(2,1)S(1)} async-done(((bf16[32,32,128]{2,1,0:T(8,128)(2,1)}), bf16[32,32,128]{2,1,0:T(8,128)(2,1)S(1)}, u32[]{:S(2)}, u32[]{:S(2)}) %all-to-all-start.2) | async-done | bytes 262176 | tf_op jit(solution)/shard_map/all_to_all | solution.py:603
  78.8 0.8 first_rows.1
  (17 shorter events, 0.4 us)
Async XLA Ops:
  0.6 1.2 %copy-start.2 = (bf16[1,2,32,64,128]{4,3,2,1,0:T(8,128)(2,1)S(1)}, bf16[1,2,32,64,128]{4,3,2,1,0:T(8,128)(2,1)}, u32[]{:S(2)}) copy-start(bf16[1,2,32,64,128]{4,3,2,1,0:T(8,128)(2,1)} %param.5) | copy-start | bytes 3145732
  1.9 10.2 %collective-permute-start = (bf16[2048,128]{1,0:T(8,128)(2,1)S(1)}, bf16[2048,128]{1,0:T(8,128)(2,1)S(1)}, u32[]{:S(2)}, u32[]{:S(2)}) collective-permute-start(bf16[2048,128]{1,0:T(8,128)(2,1)S(1)} %get-tuple-element.17.near), channel_id=1, source_target_pairs={{0,4},{4,0},{1,5},{5,1},{2,6},{6,2},{3,7},{7,3},{8,12},{12,8},{9,1... | collective-permute-start | bytes 1572872 | tf_op jit(solution)/shard_map/ppermute | solution.py:573
  5.3 6.9 %copy-start = (bf16[1,2,32,64,128]{4,3,2,1,0:T(8,128)(2,1)S(1)}, bf16[1,2,32,64,128]{4,3,2,1,0:T(8,128)(2,1)}, u32[]{:S(2)}) copy-start(bf16[1,2,32,64,128]{4,3,2,1,0:T(8,128)(2,1)} %param.6) | copy-start | bytes 3145732
  5.3 14.9 %collective-permute-start.1 = (bf16[2048,128]{1,0:T(8,128)(2,1)S(1)}, bf16[2048,128]{1,0:T(8,128)(2,1)S(1)}, u32[]{:S(2)}, u32[]{:S(2)}) collective-permute-start(bf16[2048,128]{1,0:T(8,128)(2,1)S(1)} %get-tuple-element.18.far), channel_id=1, source_target_pairs={{4,8},{12,16},{20,24},{28,32},{36,40},{44,48},{52,56},{60,64},{68,... | collective-permute-start | bytes 1572872 | tf_op jit(solution)/shard_map/ppermute | solution.py:572
  7.3 1.2 %copy-start.1 = (bf16[3456,128]{1,0:T(8,128)(2,1)S(1)}, bf16[3456,128]{1,0:T(8,128)(2,1)}, u32[]{:S(2)}) copy-start(bf16[3456,128]{1,0:T(8,128)(2,1)} %weight.9) | copy-start | bytes 2654212
  18.0 7.7 %copy-start.5 = (bf16[2048,128]{1,0:T(8,128)(2,1)}, bf16[2048,128]{1,0:T(8,128)(2,1)S(1)}, u32[]{:S(2)}) copy-start(bf16[2048,128]{1,0:T(8,128)(2,1)S(1)} %get-tuple-element.25.near) | copy-start | bytes 1572868
  25.4 2.2 %collective-permute-start.3 = (bf16[64,32,128]{2,1,0:T(8,128)(2,1)S(1)}, bf16[64,32,128]{2,1,0:T(8,128)(2,1)S(1)}, u32[]{:S(2)}, u32[]{:S(2)}) collective-permute-start(bf16[64,32,128]{2,1,0:T(8,128)(2,1)S(1)} %get-tuple-element.24), channel_id=1, source_target_pairs={{0,4},{4,0},{1,5},{5,1},{2,6},{6,2},{3,7},{7,3},{8,12},{12,8},{9,1... | collective-permute-start | bytes 1572872 | tf_op jit(solution)/shard_map/ppermute | solution.py:589
  25.7 20.9 %collective-permute-start.4 = (bf16[2048,128]{1,0:T(8,128)(2,1)S(1)}, bf16[2048,128]{1,0:T(8,128)(2,1)S(1)}, u32[]{:S(2)}, u32[]{:S(2)}) collective-permute-start(bf16[2048,128]{1,0:T(8,128)(2,1)S(1)} %get-tuple-element.25.near), channel_id=1, source_target_pairs={{0,4},{4,0},{1,5},{5,1},{2,6},{6,2},{3,7},{7,3},{8,12},{12,8},{9,1... | collective-permute-start | bytes 1572872 | tf_op jit(solution)/shard_map/ppermute | solution.py:573
  28.5 17.4 %all-to-all-start = ((bf16[16,4,32,128]{3,2,1,0:T(8,128)(2,1)}), bf16[16,4,32,128]{3,2,1,0:T(8,128)(2,1)S(1)}, u32[]{:S(2)}, u32[]{:S(2)}) async-start(bf16[16,4,32,128]{3,2,1,0:T(8,128)(2,1)} %bitcast.3.later), calls=%async_computation | async-start | bytes 1048576 | tf_op jit(solution)/shard_map/all_to_all | solution.py:591
  35.2 34.8 %collective-permute-start.2 = (bf16[2048,128]{1,0:T(8,128)(2,1)}, bf16[2048,128]{1,0:T(8,128)(2,1)}, u32[]{:S(2)}, u32[]{:S(2)}) collective-permute-start(bf16[2048,128]{1,0:T(8,128)(2,1)} %get-tuple-element.22.far), channel_id=1, source_target_pairs={{4,8},{12,16},{20,24},{28,32},{36,40},{44,48},{52,56},{60,64},{68,... | collective-permute-start | bytes 1572872 | tf_op jit(solution)/shard_map/ppermute | solution.py:572
  46.6 8.2 %copy-start.6 = (bf16[2048,128]{1,0:T(8,128)(2,1)}, bf16[2048,128]{1,0:T(8,128)(2,1)S(1)}, u32[]{:S(2)}) copy-start(bf16[2048,128]{1,0:T(8,128)(2,1)S(1)} %collective-permute-done.4.halo) | copy-start | bytes 1572868
  46.6 14.8 %all-to-all-start.1 = ((bf16[8,32,128]{2,1,0:T(8,128)(2,1)}), bf16[8,32,128]{2,1,0:T(8,128)(2,1)S(1)}, u32[]{:S(2)}, u32[]{:S(2)}) async-start(bf16[8,32,128]{2,1,0:T(8,128)(2,1)} %mixed_rows.1), calls=%async_computation.1 | async-start | bytes 131072 | tf_op jit(solution)/shard_map/all_to_all | solution.py:597
  54.8 6.6 %copy-start.3 = (f32[864,128]{1,0:T(8,128)S(1)}, f32[864,128]{1,0:T(8,128)}, u32[]{:S(2)}) copy-start(f32[864,128]{1,0:T(8,128)} %first.1) | copy-start | bytes 1327108
  54.8 6.6 %copy-start.4 = (f32[864,128]{1,0:T(8,128)S(1)}, f32[864,128]{1,0:T(8,128)}, u32[]{:S(2)}) copy-start(f32[864,128]{1,0:T(8,128)} %second.1) | copy-start | bytes 1327108
  62.2 16.6 %all-to-all-start.2 = ((bf16[32,32,128]{2,1,0:T(8,128)(2,1)}), bf16[32,32,128]{2,1,0:T(8,128)(2,1)S(1)}, u32[]{:S(2)}, u32[]{:S(2)}) async-start(bf16[32,32,128]{2,1,0:T(8,128)(2,1)} %spread_step.1), calls=%async_computation.2 | async-start | bytes 524288 | tf_op jit(solution)/shard_map/all_to_all | solution.py:603

commit v9 on v8

--- a/solution.py
+++ b/solution.py
@@ -320,8 +320,16 @@
     )(core, begun, halo, weight, inner, upstream, vol_t)
 
 
-def halves_kernel(part, other, half):
-    half[...] = (part[0:64] + other[...].astype(F32)).astype(BF)
+def halves_kernel(part, other, half, held, sems):
+    copies = []
+    for k in range(4):
+        rows = slice(k * 16, (k + 1) * 16)
+        held[rows] = (part[rows] + other[rows].astype(F32)).astype(BF)
+        copy = pltpu.make_async_copy(held.at[rows], half.at[rows], sems.at[k])
+        copy.start()
+        copies.append(copy)
+    for copy in copies:
+        copy.wait()
 
 
 def both_halves(part, other):
@@ -329,7 +337,11 @@
         halves_kernel,
         out_shape=jax.ShapeDtypeStruct((64, CHUNK, C), BF),
         in_specs=[VMEM, VMEM],
-        out_specs=VMEM,
+        out_specs=HBM,
+        scratch_shapes=[
+            pltpu.VMEM((64, CHUNK, C), BF),
+            pltpu.SemaphoreType.DMA((4,)),
+        ],
         compiler_params=SMALL,
         cost_estimate=cost(1 << 18, 2 << 20),
         name="both_halves",
@@ -589,8 +601,9 @@
     other = lax.ppermute(sent, "core", [(0, 1), (1, 0)])
     half = both_halves(part, other).reshape(16, 4, CHUNK, C)
     got = lax.all_to_all(half, ("x", "y"), 0, 0)
-    grad_near, grad_far = from_neighbours(near, far)
     local = inner_back(at_core, near, far, weight, half)
+    far_sent, local = lax.optimization_barrier((far, local))
+    grad_near, grad_far = from_neighbours(near, far_sent)
     got, local = lax.optimization_barrier((got, local))
     part = mixed_rows(got)
     grad_near, part = lax.optimization_barrier((grad_near, part))

time: 80.5 us -> 83.6 us (1.039)
  starting transfers between devices: 32.4 us -> 35.4 us
    all_to_all x1, starting transfers between devices: 7.77 us -> 10.7 us  [body(): whole = lax.all_to_all(step, ('core', 'x', 'y'), 0, 0)]
    unnamed x14 -> x18, local copies, waits for them, and re-layouts: 2.41 us -> 2.42 us
  transfers between devices with their start and end apart: 8 -> 8, of which waited for: 5 -> 5; matrix products, arithmetic and copies ran while one was open for 0% -> 0% of each run, Pallas kernels for 34% -> 33%
where the time goes in v9:
time: 83.6 us; the launch traced here: 83 us
  starting transfers between devices  35.4 us (42%)
  Pallas kernels  34 us (41%)
  waiting for transfers between devices  10.2 us (12%)
  local copies, waits for them, and re-layouts  2.42 us (3%)
  between operations  1.01 us (1%)
    all_to_all x1, starting transfers between devices, body(): whole = lax.all_to_all(step, ('core', 'x', 'y'), 0, 0)  10.7 us
    pallas_call x2, Pallas kernels, outer_back(): pl.pallas_call(outer_back_kernel, out_shape=jax.ShapeDtypeStruct((2, CELL...  9.27 us
    all_to_all x1, starting transfers between devices, body(): got = lax.all_to_all(part, ('zl', 'sample'), 0, 0)  8.19 us
    all_to_all x1, starting transfers between devices, body(): got = lax.all_to_all(half, ('x', 'y'), 0, 0)  6.72 us
    pallas_call x1, Pallas kernels, inner_back(): pl.pallas_call(inner_back_kernel, out_shape=jax.ShapeDtypeStruct((2, CELL...  6.17 us
    pallas_call x1, Pallas kernels, far_side(): pl.pallas_call(far_kernel, out_shape=[PLANE, jax.ShapeDtypeStruct(PART, F...  5.87 us
    pallas_call x1, Pallas kernels, near_side(): pl.pallas_call(near_kernel, out_shape=[PLANE, jax.ShapeDtypeStruct(PART,...  5.82 us
    ppermute x2, starting transfers between devices, from_neighbours(): far_halo = lax.ppermute(far, SPACE, pairs + [(j, i) for i, j in pairs])  5.67 us
  transfers between devices with their start and end apart: 8, of which 5 were waited for; matrix products, arithmetic and copies ran while one was open for 0% of the time, Pallas kernels for 33%

profile of v9, /device:TPU:1, one launch (start us, length us, event | category | flops | bytes accessed | tf_op | source)
XLA Modules:
  0.0 83.0 jit_solution(6136787056384291688)
XLA Ops:
  0.6 1.2 %copy-done.2 = bf16[1,2,32,64,128]{4,3,2,1,0:T(8,128)(2,1)S(1)} copy-done((bf16[1,2,32,64,128]{4,3,2,1,0:T(8,128)(2,1)S(1)}, bf16[1,2,32,64,128]{4,3,2,1,0:T(8,128)(2,1)}, u32[]{:S(2)}) %copy-start.2) | copy-done | bytes 1048600
  1.9 3.3 %collective-permute-start = (bf16[2048,128]{1,0:T(8,128)(2,1)S(1)}, bf16[2048,128]{1,0:T(8,128)(2,1)S(1)}, u32[]{:S(2)}, u32[]{:S(2)}) collective-permute-start(bf16[2048,128]{1,0:T(8,128)(2,1)S(1)} %get-tuple-element.19.near), channel_id=1, source_target_pairs={{0,4},{4,0},{1,5},{5,1},{2,6},{6,2},{3,7},{7,3},{8,12},{12,8},{9,1... | collective-permute-start | bytes 1572872 | tf_op jit(solution)/shard_map/ppermute | solution.py:585
  5.3 2.0 %collective-permute-start.1 = (bf16[2048,128]{1,0:T(8,128)(2,1)S(1)}, bf16[2048,128]{1,0:T(8,128)(2,1)S(1)}, u32[]{:S(2)}, u32[]{:S(2)}) collective-permute-start(bf16[2048,128]{1,0:T(8,128)(2,1)S(1)} %get-tuple-element.20.far), channel_id=1, source_target_pairs={{4,8},{12,16},{20,24},{28,32},{36,40},{44,48},{52,56},{60,64},{68,... | collective-permute-start | bytes 1572872 | tf_op jit(solution)/shard_map/ppermute | solution.py:584
  7.3 1.2 %copy-done.1 = bf16[3456,128]{1,0:T(8,128)(2,1)S(1)} copy-done((bf16[3456,128]{1,0:T(8,128)(2,1)S(1)}, bf16[3456,128]{1,0:T(8,128)(2,1)}, u32[]{:S(2)}) %copy-start.1) | copy-done | bytes 884760
  8.5 3.7 %inner_conv.1 = (f32[2,2048,128]{2,1,0:T(8,128)S(1)}, bf16[256,2048]{1,0:T(8,128)(2,1)S(1)}) custom-call(s32[1]{0:T(128)} %bitcast.core_ref.at_ref, bf16[2048,128]{1,0:T(8,128)(2,1)S(1)} %get-tuple-element.19.near, bf16[2048,128]{1,0:T(8,128)(2,1)S(1)} %get-tuple-element.20.far, bf16[3456,128]{1,0:T(8,128)(2,1)S(1)} %copy-done.1), custom_call_target="tpu_custom_call" | custom-call | flops 2415919104 | bytes 5242880 | tf_op jit(solution)/shard_map/inner_conv/pallas_call | solution.py:139
  12.2 5.8 %near_side.1 = (bf16[2048,128]{1,0:T(8,128)(2,1)S(1)}, f32[128,32,128]{2,1,0:T(8,128)S(1)}) custom-call(s32[1]{0:T(128)} %bitcast.core_ref.at_ref, bf16[2048,128]{1,0:T(8,128)(2,1)S(1)} %collective-permute-done.refs_0_, bf16[3456,128]{1,0:T(8,128)(2,1)S(1)} %copy-done.1, f32[2,2048,128]{2,1,0:T(8,128)S(1)} %get-tuple-element.21.refs_2_.inner, ...), custom_call_target="tpu_custom_call" | custom-call | flops 3623878656 | bytes 5242880 | tf_op jit(solution)/shard_map/near_side/pallas_call | solution.py:294
  18.0 2.1 %collective-permute-done.1.halo = bf16[2048,128]{1,0:T(8,128)(2,1)S(1)} collective-permute-done((bf16[2048,128]{1,0:T(8,128)(2,1)S(1)}, bf16[2048,128]{1,0:T(8,128)(2,1)S(1)}, u32[]{:S(2)}, u32[]{:S(2)}) %collective-permute-start.1) | collective-permute-done | bytes 524320 | tf_op jit(solution)/shard_map/ppermute | solution.py:584
  20.1 5.9 %far_side.1 = (bf16[2048,128]{1,0:T(8,128)(2,1)S(1)}, f32[128,32,128]{2,1,0:T(8,128)S(1)}, bf16[64,32,128]{2,1,0:T(8,128)(2,1)S(1)}) custom-call(s32[1]{0:T(128)} %bitcast.core_ref.at_ref, f32[128,32,128]{2,1,0:T(8,128)S(1)} %get-tuple-element.23.begun, bf16[2048,128]{1,0:T(8,128)(2,1)S(1)} %collective-permute-done.1.halo, bf16[3456,128]{1,0:T(8,128)(2,1)S(1)} %copy-done.1, ...), custom_call_target="tpu_custom_call" | custom-call | flops 3623878656 | bytes 5242880 | tf_op jit(solution)/shard_map/far_side/pallas_call | solution.py:307
  26.3 0.5 collective-permute-start.4
  26.8 1.4 %collective-permute-done.2.other = bf16[64,32,128]{2,1,0:T(8,128)(2,1)S(1)} collective-permute-done((bf16[64,32,128]{2,1,0:T(8,128)(2,1)S(1)}, bf16[64,32,128]{2,1,0:T(8,128)(2,1)S(1)}, u32[]{:S(2)}, u32[]{:S(2)}) %collective-permute-start.2) | collective-permute-done | bytes 524320 | tf_op jit(solution)/shard_map/ppermute | solution.py:601
  28.2 0.9 %both_halves.1 = bf16[64,32,128]{2,1,0:T(8,128)(2,1)} custom-call(f32[128,32,128]{2,1,0:T(8,128)S(1)} %get-tuple-element.26.part, bf16[64,32,128]{2,1,0:T(8,128)(2,1)S(1)} %collective-permute-done.2.other), custom_call_target="tpu_custom_call" | custom-call | flops 262144 | bytes 2097152 | tf_op jit(solution)/shard_map/both_halves/pallas_call | solution.py:336
  29.1 6.7 %all-to-all-start = ((bf16[16,4,32,128]{3,2,1,0:T(8,128)(2,1)}), bf16[16,4,32,128]{3,2,1,0:T(8,128)(2,1)S(1)}, u32[]{:S(2)}, u32[]{:S(2)}) async-start(bf16[16,4,32,128]{3,2,1,0:T(8,128)(2,1)} %bitcast.3.later), calls=%async_computation | async-start | bytes 1048576 | tf_op jit(solution)/shard_map/all_to_all | solution.py:603
  35.8 6.2 %inner_back.1.kept = f32[2,2048,128]{2,1,0:T(8,128)} custom-call(s32[1]{0:T(128)} %bitcast.core_ref.at_ref, bf16[2048,128]{1,0:T(8,128)(2,1)} %copy-done.7, bf16[2048,128]{1,0:T(8,128)(2,1)} %copy-done.5, bf16[3456,128]{1,0:T(8,128)(2,1)} %weight.9, bf16[16,4,32,128]{3,2,1,0:T(8,128)(2,1)} %bitcast.3.later), custom_call_target="tpu_custom_call" | custom-call | flops 2415919104 | bytes 5242880 | tf_op jit(solution)/shard_map/inner_back/pallas_call | solution.py:394
  42.0 3.6 %collective-permute-start.3 = (bf16[2048,128]{1,0:T(8,128)(2,1)S(1)}, bf16[2048,128]{1,0:T(8,128)(2,1)}, u32[]{:S(2)}, u32[]{:S(2)}) collective-permute-start(bf16[2048,128]{1,0:T(8,128)(2,1)S(1)} %copy-done.6), channel_id=1, source_target_pairs={{4,8},{12,16},{20,24},{28,32},{36,40},{44,48},{52,56},{60,64},{68,... | collective-permute-start | bytes 1572872 | tf_op jit(solution)/shard_map/ppermute | solution.py:584
  45.6 0.5 all-to-all-done.got
  46.2 0.7 mixed_rows.1
  46.9 8.2 %all-to-all-start.1 = ((bf16[8,32,128]{2,1,0:T(8,128)(2,1)}), bf16[8,32,128]{2,1,0:T(8,128)(2,1)S(1)}, u32[]{:S(2)}, u32[]{:S(2)}) async-start(bf16[8,32,128]{2,1,0:T(8,128)(2,1)} %mixed_rows.1), calls=%async_computation.1 | async-start | bytes 131072 | tf_op jit(solution)/shard_map/all_to_all | solution.py:610
  55.1 4.7 %near_back.1.rest_0_ = bf16[2,2048,128]{2,1,0:T(8,128)(2,1)} custom-call(s32[1]{0:T(128)S(6)} %sub.3.at_ref, bf16[2048,128]{1,0:T(8,128)(2,1)} %copy-done.8, bf16[3456,128]{1,0:T(8,128)(2,1)} %weight.9, bf16[2,2048,128]{2,1,0:T(8,128)(2,1)} %bitcast.7, f32[2,2048,128]{2,1,0:T(8,128)} %inner_back.1.kept), custom_call_target="tpu_custom_call" | custom-call | flops 1207959552 | bytes 3145728 | tf_op jit(solution)/shard_map/near_back/pallas_call | solution.py:458
  59.8 1.9 %all-to-all-done.1.got = bf16[8,32,128]{2,1,0:T(8,128)(2,1)S(1)} async-done(((bf16[8,32,128]{2,1,0:T(8,128)(2,1)}), bf16[8,32,128]{2,1,0:T(8,128)(2,1)S(1)}, u32[]{:S(2)}, u32[]{:S(2)}) %all-to-all-start.1) | async-done | bytes 65568 | tf_op jit(solution)/shard_map/all_to_all | solution.py:610
  61.7 0.8 spread_step.1
  62.4 10.7 %all-to-all-start.2 = ((bf16[32,32,128]{2,1,0:T(8,128)(2,1)}), bf16[32,32,128]{2,1,0:T(8,128)(2,1)S(1)}, u32[]{:S(2)}, u32[]{:S(2)}) async-start(bf16[32,32,128]{2,1,0:T(8,128)(2,1)} %spread_step.1), calls=%async_computation.2 | async-start | bytes 524288 | tf_op jit(solution)/shard_map/all_to_all | solution.py:616
  73.2 4.6 %far_back.1 = bf16[2,2048,128]{2,1,0:T(8,128)(2,1)} custom-call(s32[1]{0:T(128)} %bitcast.core_ref.at_ref, bf16[2048,128]{1,0:T(8,128)(2,1)} %collective-permute-done.3.halo, bf16[3456,128]{1,0:T(8,128)(2,1)} %weight.9, bf16[2,2048,128]{2,1,0:T(8,128)(2,1)} %bitcast.8, f32[2,2048,128]{2,1,0:T(8,128)} %inner_back.1.kept, ...), custom_call_target="tpu_custom_call", output_to_operand_aliasing={{}: (5, {})} | custom-call | flops 1207959552 | bytes 3145728 | tf_op jit(solution)/shard_map/far_back/pallas_call | solution.py:458
  77.8 4.2 %all-to-all-done.2 = bf16[32,32,128]{2,1,0:T(8,128)(2,1)S(1)} async-done(((bf16[32,32,128]{2,1,0:T(8,128)(2,1)}), bf16[32,32,128]{2,1,0:T(8,128)(2,1)S(1)}, u32[]{:S(2)}, u32[]{:S(2)}) %all-to-all-start.2) | async-done | bytes 262176 | tf_op jit(solution)/shard_map/all_to_all | solution.py:616
  82.0 0.8 first_rows.1
  (21 shorter events, 0.4 us)
Async XLA Ops:
  0.6 1.2 %copy-start.2 = (bf16[1,2,32,64,128]{4,3,2,1,0:T(8,128)(2,1)S(1)}, bf16[1,2,32,64,128]{4,3,2,1,0:T(8,128)(2,1)}, u32[]{:S(2)}) copy-start(bf16[1,2,32,64,128]{4,3,2,1,0:T(8,128)(2,1)} %param.5) | copy-start | bytes 3145732
  1.9 10.2 %collective-permute-start = (bf16[2048,128]{1,0:T(8,128)(2,1)S(1)}, bf16[2048,128]{1,0:T(8,128)(2,1)S(1)}, u32[]{:S(2)}, u32[]{:S(2)}) collective-permute-start(bf16[2048,128]{1,0:T(8,128)(2,1)S(1)} %get-tuple-element.19.near), channel_id=1, source_target_pairs={{0,4},{4,0},{1,5},{5,1},{2,6},{6,2},{3,7},{7,3},{8,12},{12,8},{9,1... | collective-permute-start | bytes 1572872 | tf_op jit(solution)/shard_map/ppermute | solution.py:585
  5.3 6.9 %copy-start = (bf16[1,2,32,64,128]{4,3,2,1,0:T(8,128)(2,1)S(1)}, bf16[1,2,32,64,128]{4,3,2,1,0:T(8,128)(2,1)}, u32[]{:S(2)}) copy-start(bf16[1,2,32,64,128]{4,3,2,1,0:T(8,128)(2,1)} %param.6) | copy-start | bytes 3145732
  5.3 14.9 %collective-permute-start.1 = (bf16[2048,128]{1,0:T(8,128)(2,1)S(1)}, bf16[2048,128]{1,0:T(8,128)(2,1)S(1)}, u32[]{:S(2)}, u32[]{:S(2)}) collective-permute-start(bf16[2048,128]{1,0:T(8,128)(2,1)S(1)} %get-tuple-element.20.far), channel_id=1, source_target_pairs={{4,8},{12,16},{20,24},{28,32},{36,40},{44,48},{52,56},{60,64},{68,... | collective-permute-start | bytes 1572872 | tf_op jit(solution)/shard_map/ppermute | solution.py:584
  7.3 1.2 %copy-start.1 = (bf16[3456,128]{1,0:T(8,128)(2,1)S(1)}, bf16[3456,128]{1,0:T(8,128)(2,1)}, u32[]{:S(2)}) copy-start(bf16[3456,128]{1,0:T(8,128)(2,1)} %weight.9) | copy-start | bytes 2654212
  18.0 8.3 %copy-start.7 = (bf16[2048,128]{1,0:T(8,128)(2,1)}, bf16[2048,128]{1,0:T(8,128)(2,1)S(1)}, u32[]{:S(2)}) copy-start(bf16[2048,128]{1,0:T(8,128)(2,1)S(1)} %get-tuple-element.25.near) | copy-start | bytes 1572868
  26.0 3.1 %copy-start.5 = (bf16[2048,128]{1,0:T(8,128)(2,1)}, bf16[2048,128]{1,0:T(8,128)(2,1)S(1)}, u32[]{:S(2)}) copy-start(bf16[2048,128]{1,0:T(8,128)(2,1)S(1)} %get-tuple-element.28.far) | copy-start | bytes 1572868
  26.0 2.2 %collective-permute-start.2 = (bf16[64,32,128]{2,1,0:T(8,128)(2,1)S(1)}, bf16[64,32,128]{2,1,0:T(8,128)(2,1)S(1)}, u32[]{:S(2)}, u32[]{:S(2)}) collective-permute-start(bf16[64,32,128]{2,1,0:T(8,128)(2,1)S(1)} %get-tuple-element.27), channel_id=1, source_target_pairs={{0,4},{4,0},{1,5},{5,1},{2,6},{6,2},{3,7},{7,3},{8,12},{12,8},{9,1... | collective-permute-start | bytes 1572872 | tf_op jit(solution)/shard_map/ppermute | solution.py:601
  26.3 20.6 %collective-permute-start.4 = (bf16[2048,128]{1,0:T(8,128)(2,1)S(1)}, bf16[2048,128]{1,0:T(8,128)(2,1)S(1)}, u32[]{:S(2)}, u32[]{:S(2)}) collective-permute-start(bf16[2048,128]{1,0:T(8,128)(2,1)S(1)} %get-tuple-element.25.near), channel_id=1, source_target_pairs={{0,4},{4,0},{1,5},{5,1},{2,6},{6,2},{3,7},{7,3},{8,12},{12,8},{9,1... | collective-permute-start | bytes 1572872 | tf_op jit(solution)/shard_map/ppermute | solution.py:585
  29.1 17.1 %all-to-all-start = ((bf16[16,4,32,128]{3,2,1,0:T(8,128)(2,1)}), bf16[16,4,32,128]{3,2,1,0:T(8,128)(2,1)S(1)}, u32[]{:S(2)}, u32[]{:S(2)}) async-start(bf16[16,4,32,128]{3,2,1,0:T(8,128)(2,1)} %bitcast.3.later), calls=%async_computation | async-start | bytes 1048576 | tf_op jit(solution)/shard_map/all_to_all | solution.py:603
  35.8 6.2 %copy-start.6 = (bf16[2048,128]{1,0:T(8,128)(2,1)S(1)}, bf16[2048,128]{1,0:T(8,128)(2,1)}, u32[]{:S(2)}) copy-start(bf16[2048,128]{1,0:T(8,128)(2,1)} %copy-done.5) | copy-start | bytes 1572868
  42.0 31.2 %collective-permute-start.3 = (bf16[2048,128]{1,0:T(8,128)(2,1)S(1)}, bf16[2048,128]{1,0:T(8,128)(2,1)}, u32[]{:S(2)}, u32[]{:S(2)}) collective-permute-start(bf16[2048,128]{1,0:T(8,128)(2,1)S(1)} %copy-done.6), channel_id=1, source_target_pairs={{4,8},{12,16},{20,24},{28,32},{36,40},{44,48},{52,56},{60,64},{68,... | collective-permute-start | bytes 1572872 | tf_op jit(solution)/shard_map/ppermute | solution.py:584
  46.9 8.2 %copy-start.8 = (bf16[2048,128]{1,0:T(8,128)(2,1)}, bf16[2048,128]{1,0:T(8,128)(2,1)S(1)}, u32[]{:S(2)}) copy-start(bf16[2048,128]{1,0:T(8,128)(2,1)S(1)} %collective-permute-done.4.halo) | copy-start | bytes 1572868
  46.9 14.8 %all-to-all-start.1 = ((bf16[8,32,128]{2,1,0:T(8,128)(2,1)}), bf16[8,32,128]{2,1,0:T(8,128)(2,1)S(1)}, u32[]{:S(2)}, u32[]{:S(2)}) async-start(bf16[8,32,128]{2,1,0:T(8,128)(2,1)} %mixed_rows.1), calls=%async_computation.1 | async-start | bytes 131072 | tf_op jit(solution)/shard_map/all_to_all | solution.py:610
  55.1 6.6 %copy-start.3 = (f32[864,128]{1,0:T(8,128)S(1)}, f32[864,128]{1,0:T(8,128)}, u32[]{:S(2)}) copy-start(f32[864,128]{1,0:T(8,128)} %first.1) | copy-start | bytes 1327108
  55.1 6.6 %copy-start.4 = (f32[864,128]{1,0:T(8,128)S(1)}, f32[864,128]{1,0:T(8,128)}, u32[]{:S(2)}) copy-start(f32[864,128]{1,0:T(8,128)} %second.1) | copy-start | bytes 1327108
  62.4 19.6 %all-to-all-start.2 = ((bf16[32,32,128]{2,1,0:T(8,128)(2,1)}), bf16[32,32,128]{2,1,0:T(8,128)(2,1)S(1)}, u32[]{:S(2)}, u32[]{:S(2)}) async-start(bf16[32,32,128]{2,1,0:T(8,128)(2,1)} %spread_step.1), calls=%async_computation.2 | async-start | bytes 524288 | tf_op jit(solution)/shard_map/all_to_all | solution.py:616

commit v10 on v8

--- a/solution.py
+++ b/solution.py
@@ -23,6 +23,7 @@
 PADDED = CELLS + 2 * COLS
 STRIP = 256
 TILE = 512
+SIDE_TILE = 1024
 BF = jnp.bfloat16
 F32 = jnp.float32
 VMEM = pl.BlockSpec(memory_space=pltpu.VMEM)
@@ -193,33 +194,33 @@
             part[place(core, group, owner)] = jnp.zeros((CHUNK, C), F32)
 
     def leave(i):
-        at = pl.multiple_of(i * TILE, TILE)
-        held_at = pl.ds(pl.multiple_of(at + COLS, COLS), TILE)
+        at = pl.multiple_of(i * SIDE_TILE, SIDE_TILE)
+        held_at = pl.ds(pl.multiple_of(at + COLS, COLS), SIDE_TILE)
         return pltpu.make_async_copy(
-            shifts.at[1, held_at, :], grad.at[pl.ds(at, TILE), :], leave_sems.at[i]
+            shifts.at[1, held_at, :], grad.at[pl.ds(at, SIDE_TILE), :], leave_sems.at[i]
         )
 
     def tile(i, carry):
-        at = pl.multiple_of(i * TILE, TILE)
-        rows = pl.ds(at, TILE)
-        to = pl.ds(pl.multiple_of(at + COLS, COLS), TILE)
+        at = pl.multiple_of(i * SIDE_TILE, SIDE_TILE)
+        rows = pl.ds(at, SIDE_TILE)
+        to = pl.ds(pl.multiple_of(at + COLS, COLS), SIDE_TILE)
         preact = inner[z, rows, :] + jnp.dot(
-            taps_of(field, at, TILE), held[...], preferred_element_type=F32
+            taps_of(field, at, SIDE_TILE), held[...], preferred_element_type=F32
         )
         s = jax.nn.sigmoid(preact)
         slopes = s * (1.0 + preact * (1.0 - s))
         here = (upstream[z, rows, :].astype(F32) * slopes).astype(BF)
         wide = here.astype(F32)
-        col = lax.broadcasted_iota(jnp.int32, (TILE, C), 0) & (COLS - 1)
+        col = lax.broadcasted_iota(jnp.int32, (SIDE_TILE, C), 0) & (COLS - 1)
         shifts[1, to, :] = here
         leave(i).start()
         shifts[0, to, :] = jnp.where(col == 0, 0.0, pltpu.roll(wide, 1, 0)).astype(BF)
         shifts[2, to, :] = jnp.where(
-            col == COLS - 1, 0.0, pltpu.roll(wide, TILE - 1, 0)
+            col == COLS - 1, 0.0, pltpu.roll(wide, SIDE_TILE - 1, 0)
         ).astype(BF)
         return carry
 
-    lax.fori_loop(0, CELLS // TILE, tile, 0)
+    lax.fori_loop(0, CELLS // SIDE_TILE, tile, 0)
 
     lhs = jnp.concatenate([vol_t[...], turned[...]], axis=0)
     offset_of = (1 - z, 2 - z, 2 * z)
@@ -242,7 +243,7 @@
                     first = p * C + i * CHUNK
                     block = got[first : first + CHUNK, k * C : (k + 1) * C]
                     part[at] = block if begun is None else begun[at] + block
-    for i in range(CELLS // TILE):
+    for i in range(CELLS // SIDE_TILE):
         leave(i).wait()
 
 
@@ -286,7 +287,7 @@
     pltpu.VMEM((3, PADDED, C), BF),
     pltpu.VMEM((C, CELLS), BF),
     pltpu.SemaphoreType.DMA,
-    pltpu.SemaphoreType.DMA((CELLS // TILE,)),
+    pltpu.SemaphoreType.DMA((CELLS // SIDE_TILE,)),
 ]
 
 

time: 80.5 us -> 80.1 us (level)
  Pallas kernels: 33.4 us -> 32 us
  waiting for transfers between devices: 10.6 us -> 11.8 us
    ppermute x2, waiting for transfers between devices: 2.12 us -> 3.12 us  [from_neighbours(): far_halo = lax.ppermute(far, SPACE, pairs + [(j, i) for i, j in pairs])]
    pallas_call x1, Pallas kernels: 5.82 us -> 4.82 us  [near_side(): pl.pallas_call(near_kernel, out_shape=[PLANE, jax.ShapeDtypeStruct(PART,...]
  transfers between devices with their start and end apart: 8 -> 8, of which waited for: 5 -> 5; matrix products, arithmetic and copies ran while one was open for 0% -> 0% of each run, Pallas kernels for 34% -> 33%
where the time goes in v10:
time: 80.1 us; the launch traced here: 79.4 us
  starting transfers between devices  32.2 us (40%)
  Pallas kernels  32 us (40%)
  waiting for transfers between devices  11.8 us (15%)
  local copies, waits for them, and re-layouts  2.41 us (3%)
  between operations  0.97 us (1%)
    pallas_call x2, Pallas kernels, outer_back(): pl.pallas_call(outer_back_kernel, out_shape=jax.ShapeDtypeStruct((2, CELL...  9.27 us
    all_to_all x1, starting transfers between devices, body(): got = lax.all_to_all(part, ('zl', 'sample'), 0, 0)  8.18 us
    all_to_all x1, starting transfers between devices, body(): whole = lax.all_to_all(step, ('core', 'x', 'y'), 0, 0)  7.77 us
    all_to_all x1, starting transfers between devices, body(): got = lax.all_to_all(half, ('x', 'y'), 0, 0)  6.89 us
    pallas_call x1, Pallas kernels, inner_back(): pl.pallas_call(inner_back_kernel, out_shape=jax.ShapeDtypeStruct((2, CELL...  6.14 us
    ppermute x2, starting transfers between devices, from_neighbours(): far_halo = lax.ppermute(far, SPACE, pairs + [(j, i) for i, j in pairs])  5.47 us
    pallas_call x1, Pallas kernels, far_side(): pl.pallas_call(far_kernel, out_shape=[PLANE, jax.ShapeDtypeStruct(PART, F...  4.9 us
    pallas_call x1, Pallas kernels, near_side(): pl.pallas_call(near_kernel, out_shape=[PLANE, jax.ShapeDtypeStruct(PART,...  4.82 us
  transfers between devices with their start and end apart: 8, of which 5 were waited for; matrix products, arithmetic and copies ran while one was open for 0% of the time, Pallas kernels for 33%

profile of v10, /device:TPU:1, one launch (start us, length us, event | category | flops | bytes accessed | tf_op | source)
XLA Modules:
  0.0 79.4 jit_solution(9810495064367776138)
XLA Ops:
  0.6 1.2 %copy-done.2 = bf16[1,2,32,64,128]{4,3,2,1,0:T(8,128)(2,1)S(1)} copy-done((bf16[1,2,32,64,128]{4,3,2,1,0:T(8,128)(2,1)S(1)}, bf16[1,2,32,64,128]{4,3,2,1,0:T(8,128)(2,1)}, u32[]{:S(2)}) %copy-start.2) | copy-done | bytes 1048600
  1.9 3.3 %collective-permute-start = (bf16[2048,128]{1,0:T(8,128)(2,1)S(1)}, bf16[2048,128]{1,0:T(8,128)(2,1)S(1)}, u32[]{:S(2)}, u32[]{:S(2)}) collective-permute-start(bf16[2048,128]{1,0:T(8,128)(2,1)S(1)} %get-tuple-element.17.near), channel_id=1, source_target_pairs={{0,4},{4,0},{1,5},{5,1},{2,6},{6,2},{3,7},{7,3},{8,12},{12,8},{9,1... | collective-permute-start | bytes 1572872 | tf_op jit(solution)/shard_map/ppermute | solution.py:574
  5.3 2.0 %collective-permute-start.1 = (bf16[2048,128]{1,0:T(8,128)(2,1)S(1)}, bf16[2048,128]{1,0:T(8,128)(2,1)S(1)}, u32[]{:S(2)}, u32[]{:S(2)}) collective-permute-start(bf16[2048,128]{1,0:T(8,128)(2,1)S(1)} %get-tuple-element.18.far), channel_id=1, source_target_pairs={{4,8},{12,16},{20,24},{28,32},{36,40},{44,48},{52,56},{60,64},{68,... | collective-permute-start | bytes 1572872 | tf_op jit(solution)/shard_map/ppermute | solution.py:573
  7.3 1.2 %copy-done.1 = bf16[3456,128]{1,0:T(8,128)(2,1)S(1)} copy-done((bf16[3456,128]{1,0:T(8,128)(2,1)S(1)}, bf16[3456,128]{1,0:T(8,128)(2,1)}, u32[]{:S(2)}) %copy-start.1) | copy-done | bytes 884760
  8.5 3.7 %inner_conv.1 = (f32[2,2048,128]{2,1,0:T(8,128)S(1)}, bf16[256,2048]{1,0:T(8,128)(2,1)S(1)}) custom-call(s32[1]{0:T(128)} %bitcast.core_ref.at_ref, bf16[2048,128]{1,0:T(8,128)(2,1)S(1)} %get-tuple-element.17.near, bf16[2048,128]{1,0:T(8,128)(2,1)S(1)} %get-tuple-element.18.far, bf16[3456,128]{1,0:T(8,128)(2,1)S(1)} %copy-done.1), custom_call_target="tpu_custom_call" | custom-call | flops 2415919104 | bytes 5242880 | tf_op jit(solution)/shard_map/inner_conv/pallas_call | solution.py:140
  12.2 4.8 %near_side.1 = (bf16[2048,128]{1,0:T(8,128)(2,1)S(1)}, f32[128,32,128]{2,1,0:T(8,128)S(1)}) custom-call(s32[1]{0:T(128)} %bitcast.core_ref.at_ref, bf16[2048,128]{1,0:T(8,128)(2,1)S(1)} %collective-permute-done.refs_0_, bf16[3456,128]{1,0:T(8,128)(2,1)S(1)} %copy-done.1, f32[2,2048,128]{2,1,0:T(8,128)S(1)} %get-tuple-element.19.refs_2_.inner, ...), custom_call_target="tpu_custom_call" | custom-call | flops 3623878656 | bytes 5242880 | tf_op jit(solution)/shard_map/near_side/pallas_call | solution.py:295
  17.0 3.1 %collective-permute-done.1.halo = bf16[2048,128]{1,0:T(8,128)(2,1)S(1)} collective-permute-done((bf16[2048,128]{1,0:T(8,128)(2,1)S(1)}, bf16[2048,128]{1,0:T(8,128)(2,1)S(1)}, u32[]{:S(2)}, u32[]{:S(2)}) %collective-permute-start.1) | collective-permute-done | bytes 524320 | tf_op jit(solution)/shard_map/ppermute | solution.py:573
  20.1 4.9 %far_side.1 = (bf16[2048,128]{1,0:T(8,128)(2,1)}, f32[128,32,128]{2,1,0:T(8,128)S(1)}, bf16[64,32,128]{2,1,0:T(8,128)(2,1)S(1)}) custom-call(s32[1]{0:T(128)} %bitcast.core_ref.at_ref, f32[128,32,128]{2,1,0:T(8,128)S(1)} %get-tuple-element.21.begun, bf16[2048,128]{1,0:T(8,128)(2,1)S(1)} %collective-permute-done.1.halo, bf16[3456,128]{1,0:T(8,128)(2,1)S(1)} %copy-done.1, ...), custom_call_target="tpu_custom_call" | custom-call | flops 3623878656 | bytes 5242880 | tf_op jit(solution)/shard_map/far_side/pallas_call | solution.py:308
  25.1 0.5 collective-permute-start.4
  25.6 1.4 %collective-permute-done.3.other = bf16[64,32,128]{2,1,0:T(8,128)(2,1)S(1)} collective-permute-done((bf16[64,32,128]{2,1,0:T(8,128)(2,1)S(1)}, bf16[64,32,128]{2,1,0:T(8,128)(2,1)S(1)}, u32[]{:S(2)}, u32[]{:S(2)}) %collective-permute-start.3) | collective-permute-done | bytes 524320 | tf_op jit(solution)/shard_map/ppermute | solution.py:590
  27.0 0.9 %both_halves.1 = bf16[64,32,128]{2,1,0:T(8,128)(2,1)} custom-call(f32[128,32,128]{2,1,0:T(8,128)S(1)} %get-tuple-element.23.part, bf16[64,32,128]{2,1,0:T(8,128)(2,1)S(1)} %collective-permute-done.3.other), custom_call_target="tpu_custom_call" | custom-call | flops 262144 | bytes 2097152 | tf_op jit(solution)/shard_map/both_halves/pallas_call | solution.py:329
  27.9 6.9 %all-to-all-start = ((bf16[16,4,32,128]{3,2,1,0:T(8,128)(2,1)}), bf16[16,4,32,128]{3,2,1,0:T(8,128)(2,1)S(1)}, u32[]{:S(2)}, u32[]{:S(2)}) async-start(bf16[16,4,32,128]{3,2,1,0:T(8,128)(2,1)} %bitcast.3.later), calls=%async_computation | async-start | bytes 1048576 | tf_op jit(solution)/shard_map/all_to_all | solution.py:592
  34.8 3.4 %collective-permute-start.2 = (bf16[2048,128]{1,0:T(8,128)(2,1)}, bf16[2048,128]{1,0:T(8,128)(2,1)}, u32[]{:S(2)}, u32[]{:S(2)}) collective-permute-start(bf16[2048,128]{1,0:T(8,128)(2,1)} %get-tuple-element.22.far), channel_id=1, source_target_pairs={{4,8},{12,16},{20,24},{28,32},{36,40},{44,48},{52,56},{60,64},{68,... | collective-permute-start | bytes 1572872 | tf_op jit(solution)/shard_map/ppermute | solution.py:573
  38.3 6.1 %inner_back.1.kept = f32[2,2048,128]{2,1,0:T(8,128)} custom-call(s32[1]{0:T(128)} %bitcast.core_ref.at_ref, bf16[2048,128]{1,0:T(8,128)(2,1)} %copy-done.5, bf16[2048,128]{1,0:T(8,128)(2,1)} %get-tuple-element.22.far, bf16[3456,128]{1,0:T(8,128)(2,1)} %weight.9, bf16[16,4,32,128]{3,2,1,0:T(8,128)(2,1)} %bitcast.3.later), custom_call_target="tpu_custom_call" | custom-call | flops 2415919104 | bytes 5242880 | tf_op jit(solution)/shard_map/inner_back/pallas_call | solution.py:383
  44.4 1.1 %all-to-all-done.got = bf16[16,4,32,128]{3,2,1,0:T(8,128)(2,1)S(1)} async-done(((bf16[16,4,32,128]{3,2,1,0:T(8,128)(2,1)}), bf16[16,4,32,128]{3,2,1,0:T(8,128)(2,1)S(1)}, u32[]{:S(2)}, u32[]{:S(2)}) %all-to-all-start) | async-done | bytes 524320 | tf_op jit(solution)/shard_map/all_to_all | solution.py:592
  45.5 0.7 mixed_rows.1
  46.2 8.2 %all-to-all-start.1 = ((bf16[8,32,128]{2,1,0:T(8,128)(2,1)}), bf16[8,32,128]{2,1,0:T(8,128)(2,1)S(1)}, u32[]{:S(2)}, u32[]{:S(2)}) async-start(bf16[8,32,128]{2,1,0:T(8,128)(2,1)} %mixed_rows.1), calls=%async_computation.1 | async-start | bytes 131072 | tf_op jit(solution)/shard_map/all_to_all | solution.py:598
  54.5 4.7 %near_back.1.rest_0_ = bf16[2,2048,128]{2,1,0:T(8,128)(2,1)} custom-call(s32[1]{0:T(128)S(6)} %sub.3.at_ref, bf16[2048,128]{1,0:T(8,128)(2,1)} %copy-done.6, bf16[3456,128]{1,0:T(8,128)(2,1)} %weight.9, bf16[2,2048,128]{2,1,0:T(8,128)(2,1)} %bitcast.7, f32[2,2048,128]{2,1,0:T(8,128)} %inner_back.1.kept), custom_call_target="tpu_custom_call" | custom-call | flops 1207959552 | bytes 3145728 | tf_op jit(solution)/shard_map/near_back/pallas_call | solution.py:447
  59.1 1.9 %all-to-all-done.1.got = bf16[8,32,128]{2,1,0:T(8,128)(2,1)S(1)} async-done(((bf16[8,32,128]{2,1,0:T(8,128)(2,1)}), bf16[8,32,128]{2,1,0:T(8,128)(2,1)S(1)}, u32[]{:S(2)}, u32[]{:S(2)}) %all-to-all-start.1) | async-done | bytes 65568 | tf_op jit(solution)/shard_map/all_to_all | solution.py:598
  61.1 0.8 spread_step.1
  61.8 7.8 %all-to-all-start.2 = ((bf16[32,32,128]{2,1,0:T(8,128)(2,1)}), bf16[32,32,128]{2,1,0:T(8,128)(2,1)S(1)}, u32[]{:S(2)}, u32[]{:S(2)}) async-start(bf16[32,32,128]{2,1,0:T(8,128)(2,1)} %spread_step.1), calls=%async_computation.2 | async-start | bytes 524288 | tf_op jit(solution)/shard_map/all_to_all | solution.py:604
  69.6 4.6 %far_back.1 = bf16[2,2048,128]{2,1,0:T(8,128)(2,1)} custom-call(s32[1]{0:T(128)} %bitcast.core_ref.at_ref, bf16[2048,128]{1,0:T(8,128)(2,1)} %collective-permute-done.2.halo, bf16[3456,128]{1,0:T(8,128)(2,1)} %weight.9, bf16[2,2048,128]{2,1,0:T(8,128)(2,1)} %bitcast.8, f32[2,2048,128]{2,1,0:T(8,128)} %inner_back.1.kept, ...), custom_call_target="tpu_custom_call", output_to_operand_aliasing={{}: (5, {})} | custom-call | flops 1207959552 | bytes 3145728 | tf_op jit(solution)/shard_map/far_back/pallas_call | solution.py:447
  74.2 4.2 %all-to-all-done.2 = bf16[32,32,128]{2,1,0:T(8,128)(2,1)S(1)} async-done(((bf16[32,32,128]{2,1,0:T(8,128)(2,1)}), bf16[32,32,128]{2,1,0:T(8,128)(2,1)S(1)}, u32[]{:S(2)}, u32[]{:S(2)}) %all-to-all-start.2) | async-done | bytes 262176 | tf_op jit(solution)/shard_map/all_to_all | solution.py:604
  78.4 0.8 %first_rows.1 = f32[864,128]{1,0:T(8,128)} custom-call(bf16[1024,128]{1,0:T(8,128)(2,1)S(1)} %bitcast.12), custom_call_target="tpu_custom_call" | custom-call | bytes 1048576 | tf_op jit(solution)/shard_map/first_rows/pallas_call | solution.py:503
  (17 shorter events, 0.2 us)
Async XLA Ops:
  0.6 1.2 %copy-start.2 = (bf16[1,2,32,64,128]{4,3,2,1,0:T(8,128)(2,1)S(1)}, bf16[1,2,32,64,128]{4,3,2,1,0:T(8,128)(2,1)}, u32[]{:S(2)}) copy-start(bf16[1,2,32,64,128]{4,3,2,1,0:T(8,128)(2,1)} %param.5) | copy-start | bytes 3145732
  1.9 10.2 %collective-permute-start = (bf16[2048,128]{1,0:T(8,128)(2,1)S(1)}, bf16[2048,128]{1,0:T(8,128)(2,1)S(1)}, u32[]{:S(2)}, u32[]{:S(2)}) collective-permute-start(bf16[2048,128]{1,0:T(8,128)(2,1)S(1)} %get-tuple-element.17.near), channel_id=1, source_target_pairs={{0,4},{4,0},{1,5},{5,1},{2,6},{6,2},{3,7},{7,3},{8,12},{12,8},{9,1... | collective-permute-start | bytes 1572872 | tf_op jit(solution)/shard_map/ppermute | solution.py:574
  5.3 6.9 %copy-start = (bf16[1,2,32,64,128]{4,3,2,1,0:T(8,128)(2,1)S(1)}, bf16[1,2,32,64,128]{4,3,2,1,0:T(8,128)(2,1)}, u32[]{:S(2)}) copy-start(bf16[1,2,32,64,128]{4,3,2,1,0:T(8,128)(2,1)} %param.6) | copy-start | bytes 3145732
  5.3 14.9 %collective-permute-start.1 = (bf16[2048,128]{1,0:T(8,128)(2,1)S(1)}, bf16[2048,128]{1,0:T(8,128)(2,1)S(1)}, u32[]{:S(2)}, u32[]{:S(2)}) collective-permute-start(bf16[2048,128]{1,0:T(8,128)(2,1)S(1)} %get-tuple-element.18.far), channel_id=1, source_target_pairs={{4,8},{12,16},{20,24},{28,32},{36,40},{44,48},{52,56},{60,64},{68,... | collective-permute-start | bytes 1572872 | tf_op jit(solution)/shard_map/ppermute | solution.py:573
  7.3 1.2 %copy-start.1 = (bf16[3456,128]{1,0:T(8,128)(2,1)S(1)}, bf16[3456,128]{1,0:T(8,128)(2,1)}, u32[]{:S(2)}) copy-start(bf16[3456,128]{1,0:T(8,128)(2,1)} %weight.9) | copy-start | bytes 2654212
  17.0 8.1 %copy-start.5 = (bf16[2048,128]{1,0:T(8,128)(2,1)}, bf16[2048,128]{1,0:T(8,128)(2,1)S(1)}, u32[]{:S(2)}) copy-start(bf16[2048,128]{1,0:T(8,128)(2,1)S(1)} %get-tuple-element.25.near) | copy-start | bytes 1572868
  25.0 2.0 %collective-permute-start.3 = (bf16[64,32,128]{2,1,0:T(8,128)(2,1)S(1)}, bf16[64,32,128]{2,1,0:T(8,128)(2,1)S(1)}, u32[]{:S(2)}, u32[]{:S(2)}) collective-permute-start(bf16[64,32,128]{2,1,0:T(8,128)(2,1)S(1)} %get-tuple-element.24), channel_id=1, source_target_pairs={{0,4},{4,0},{1,5},{5,1},{2,6},{6,2},{3,7},{7,3},{8,12},{12,8},{9,1... | collective-permute-start | bytes 1572872 | tf_op jit(solution)/shard_map/ppermute | solution.py:590
  25.1 21.1 %collective-permute-start.4 = (bf16[2048,128]{1,0:T(8,128)(2,1)S(1)}, bf16[2048,128]{1,0:T(8,128)(2,1)S(1)}, u32[]{:S(2)}, u32[]{:S(2)}) collective-permute-start(bf16[2048,128]{1,0:T(8,128)(2,1)S(1)} %get-tuple-element.25.near), channel_id=1, source_target_pairs={{0,4},{4,0},{1,5},{5,1},{2,6},{6,2},{3,7},{7,3},{8,12},{12,8},{9,1... | collective-permute-start | bytes 1572872 | tf_op jit(solution)/shard_map/ppermute | solution.py:574
  27.9 17.6 %all-to-all-start = ((bf16[16,4,32,128]{3,2,1,0:T(8,128)(2,1)}), bf16[16,4,32,128]{3,2,1,0:T(8,128)(2,1)S(1)}, u32[]{:S(2)}, u32[]{:S(2)}) async-start(bf16[16,4,32,128]{3,2,1,0:T(8,128)(2,1)} %bitcast.3.later), calls=%async_computation | async-start | bytes 1048576 | tf_op jit(solution)/shard_map/all_to_all | solution.py:592
  34.8 34.8 %collective-permute-start.2 = (bf16[2048,128]{1,0:T(8,128)(2,1)}, bf16[2048,128]{1,0:T(8,128)(2,1)}, u32[]{:S(2)}, u32[]{:S(2)}) collective-permute-start(bf16[2048,128]{1,0:T(8,128)(2,1)} %get-tuple-element.22.far), channel_id=1, source_target_pairs={{4,8},{12,16},{20,24},{28,32},{36,40},{44,48},{52,56},{60,64},{68,... | collective-permute-start | bytes 1572872 | tf_op jit(solution)/shard_map/ppermute | solution.py:573
  46.2 8.2 %copy-start.6 = (bf16[2048,128]{1,0:T(8,128)(2,1)}, bf16[2048,128]{1,0:T(8,128)(2,1)S(1)}, u32[]{:S(2)}) copy-start(bf16[2048,128]{1,0:T(8,128)(2,1)S(1)} %collective-permute-done.4.halo) | copy-start | bytes 1572868
  46.2 14.8 %all-to-all-start.1 = ((bf16[8,32,128]{2,1,0:T(8,128)(2,1)}), bf16[8,32,128]{2,1,0:T(8,128)(2,1)S(1)}, u32[]{:S(2)}, u32[]{:S(2)}) async-start(bf16[8,32,128]{2,1,0:T(8,128)(2,1)} %mixed_rows.1), calls=%async_computation.1 | async-start | bytes 131072 | tf_op jit(solution)/shard_map/all_to_all | solution.py:598
  54.4 6.6 %copy-start.3 = (f32[864,128]{1,0:T(8,128)S(1)}, f32[864,128]{1,0:T(8,128)}, u32[]{:S(2)}) copy-start(f32[864,128]{1,0:T(8,128)} %first.1) | copy-start | bytes 1327108
  54.4 6.6 %copy-start.4 = (f32[864,128]{1,0:T(8,128)S(1)}, f32[864,128]{1,0:T(8,128)}, u32[]{:S(2)}) copy-start(f32[864,128]{1,0:T(8,128)} %second.1) | copy-start | bytes 1327108
  61.8 16.6 %all-to-all-start.2 = ((bf16[32,32,128]{2,1,0:T(8,128)(2,1)}), bf16[32,32,128]{2,1,0:T(8,128)(2,1)S(1)}, u32[]{:S(2)}, u32[]{:S(2)}) async-start(bf16[32,32,128]{2,1,0:T(8,128)(2,1)} %spread_step.1), calls=%async_computation.2 | async-start | bytes 524288 | tf_op jit(solution)/shard_map/all_to_all | solution.py:604

commit v11 on v10

--- a/solution.py
+++ b/solution.py
@@ -321,8 +321,16 @@
     )(core, begun, halo, weight, inner, upstream, vol_t)
 
 
-def halves_kernel(part, other, half):
-    half[...] = (part[0:64] + other[...].astype(F32)).astype(BF)
+def halves_kernel(part, other, half, held, sems):
+    copies = []
+    for k in range(4):
+        rows = slice(k * 16, (k + 1) * 16)
+        held[rows] = (part[rows] + other[rows].astype(F32)).astype(BF)
+        copy = pltpu.make_async_copy(held.at[rows], half.at[rows], sems.at[k])
+        copy.start()
+        copies.append(copy)
+    for copy in copies:
+        copy.wait()
 
 
 def both_halves(part, other):
@@ -330,7 +338,11 @@
         halves_kernel,
         out_shape=jax.ShapeDtypeStruct((64, CHUNK, C), BF),
         in_specs=[VMEM, VMEM],
-        out_specs=VMEM,
+        out_specs=HBM,
+        scratch_shapes=[
+            pltpu.VMEM((64, CHUNK, C), BF),
+            pltpu.SemaphoreType.DMA((4,)),
+        ],
         compiler_params=SMALL,
         cost_estimate=cost(1 << 18, 2 << 20),
         name="both_halves",

time: 80.1 us -> 80 us (level)
  no operation moved by 1% of the time
where the time goes in v11:
time: 80 us; the launch traced here: 79.4 us
  starting transfers between devices  32.2 us (40%)
  Pallas kernels  31.9 us (40%)
  waiting for transfers between devices  11.8 us (15%)
  local copies, waits for them, and re-layouts  2.41 us (3%)
  between operations  0.98 us (1%)
    pallas_call x2, Pallas kernels, outer_back(): pl.pallas_call(outer_back_kernel, out_shape=jax.ShapeDtypeStruct((2, CELL...  9.26 us
    all_to_all x1, starting transfers between devices, body(): got = lax.all_to_all(part, ('zl', 'sample'), 0, 0)  8.18 us
    all_to_all x1, starting transfers between devices, body(): whole = lax.all_to_all(step, ('core', 'x', 'y'), 0, 0)  7.77 us
    all_to_all x1, starting transfers between devices, body(): got = lax.all_to_all(half, ('x', 'y'), 0, 0)  6.9 us
    pallas_call x1, Pallas kernels, inner_back(): pl.pallas_call(inner_back_kernel, out_shape=jax.ShapeDtypeStruct((2, CELL...  6.13 us
    ppermute x2, starting transfers between devices, from_neighbours(): far_halo = lax.ppermute(far, SPACE, pairs + [(j, i) for i, j in pairs])  5.47 us
    pallas_call x1, Pallas kernels, far_side(): pl.pallas_call(far_kernel, out_shape=[PLANE, jax.ShapeDtypeStruct(PART, F...  4.9 us
    pallas_call x1, Pallas kernels, near_side(): pl.pallas_call(near_kernel, out_shape=[PLANE, jax.ShapeDtypeStruct(PART,...  4.82 us
  transfers between devices with their start and end apart: 8, of which 5 were waited for; matrix products, arithmetic and copies ran while one was open for 0% of the time, Pallas kernels for 33%

profile of v11, /device:TPU:1, one launch (start us, length us, event | category | flops | bytes accessed | tf_op | source)
XLA Modules:
  0.0 79.4 jit_solution(4918731915562218791)
XLA Ops:
  0.6 1.2 %copy-done.2 = bf16[1,2,32,64,128]{4,3,2,1,0:T(8,128)(2,1)S(1)} copy-done((bf16[1,2,32,64,128]{4,3,2,1,0:T(8,128)(2,1)S(1)}, bf16[1,2,32,64,128]{4,3,2,1,0:T(8,128)(2,1)}, u32[]{:S(2)}) %copy-start.2) | copy-done | bytes 1048600
  1.9 3.3 %collective-permute-start = (bf16[2048,128]{1,0:T(8,128)(2,1)S(1)}, bf16[2048,128]{1,0:T(8,128)(2,1)S(1)}, u32[]{:S(2)}, u32[]{:S(2)}) collective-permute-start(bf16[2048,128]{1,0:T(8,128)(2,1)S(1)} %get-tuple-element.17.near), channel_id=1, source_target_pairs={{0,4},{4,0},{1,5},{5,1},{2,6},{6,2},{3,7},{7,3},{8,12},{12,8},{9,1... | collective-permute-start | bytes 1572872 | tf_op jit(solution)/shard_map/ppermute | solution.py:586
  5.3 2.0 %collective-permute-start.1 = (bf16[2048,128]{1,0:T(8,128)(2,1)S(1)}, bf16[2048,128]{1,0:T(8,128)(2,1)S(1)}, u32[]{:S(2)}, u32[]{:S(2)}) collective-permute-start(bf16[2048,128]{1,0:T(8,128)(2,1)S(1)} %get-tuple-element.18.far), channel_id=1, source_target_pairs={{4,8},{12,16},{20,24},{28,32},{36,40},{44,48},{52,56},{60,64},{68,... | collective-permute-start | bytes 1572872 | tf_op jit(solution)/shard_map/ppermute | solution.py:585
  7.3 1.2 %copy-done.1 = bf16[3456,128]{1,0:T(8,128)(2,1)S(1)} copy-done((bf16[3456,128]{1,0:T(8,128)(2,1)S(1)}, bf16[3456,128]{1,0:T(8,128)(2,1)}, u32[]{:S(2)}) %copy-start.1) | copy-done | bytes 884760
  8.5 3.7 %inner_conv.1 = (f32[2,2048,128]{2,1,0:T(8,128)S(1)}, bf16[256,2048]{1,0:T(8,128)(2,1)S(1)}) custom-call(s32[1]{0:T(128)} %bitcast.core_ref.at_ref, bf16[2048,128]{1,0:T(8,128)(2,1)S(1)} %get-tuple-element.17.near, bf16[2048,128]{1,0:T(8,128)(2,1)S(1)} %get-tuple-element.18.far, bf16[3456,128]{1,0:T(8,128)(2,1)S(1)} %copy-done.1), custom_call_target="tpu_custom_call" | custom-call | flops 2415919104 | bytes 5242880 | tf_op jit(solution)/shard_map/inner_conv/pallas_call | solution.py:140
  12.2 4.8 %near_side.1 = (bf16[2048,128]{1,0:T(8,128)(2,1)S(1)}, f32[128,32,128]{2,1,0:T(8,128)S(1)}) custom-call(s32[1]{0:T(128)} %bitcast.core_ref.at_ref, bf16[2048,128]{1,0:T(8,128)(2,1)S(1)} %collective-permute-done.refs_0_, bf16[3456,128]{1,0:T(8,128)(2,1)S(1)} %copy-done.1, f32[2,2048,128]{2,1,0:T(8,128)S(1)} %get-tuple-element.19.refs_2_.inner, ...), custom_call_target="tpu_custom_call" | custom-call | flops 3623878656 | bytes 5242880 | tf_op jit(solution)/shard_map/near_side/pallas_call | solution.py:295
  17.0 3.1 %collective-permute-done.1.halo = bf16[2048,128]{1,0:T(8,128)(2,1)S(1)} collective-permute-done((bf16[2048,128]{1,0:T(8,128)(2,1)S(1)}, bf16[2048,128]{1,0:T(8,128)(2,1)S(1)}, u32[]{:S(2)}, u32[]{:S(2)}) %collective-permute-start.1) | collective-permute-done | bytes 524320 | tf_op jit(solution)/shard_map/ppermute | solution.py:585
  20.1 4.9 %far_side.1 = (bf16[2048,128]{1,0:T(8,128)(2,1)}, f32[128,32,128]{2,1,0:T(8,128)S(1)}, bf16[64,32,128]{2,1,0:T(8,128)(2,1)S(1)}) custom-call(s32[1]{0:T(128)} %bitcast.core_ref.at_ref, f32[128,32,128]{2,1,0:T(8,128)S(1)} %get-tuple-element.21.begun, bf16[2048,128]{1,0:T(8,128)(2,1)S(1)} %collective-permute-done.1.halo, bf16[3456,128]{1,0:T(8,128)(2,1)S(1)} %copy-done.1, ...), custom_call_target="tpu_custom_call" | custom-call | flops 3623878656 | bytes 5242880 | tf_op jit(solution)/shard_map/far_side/pallas_call | solution.py:308
  25.1 0.5 collective-permute-start.4
  25.6 1.4 %collective-permute-done.3.other = bf16[64,32,128]{2,1,0:T(8,128)(2,1)S(1)} collective-permute-done((bf16[64,32,128]{2,1,0:T(8,128)(2,1)S(1)}, bf16[64,32,128]{2,1,0:T(8,128)(2,1)S(1)}, u32[]{:S(2)}, u32[]{:S(2)}) %collective-permute-start.3) | collective-permute-done | bytes 524320 | tf_op jit(solution)/shard_map/ppermute | solution.py:602
  27.0 0.9 %both_halves.1 = bf16[64,32,128]{2,1,0:T(8,128)(2,1)} custom-call(f32[128,32,128]{2,1,0:T(8,128)S(1)} %get-tuple-element.23.part, bf16[64,32,128]{2,1,0:T(8,128)(2,1)S(1)} %collective-permute-done.3.other), custom_call_target="tpu_custom_call" | custom-call | flops 262144 | bytes 2097152 | tf_op jit(solution)/shard_map/both_halves/pallas_call | solution.py:337
  27.9 6.9 %all-to-all-start = ((bf16[16,4,32,128]{3,2,1,0:T(8,128)(2,1)}), bf16[16,4,32,128]{3,2,1,0:T(8,128)(2,1)S(1)}, u32[]{:S(2)}, u32[]{:S(2)}) async-start(bf16[16,4,32,128]{3,2,1,0:T(8,128)(2,1)} %bitcast.3.later), calls=%async_computation | async-start | bytes 1048576 | tf_op jit(solution)/shard_map/all_to_all | solution.py:604
  34.8 3.4 %collective-permute-start.2 = (bf16[2048,128]{1,0:T(8,128)(2,1)}, bf16[2048,128]{1,0:T(8,128)(2,1)}, u32[]{:S(2)}, u32[]{:S(2)}) collective-permute-start(bf16[2048,128]{1,0:T(8,128)(2,1)} %get-tuple-element.22.far), channel_id=1, source_target_pairs={{4,8},{12,16},{20,24},{28,32},{36,40},{44,48},{52,56},{60,64},{68,... | collective-permute-start | bytes 1572872 | tf_op jit(solution)/shard_map/ppermute | solution.py:585
  38.2 6.1 %inner_back.1.kept = f32[2,2048,128]{2,1,0:T(8,128)} custom-call(s32[1]{0:T(128)} %bitcast.core_ref.at_ref, bf16[2048,128]{1,0:T(8,128)(2,1)} %copy-done.5, bf16[2048,128]{1,0:T(8,128)(2,1)} %get-tuple-element.22.far, bf16[3456,128]{1,0:T(8,128)(2,1)} %weight.9, bf16[16,4,32,128]{3,2,1,0:T(8,128)(2,1)} %bitcast.3.later), custom_call_target="tpu_custom_call" | custom-call | flops 2415919104 | bytes 5242880 | tf_op jit(solution)/shard_map/inner_back/pallas_call | solution.py:395
  44.4 1.1 %all-to-all-done.got = bf16[16,4,32,128]{3,2,1,0:T(8,128)(2,1)S(1)} async-done(((bf16[16,4,32,128]{3,2,1,0:T(8,128)(2,1)}), bf16[16,4,32,128]{3,2,1,0:T(8,128)(2,1)S(1)}, u32[]{:S(2)}, u32[]{:S(2)}) %all-to-all-start) | async-done | bytes 524320 | tf_op jit(solution)/shard_map/all_to_all | solution.py:604
  45.5 0.7 mixed_rows.1
  46.2 8.2 %all-to-all-start.1 = ((bf16[8,32,128]{2,1,0:T(8,128)(2,1)}), bf16[8,32,128]{2,1,0:T(8,128)(2,1)S(1)}, u32[]{:S(2)}, u32[]{:S(2)}) async-start(bf16[8,32,128]{2,1,0:T(8,128)(2,1)} %mixed_rows.1), calls=%async_computation.1 | async-start | bytes 131072 | tf_op jit(solution)/shard_map/all_to_all | solution.py:610
  54.4 4.7 %near_back.1.rest_0_ = bf16[2,2048,128]{2,1,0:T(8,128)(2,1)} custom-call(s32[1]{0:T(128)S(6)} %sub.3.at_ref, bf16[2048,128]{1,0:T(8,128)(2,1)} %copy-done.6, bf16[3456,128]{1,0:T(8,128)(2,1)} %weight.9, bf16[2,2048,128]{2,1,0:T(8,128)(2,1)} %bitcast.7, f32[2,2048,128]{2,1,0:T(8,128)} %inner_back.1.kept), custom_call_target="tpu_custom_call" | custom-call | flops 1207959552 | bytes 3145728 | tf_op jit(solution)/shard_map/near_back/pallas_call | solution.py:459
  59.1 1.9 %all-to-all-done.1.got = bf16[8,32,128]{2,1,0:T(8,128)(2,1)S(1)} async-done(((bf16[8,32,128]{2,1,0:T(8,128)(2,1)}), bf16[8,32,128]{2,1,0:T(8,128)(2,1)S(1)}, u32[]{:S(2)}, u32[]{:S(2)}) %all-to-all-start.1) | async-done | bytes 65568 | tf_op jit(solution)/shard_map/all_to_all | solution.py:610
  61.0 0.8 spread_step.1
  61.8 7.8 %all-to-all-start.2 = ((bf16[32,32,128]{2,1,0:T(8,128)(2,1)}), bf16[32,32,128]{2,1,0:T(8,128)(2,1)S(1)}, u32[]{:S(2)}, u32[]{:S(2)}) async-start(bf16[32,32,128]{2,1,0:T(8,128)(2,1)} %spread_step.1), calls=%async_computation.2 | async-start | bytes 524288 | tf_op jit(solution)/shard_map/all_to_all | solution.py:616
  69.6 4.6 %far_back.1 = bf16[2,2048,128]{2,1,0:T(8,128)(2,1)} custom-call(s32[1]{0:T(128)} %bitcast.core_ref.at_ref, bf16[2048,128]{1,0:T(8,128)(2,1)} %collective-permute-done.2.halo, bf16[3456,128]{1,0:T(8,128)(2,1)} %weight.9, bf16[2,2048,128]{2,1,0:T(8,128)(2,1)} %bitcast.8, f32[2,2048,128]{2,1,0:T(8,128)} %inner_back.1.kept, ...), custom_call_target="tpu_custom_call", output_to_operand_aliasing={{}: (5, {})} | custom-call | flops 1207959552 | bytes 3145728 | tf_op jit(solution)/shard_map/far_back/pallas_call | solution.py:459
  74.2 4.2 %all-to-all-done.2 = bf16[32,32,128]{2,1,0:T(8,128)(2,1)S(1)} async-done(((bf16[32,32,128]{2,1,0:T(8,128)(2,1)}), bf16[32,32,128]{2,1,0:T(8,128)(2,1)S(1)}, u32[]{:S(2)}, u32[]{:S(2)}) %all-to-all-start.2) | async-done | bytes 262176 | tf_op jit(solution)/shard_map/all_to_all | solution.py:616
  78.4 0.8 %first_rows.1 = f32[864,128]{1,0:T(8,128)} custom-call(bf16[1024,128]{1,0:T(8,128)(2,1)S(1)} %bitcast.12), custom_call_target="tpu_custom_call" | custom-call | bytes 1048576 | tf_op jit(solution)/shard_map/first_rows/pallas_call | solution.py:515
  (17 shorter events, 0.2 us)
Async XLA Ops:
  0.6 1.2 %copy-start.2 = (bf16[1,2,32,64,128]{4,3,2,1,0:T(8,128)(2,1)S(1)}, bf16[1,2,32,64,128]{4,3,2,1,0:T(8,128)(2,1)}, u32[]{:S(2)}) copy-start(bf16[1,2,32,64,128]{4,3,2,1,0:T(8,128)(2,1)} %param.5) | copy-start | bytes 3145732
  1.9 10.2 %collective-permute-start = (bf16[2048,128]{1,0:T(8,128)(2,1)S(1)}, bf16[2048,128]{1,0:T(8,128)(2,1)S(1)}, u32[]{:S(2)}, u32[]{:S(2)}) collective-permute-start(bf16[2048,128]{1,0:T(8,128)(2,1)S(1)} %get-tuple-element.17.near), channel_id=1, source_target_pairs={{0,4},{4,0},{1,5},{5,1},{2,6},{6,2},{3,7},{7,3},{8,12},{12,8},{9,1... | collective-permute-start | bytes 1572872 | tf_op jit(solution)/shard_map/ppermute | solution.py:586
  5.3 6.9 %copy-start = (bf16[1,2,32,64,128]{4,3,2,1,0:T(8,128)(2,1)S(1)}, bf16[1,2,32,64,128]{4,3,2,1,0:T(8,128)(2,1)}, u32[]{:S(2)}) copy-start(bf16[1,2,32,64,128]{4,3,2,1,0:T(8,128)(2,1)} %param.6) | copy-start | bytes 3145732
  5.3 14.9 %collective-permute-start.1 = (bf16[2048,128]{1,0:T(8,128)(2,1)S(1)}, bf16[2048,128]{1,0:T(8,128)(2,1)S(1)}, u32[]{:S(2)}, u32[]{:S(2)}) collective-permute-start(bf16[2048,128]{1,0:T(8,128)(2,1)S(1)} %get-tuple-element.18.far), channel_id=1, source_target_pairs={{4,8},{12,16},{20,24},{28,32},{36,40},{44,48},{52,56},{60,64},{68,... | collective-permute-start | bytes 1572872 | tf_op jit(solution)/shard_map/ppermute | solution.py:585
  7.3 1.2 %copy-start.1 = (bf16[3456,128]{1,0:T(8,128)(2,1)S(1)}, bf16[3456,128]{1,0:T(8,128)(2,1)}, u32[]{:S(2)}) copy-start(bf16[3456,128]{1,0:T(8,128)(2,1)} %weight.9) | copy-start | bytes 2654212
  17.0 8.1 %copy-start.5 = (bf16[2048,128]{1,0:T(8,128)(2,1)}, bf16[2048,128]{1,0:T(8,128)(2,1)S(1)}, u32[]{:S(2)}) copy-start(bf16[2048,128]{1,0:T(8,128)(2,1)S(1)} %get-tuple-element.25.near) | copy-start | bytes 1572868
  25.0 2.0 %collective-permute-start.3 = (bf16[64,32,128]{2,1,0:T(8,128)(2,1)S(1)}, bf16[64,32,128]{2,1,0:T(8,128)(2,1)S(1)}, u32[]{:S(2)}, u32[]{:S(2)}) collective-permute-start(bf16[64,32,128]{2,1,0:T(8,128)(2,1)S(1)} %get-tuple-element.24), channel_id=1, source_target_pairs={{0,4},{4,0},{1,5},{5,1},{2,6},{6,2},{3,7},{7,3},{8,12},{12,8},{9,1... | collective-permute-start | bytes 1572872 | tf_op jit(solution)/shard_map/ppermute | solution.py:602
  25.1 21.1 %collective-permute-start.4 = (bf16[2048,128]{1,0:T(8,128)(2,1)S(1)}, bf16[2048,128]{1,0:T(8,128)(2,1)S(1)}, u32[]{:S(2)}, u32[]{:S(2)}) collective-permute-start(bf16[2048,128]{1,0:T(8,128)(2,1)S(1)} %get-tuple-element.25.near), channel_id=1, source_target_pairs={{0,4},{4,0},{1,5},{5,1},{2,6},{6,2},{3,7},{7,3},{8,12},{12,8},{9,1... | collective-permute-start | bytes 1572872 | tf_op jit(solution)/shard_map/ppermute | solution.py:586
  27.9 17.6 %all-to-all-start = ((bf16[16,4,32,128]{3,2,1,0:T(8,128)(2,1)}), bf16[16,4,32,128]{3,2,1,0:T(8,128)(2,1)S(1)}, u32[]{:S(2)}, u32[]{:S(2)}) async-start(bf16[16,4,32,128]{3,2,1,0:T(8,128)(2,1)} %bitcast.3.later), calls=%async_computation | async-start | bytes 1048576 | tf_op jit(solution)/shard_map/all_to_all | solution.py:604
  34.8 34.8 %collective-permute-start.2 = (bf16[2048,128]{1,0:T(8,128)(2,1)}, bf16[2048,128]{1,0:T(8,128)(2,1)}, u32[]{:S(2)}, u32[]{:S(2)}) collective-permute-start(bf16[2048,128]{1,0:T(8,128)(2,1)} %get-tuple-element.22.far), channel_id=1, source_target_pairs={{4,8},{12,16},{20,24},{28,32},{36,40},{44,48},{52,56},{60,64},{68,... | collective-permute-start | bytes 1572872 | tf_op jit(solution)/shard_map/ppermute | solution.py:585
  46.2 8.2 %copy-start.6 = (bf16[2048,128]{1,0:T(8,128)(2,1)}, bf16[2048,128]{1,0:T(8,128)(2,1)S(1)}, u32[]{:S(2)}) copy-start(bf16[2048,128]{1,0:T(8,128)(2,1)S(1)} %collective-permute-done.4.halo) | copy-start | bytes 1572868
  46.2 14.8 %all-to-all-start.1 = ((bf16[8,32,128]{2,1,0:T(8,128)(2,1)}), bf16[8,32,128]{2,1,0:T(8,128)(2,1)S(1)}, u32[]{:S(2)}, u32[]{:S(2)}) async-start(bf16[8,32,128]{2,1,0:T(8,128)(2,1)} %mixed_rows.1), calls=%async_computation.1 | async-start | bytes 131072 | tf_op jit(solution)/shard_map/all_to_all | solution.py:610
  54.4 6.6 %copy-start.3 = (f32[864,128]{1,0:T(8,128)S(1)}, f32[864,128]{1,0:T(8,128)}, u32[]{:S(2)}) copy-start(f32[864,128]{1,0:T(8,128)} %first.1) | copy-start | bytes 1327108
  54.4 6.6 %copy-start.4 = (f32[864,128]{1,0:T(8,128)S(1)}, f32[864,128]{1,0:T(8,128)}, u32[]{:S(2)}) copy-start(f32[864,128]{1,0:T(8,128)} %second.1) | copy-start | bytes 1327108
  61.8 16.6 %all-to-all-start.2 = ((bf16[32,32,128]{2,1,0:T(8,128)(2,1)}), bf16[32,32,128]{2,1,0:T(8,128)(2,1)S(1)}, u32[]{:S(2)}, u32[]{:S(2)}) async-start(bf16[32,32,128]{2,1,0:T(8,128)(2,1)} %spread_step.1), calls=%async_computation.2 | async-start | bytes 524288 | tf_op jit(solution)/shard_map/all_to_all | solution.py:616
